TPU v7x, 256 devices: a whole 4x4x8 slice. The times are simulated.
256 devices in a mesh: dp: 8 (over x_lo, y), slab: 32 (over x_hi, z, core).
Axes of the slice: x: 4 (x_hi: 2, x_lo: 2; x = x_hi * 2 + x_lo), y: 4, z: 8, core: 2. Of those that a mesh axis runs over, the one named last changes fastest.
Arguments:
- field: bfloat16 [8, 64, 64, 4096], P('dp', 'slab'), may hold values from -6 to 6
- cotangent: bfloat16 [8, 64, 64, 4096], P('dp', 'slab'), may hold values from -6 to 6
- mode_weights: bfloat16 [256, 16, 64, 128], P('slab'), may hold values from -5 to 5
- w_local: bfloat16 [64, 64], replicated, may hold values from -0.75 to 0.75
- bias: float32 [64], replicated, may hold values from -4 to 4
Outputs:
- grad_field: bfloat16 [8, 64, 64, 4096], P('dp', 'slab')
- grad_modes: float32 [256, 16, 64, 128], P('slab')
All inputs are finite; a program needn't handle non-finite values.
Results may differ from a plain program's by a relative error of at most 0.005.
Values sent between devices are 32-bit elements; how exact they have to be, the bound alone decides.
No kernel may reach another device: no remote copies, remote signals or barrier semaphores. Data moves between devices by JAX's collectives and lax.ppermute only.
A program may use at most 128 MiB of HBM per device.

v0:
```python
import math

import jax
import jax.numpy as jnp
from jax import lax
from jax.sharding import PartitionSpec as P

C = 64
KX = 16
KY = 16
KT = 16
NY = 64
NT = 64
CX = 2


HIGHEST = lax.Precision.HIGHEST
SQRT_TWO_PI = math.sqrt(2.0 / math.pi)


def signed_freqs(count):
    index = jnp.arange(count, dtype=jnp.int32)
    return jnp.where(index < count // 2, index, index - count)


def trig_tables(freqs, positions, length):
    phase = (freqs[:, None] * positions[None, :] % length).astype(jnp.float32) * (
        2.0 * math.pi / length
    )
    factor = 1.0 / math.sqrt(length)
    return (jnp.cos(phase) * factor, jnp.sin(phase) * factor)


def time_table(modes, length):
    cosine, sine = trig_tables(
        jnp.arange(modes, dtype=jnp.int32), jnp.arange(length, dtype=jnp.int32), length
    )
    return jnp.concatenate([cosine, -sine], 0).T


def y_analysis(first, cosine, sine, modes):
    real_in = first[:, :, :, :modes]
    imag_in = first[:, :, :, modes:]

    def applied(table, data):
        return jnp.einsum("ky,bxytc->ktbxc", table, data, precision=HIGHEST)

    real_out = applied(cosine, real_in) + applied(sine, imag_in)
    imag_out = applied(cosine, imag_in) - applied(sine, real_in)
    joined = jnp.concatenate([real_out, imag_out], -1)
    return joined.reshape((-1,) + joined.shape[2:])


def x_analysis(data, cosine, sine):
    half = data.shape[-1] // 2
    real_in = data[..., :half]
    imag_in = data[..., half:]

    def applied(table, part_in):
        return jnp.einsum("kx,mbxc->mbkc", table, part_in, precision=HIGHEST)

    real_out = applied(cosine, real_in) + applied(sine, imag_in)
    imag_out = applied(cosine, imag_in) - applied(sine, real_in)
    return jnp.concatenate([real_out, imag_out], -1)


def x_synthesis(data, cosine, sine):
    half = data.shape[-1] // 2
    real_in = data[..., :half]
    imag_in = data[..., half:]

    def applied(table, part_in):
        return jnp.einsum("kx,mbkc->mbxc", table, part_in, precision=HIGHEST)

    real_out = applied(cosine, real_in) - applied(sine, imag_in)
    imag_out = applied(cosine, imag_in) + applied(sine, real_in)
    return jnp.concatenate([real_out, imag_out], -1)


def y_synthesis(data, cosine, sine, modes):
    half = data.shape[-1] // 2
    shaped = data.reshape((cosine.shape[0], modes) + data.shape[1:])
    real_in = shaped[..., :half]
    imag_in = shaped[..., half:]

    def applied(table, part_in):
        return jnp.einsum("ky,ktbxc->bxytc", table, part_in, precision=HIGHEST)

    real_out = applied(cosine, real_in) - applied(sine, imag_in)
    imag_out = applied(cosine, imag_in) + applied(sine, real_in)
    return jnp.concatenate([real_out, imag_out], 3)


def t_synthesis(data, table):
    return jnp.einsum("bxykc,tk->bxytc", data, table, precision=HIGHEST)


def split_parts(data):
    half = data.shape[-1] // 2
    return (data[..., :half], data[..., half:])


def mix_modes(spectra, weights):
    w_real, w_imag = split_parts(weights.astype(jnp.float32))
    s_real, s_imag = split_parts(spectra)

    def applied(left, right):
        return jnp.einsum("mbki,mkio->mbko", left, right, precision=HIGHEST)

    real_out = applied(s_real, w_real) - applied(s_imag, w_imag)
    imag_out = applied(s_real, w_imag) + applied(s_imag, w_real)
    return jnp.concatenate([real_out, imag_out], -1)


def weight_grads(spectra, grads):
    s_real, s_imag = split_parts(spectra)
    g_real, g_imag = split_parts(grads)

    def applied(left, right):
        return jnp.einsum("mbki,mbko->mkio", left, right, precision=HIGHEST)

    real_out = applied(s_real, g_real) + applied(s_imag, g_imag)
    imag_out = applied(s_real, g_imag) - applied(s_imag, g_real)
    return jnp.concatenate([real_out, imag_out], -1)


def adjoint_modes(grads, weights):
    w_real, w_imag = split_parts(weights.astype(jnp.float32))
    g_real, g_imag = split_parts(grads)

    def applied(left, right):
        return jnp.einsum("mkio,mbko->mbki", left, right, precision=HIGHEST)

    real_out = applied(w_real, g_real) + applied(w_imag, g_imag)
    imag_out = applied(w_real, g_imag) - applied(w_imag, g_real)
    return jnp.concatenate([real_out, imag_out], -1)


def gelu_slope(values):
    inner = SQRT_TWO_PI * (values + 0.044715 * values**3)
    tanh_value = jnp.tanh(inner)
    return 0.5 * (1.0 + tanh_value) + 0.5 * values * (
        1.0 - tanh_value * tanh_value
    ) * SQRT_TWO_PI * (1.0 + 3.0 * 0.044715 * values * values)


def body(field, cotangent, mode_weights, w_local, bias):
    slab_count = lax.axis_size("slab")
    x_length = CX * slab_count
    t_table = time_table(KT, NT)
    t_narrow = t_table.astype(jnp.bfloat16)
    y_cos, y_sin = trig_tables(signed_freqs(KY), jnp.arange(NY, dtype=jnp.int32), NY)
    own_points = lax.axis_index("slab") * CX + jnp.arange(CX, dtype=jnp.int32)
    own_cos, own_sin = trig_tables(signed_freqs(KX), own_points, x_length)

    def analyse(values):
        first = jnp.einsum(
            "rtc,tk->rkc", values.reshape(-1, NT, C), t_narrow, preferred_element_type=jnp.float32
        )
        second = y_analysis(first.reshape(values.shape[0], CX, NY, 2 * KT, C), y_cos, y_sin, KT)
        return lax.psum_scatter(
            x_analysis(second, own_cos, own_sin), "slab", scatter_dimension=0, tiled=True
        )

    def synthesise(spectra):
        rows_back = x_synthesis(
            lax.all_gather(spectra, "slab", axis=0, tiled=True), own_cos, own_sin
        )
        return t_synthesis(y_synthesis(rows_back, y_cos, y_sin, KT), t_table)

    spectra = analyse(field)
    spec = synthesise(mix_modes(spectra, mode_weights))
    flat = field.reshape(-1, C)
    pre_act = (
        spec.reshape(-1, C) + jnp.dot(flat, w_local, preferred_element_type=jnp.float32) + bias
    )
    grad_pre = (cotangent.reshape(-1, C).astype(jnp.float32) * gelu_slope(pre_act)).astype(
        jnp.bfloat16
    )
    grad_spectra = analyse(grad_pre.reshape(field.shape))
    grad_modes = lax.psum(weight_grads(spectra, grad_spectra), "dp")
    back = synthesise(adjoint_modes(grad_spectra, mode_weights))
    grad_rows = back.reshape(-1, C) + jnp.dot(
        grad_pre, w_local.T, preferred_element_type=jnp.float32
    )
    return (grad_rows.astype(jnp.bfloat16).reshape(field.shape), grad_modes)


def solution(mesh):
    placed = (
        P("dp", "slab", None, None),
        P("dp", "slab", None, None),
        P("slab", None, None, None),
        P(),
        P(),
    )
    return jax.shard_map(
        body,
        mesh=mesh,
        in_specs=placed,
        out_specs=(P("dp", "slab", None, None), P("slab", None, None, None)),
        check_vma=False,
    )
```

profile of v0, /device:TPU:1, one launch (start us, length us, event | category | flops | bytes accessed | tf_op | source)
XLA Modules:
  0.0 630.2 jit_solution(7064475088024300792)
XLA Ops:
  7.3 3.3 reshape.217
  10.6 3.1 copy.53
  31.8 118.0 %reduce-scatter.3.cloned.1.call-done = f32[8,1,16,128]{3,2,1,0:T(8,128)} async-done(((f32[256,1,16,128]{3,2,1,0:T(8,128)}), f32[8,1,16,128]{3,2,1,0:T(8,128)}) %reduce-scatter.3.cloned.1.call-update) | async-done | bytes 65552 | tf_op jit(solution)/shard_map/reduce_scatter | solution.py:161
  159.5 3.2 reshape.233
  162.7 3.2 reshape.250
  165.9 4.0 copy.67
  170.0 73.2 %all-gather.3.cloned.1.call-done = f32[256,1,16,128]{3,2,1,0:T(8,128)} async-done(((f32[8,1,16,128]{3,2,1,0:T(8,128)}), f32[256,1,16,128]{3,2,1,0:T(8,128)}) %all-gather.3.cloned.1.call-update) | async-done | bytes 2097168 | tf_op jit(solution)/shard_map/all_gather | solution.py:167
  243.1 4.2 fusion.224
  264.4 3.1 copy.65
  267.5 5.0 fusion.85
  272.5 4.0 copy.66
  276.5 4.0 fusion.10
  300.3 110.2 %reduce-scatter.5.cloned.1.call-done = f32[8,1,16,128]{3,2,1,0:T(8,128)} async-done(((f32[256,1,16,128]{3,2,1,0:T(8,128)}), f32[8,1,16,128]{3,2,1,0:T(8,128)}) %reduce-scatter.5.cloned.1.call-update) | async-done | bytes 65552 | tf_op jit(solution)/shard_map/reduce_scatter | solution.py:161
  411.5 3.3 fusion.27
  414.8 3.4 fusion.21
  418.2 3.4 fusion.19
  421.7 3.4 fusion.29
  428.8 3.2 pad_maximum_fusion
  432.0 77.5 %all-gather.5.cloned.1.call-done = f32[256,1,16,128]{3,2,1,0:T(8,128)} async-done(((f32[8,1,16,128]{3,2,1,0:T(8,128)}), f32[256,1,16,128]{3,2,1,0:T(8,128)}) %all-gather.5.cloned.1.call-update) | async-done | bytes 2097168 | tf_op jit(solution)/shard_map/all_gather | solution.py:167
  509.5 4.2 fusion.222
  530.5 3.1 copy.80
  533.7 5.0 fusion.83
  547.6 71.1 %all-reduce.2.cloned.1.call-done = f32[8,16,64,128]{3,2,1,0:T(8,128)} async-done(((f32[8,16,64,128]{3,2,1,0:T(8,128)}), f32[8,16,64,128]{3,2,1,0:T(8,128)}) %all-reduce.2.cloned.1.call-update) | async-done | bytes 4194320 | tf_op jit(solution)/shard_map/psum | solution.py:181
  618.7 4.8 copy.128
  (121 shorter events, 94.5 us)
Async XLA Ops:
  7.2 269.3 %copy-start = (bf16[64,64]{1,0:T(8,128)(2,1)S(1)}, bf16[64,64]{1,0:T(8,128)(2,1)}, u32[]{:S(2)}) copy-start(bf16[64,64]{1,0:T(8,128)(2,1)} %param.8) | copy-start | bytes 24580
  7.2 142.6 %reduce-scatter.3.cloned.1.call-start = ((), (), s32[]{:S(2)}) async-start(), calls=%async_computation.2 | async-start | bytes 2162688 | tf_op jit(solution)/shard_map/reduce_scatter | solution.py:161
  31.7 119.7 %copy-start.7 = (bf16[8,16,64,128]{3,2,1,0:T(8,128)(2,1)S(1)}, bf16[8,16,64,128]{3,2,1,0:T(8,128)(2,1)}, u32[]{:S(2)}) copy-start(bf16[8,16,64,128]{3,2,1,0:T(8,128)(2,1)} %param.7) | copy-start | bytes 6291460
  31.7 211.4 %all-gather.3.cloned.1.call-start = ((), (), s32[]{:S(2)}) async-start(), calls=%async_computation.3 | async-start | bytes 2162688 | tf_op jit(solution)/shard_map/all_gather | solution.py:167
  151.4 3.6 copy-start.8
  155.0 4.5 copy-start.1
  158.7 4.1 copy-start.5
  159.4 251.0 %reduce-scatter.5.cloned.1.call-start = ((), (), s32[]{:S(2)}) async-start(), calls=%async_computation.4 | async-start | bytes 2162688 | tf_op jit(solution)/shard_map/reduce_scatter | solution.py:161
  272.5 4.0 copy-start.4
  272.5 4.0 copy-start.10
  280.6 1.0 copy-start.2
  300.0 111.5 %copy-start.9 = (bf16[8,16,64,128]{3,2,1,0:T(8,128)(2,1)S(1)}, bf16[8,16,64,128]{3,2,1,0:T(8,128)(2,1)}, u32[]{:S(2)}) copy-start(bf16[8,16,64,128]{3,2,1,0:T(8,128)(2,1)} %param.7) | copy-start | bytes 6291460
  300.0 209.5 %all-gather.5.cloned.1.call-start = ((), (), s32[]{:S(2)}) async-start(), calls=%async_computation.5 | async-start | bytes 2162688 | tf_op jit(solution)/shard_map/all_gather | solution.py:167
  418.2 7.6 %copy-start.6 = (f32[8,16,64]{2,1,0:T(8,128)S(1)}, f32[8,16,64]{2,1,0:T(8,128)}, u32[]{:S(2)}) copy-start(f32[8,16,64]{2,1,0:T(8,128)} %get-tuple-element.21) | copy-start | bytes 98308
  425.8 192.9 %all-reduce.2.cloned.1.call-start = ((), (), s32[]{:S(2)}) async-start(), calls=%async_computation.6 | async-start | bytes 8388608 | tf_op jit(solution)/shard_map/psum | solution.py:181
  538.7 3.0 copy-start.3
Sparse Core Ops, SparseCore 0:
  31.8 117.9 reduce-scatter.2
  159.6 83.5 all-gather.2
  300.1 110.2 reduce-scatter.4
  425.9 83.5 all-gather.4
  512.0 106.6 all-reduce.1
where the time goes:
time: 639 us; the launch traced here: 630 us
  waiting for transfers between devices  450 us (70%)
  local copies, waits for them, and re-layouts  78.9 us (12%)
  matrix products  74.8 us (12%)
  between operations  14.6 us (2%)
  other arithmetic  11.5 us (2%)
    reduce_scatter x2, waiting for transfers between devices, analyse(): lax.psum_scatter(x_analysis(second, own_cos, own_sin), 'slab', scatter_di...  228 us
    all_gather x2, waiting for transfers between devices, synthesise(): lax.all_gather(spectra, 'slab', axis=0, tiled=True)  151 us
    psum x1, waiting for transfers between devices, body(): grad_modes = lax.psum(weight_grads(spectra, grad_spectra), 'dp')  71.1 us
    unnamed x35, local copies, waits for them, and re-layouts  19.4 us
    dot_general x8, matrix products, applied(): return jnp.einsum('ky,ktbxc->bxytc', table, part_in, precision=HIGHEST)  15.3 us
    dot_general x4, matrix products, applied(): return jnp.einsum('mkio,mbko->mbki', left, right, precision=HIGHEST)  13.6 us
  transfers between devices with their start and end apart: 5, of which 5 were waited for; matrix products, arithmetic and copies ran while one was open for 9% of the time, Pallas kernels for 0%

commit v1 on v0

v1 whole, which is shorter than its diff:
```python
import math

import jax
import jax.numpy as jnp
import ml_dtypes
import numpy as np
from jax import lax
from jax.experimental import pallas as pl
from jax.experimental.pallas import tpu as pltpu
from jax.sharding import PartitionSpec as P

C = 64
K = 16
N = 64
CX = 2
SLABS = 32
DP = 8
TP = N // 2

BF = jnp.bfloat16
F32 = jnp.float32
SQRT_TWO_PI = math.sqrt(2.0 / math.pi)


def trig(freqs):
    phase = (freqs[:, None] * np.arange(N)[None, :] % N) * (2.0 * math.pi / N)
    return np.cos(phase) / math.sqrt(N), np.sin(phase) / math.sqrt(N)


def rounded(table):
    return table.astype(np.float32).astype(ml_dtypes.bfloat16)


def wide(table):
    high = rounded(table)
    low = rounded(table - high.astype(np.float64))
    return np.concatenate([high, low, high], 1)


def twice_table(table):
    high = rounded(table)
    low = rounded(table - high.astype(np.float64))
    return np.concatenate([high, low], 1)


SIGNED = np.concatenate([np.arange(K // 2), np.arange(-K // 2, 0)])
COS, SIN = trig(SIGNED)
T_COS, T_SIN = trig(np.arange(K))
P_RE, P_IM = T_COS.T, -T_SIN.T

Y_IN = twice_table(np.stack([COS, SIN], 1).reshape(2 * K, N))
Y_OUT = wide(np.concatenate([COS, SIN], 0).T)
X_IN = wide(np.concatenate([COS, SIN], 0))
X_OUT = wide(np.concatenate([COS, SIN], 0).T)


def t_in():
    re = rounded(P_RE).astype(np.float64).reshape(TP, 2, K)
    im = rounded(P_IM).astype(np.float64).reshape(TP, 2, K)
    rows_re = np.concatenate([re, im], 0)
    rows_im = np.concatenate([im, -re], 0)
    both = np.stack([rows_re, rows_im], 0)
    table = both.transpose(0, 2, 3, 1).reshape(4 * K, 2 * TP)
    return rounded(np.concatenate([table, table], 1))


def t_out():
    re = P_RE.reshape(TP, 2, K)
    im = P_IM.reshape(TP, 2, K)
    of_c = np.stack([re, im], 2)
    of_s = np.stack([im, -re], 2)
    return wide(np.concatenate([of_c, of_s], 0).reshape(2 * TP, 4 * K))


TABLES = {
    "y_in": Y_IN,
    "t_in": t_in(),
    "y_out": Y_OUT,
    "x_in": X_IN,
    "x_out": X_OUT,
    "t_out": t_out(),
}
PLACES = {}
for name, values in TABLES.items():
    PLACES[name] = (sum(TABLES[other].shape[0] for other in PLACES), *values.shape)
PACKED = np.concatenate([np.pad(v, ((0, 0), (0, 256 - v.shape[1]))) for v in TABLES.values()], 0)


def table(ref, name):
    first, rows, columns = PLACES[name]
    return ref[first : first + rows, :columns]


def dot(left, right):
    return jnp.dot(left, right, preferred_element_type=F32)


def split(data):
    high = data.astype(BF)
    return high, (data - high.astype(F32)).astype(BF)


def stack3(data):
    high, low = split(data)
    return jnp.concatenate([high, high, low], 0)


def stack2(data):
    high, low = split(data)
    return jnp.concatenate([high, low], 0)


def low_lanes(shape):
    return lax.broadcasted_iota(jnp.int32, shape, 1) < C


def swap(data):
    return pltpu.roll(data, C, 1)


def turned(data):
    other = swap(data)
    return jnp.where(low_lanes(data.shape), -other, other)


def lanes(blocks):
    return jnp.concatenate(blocks, 1)


Y_TILES = 8


def y_analysis_store(chunk, first_tile, tiles, y_in, scratch):
    out = dot(y_in, jnp.concatenate([chunk, chunk], 0))
    for j in range(tiles):
        scratch[pl.ds(first_tile + j, 2 * K, stride=TP), :] = out[:, j * 128 : (j + 1) * 128]


def t_analysis(scratch, t_table, out_ref, x, group=4):
    low = low_lanes((K, 128))
    for first in range(0, K, group):
        data = lanes([scratch[(first + j) * 2 * TP : (first + j + 1) * 2 * TP, :] for j in range(group)])
        res = dot(t_table, stack2(data))
        for j in range(group):
            re0, re1, im0, im1 = (res[q * K : (q + 1) * K, j * 128 : (j + 1) * 128] for q in range(4))
            both = jnp.where(low, re0, im1) + swap(jnp.where(low, im0, re1))
            out_ref[2 * (first + j), x] = both[:8]
            out_ref[2 * (first + j) + 1, x] = both[8:]


def t_synthesis(w_ref, t_table, scratch, x, group=4):
    low = low_lanes((K, 128))
    zero = jnp.zeros((K, 128), F32)
    for first in range(0, K, group):
        blocks = []
        for j in range(group):
            w = jnp.concatenate([w_ref[2 * (first + j), x], w_ref[2 * (first + j) + 1, x]], 0)
            other = swap(w)
            blocks.append(
                jnp.concatenate(
                    [
                        jnp.where(low, w, zero),
                        jnp.where(low, other, zero),
                        jnp.where(low, zero, other),
                        jnp.where(low, zero, w),
                    ],
                    0,
                )
            )
        res = dot(t_table, stack3(lanes(blocks)))
        for j in range(group):
            for cs in range(2):
                scratch[pl.ds(cs * K + first + j, TP, stride=2 * K), :] = res[
                    cs * TP : (cs + 1) * TP, j * 128 : (j + 1) * 128
                ]


def y_synthesis(scratch, first_tile, tiles, y_out):
    data = lanes(
        [
            scratch[pl.ds(pl.multiple_of((first_tile + j) * 2 * K, 2 * K), 2 * K), :]
            for j in range(tiles)
        ]
    )
    return dot(y_out, stack3(data))


def channel_map(chunk, weight, tiles, contracted=0):
    rows = jnp.concatenate([chunk[:, j * 128 : (j + 1) * 128] for j in range(tiles)], 0)
    out = lax.dot_general(
        rows, weight, (((1,), (contracted,)), ((), ())), preferred_element_type=F32
    )
    return lanes([out[j * N : (j + 1) * N] for j in range(tiles)])


def lane_slice(step, tiles):
    return pl.ds(pl.multiple_of(step * tiles * 128, tiles * 128), tiles * 128)


def analyse_kernel(
    field_in, cot_in, w_in, tables_in, map_in, bias_in,
    out_ref, field_ref, cot_ref, w_ref, tables_ref, map_ref, bias_ref,
    scratch, small_map, small_bias, sems,
):
    copies = [
        pltpu.make_async_copy(source, target, sems.at[i])
        for i, (source, target) in enumerate(
            [
                (tables_in, tables_ref),
                (field_in.at[0], field_ref.at[0]),
                (field_in.at[1], field_ref.at[1]),
                (map_in, small_map),
                (bias_in, small_bias),
                (w_in, w_ref),
                (cot_in, cot_ref),
            ]
        )
    ]
    for copy in copies:
        copy.start()
    copies[0].wait()
    y_in, t_table = table(tables_ref, "y_in"), table(tables_ref, "t_in")
    for x in range(CX):
        copies[1 + x].wait()

        @pl.loop(0, TP // Y_TILES)
        def _(step):
            y_analysis_store(
                field_ref[x, :, lane_slice(step, Y_TILES)], step * Y_TILES, Y_TILES, y_in, scratch
            )

        t_analysis(scratch, t_table, out_ref, x)
    copies[3].wait()
    copies[4].wait()
    wide_map = jnp.concatenate([small_map[...]] * 2, 1)
    wide_map = jnp.concatenate([wide_map] * 2, 0)
    row = lax.broadcasted_iota(jnp.int32, (2 * C, 2 * C), 0) // C
    lane = lax.broadcasted_iota(jnp.int32, (2 * C, 2 * C), 1) // C
    map_ref[...] = jnp.where(row == lane, wide_map, jnp.zeros_like(wide_map))
    bias_ref[...] = jnp.concatenate([small_bias[...]] * 2, 1)
    copies[5].wait()
    copies[6].wait()


def gelu_slope(z):
    inner = SQRT_TWO_PI * (z + 0.044715 * z * z * z)
    tanh_value = jnp.tanh(inner)
    return 0.5 * (1.0 + tanh_value) + 0.5 * z * (1.0 - tanh_value * tanh_value) * SQRT_TWO_PI * (
        1.0 + 3.0 * 0.044715 * z * z
    )


def middle_kernel(w_ref, field_ref, cot_ref, map_ref, bias_ref, tables_ref, gz_ref, out_ref, syn, ana):
    y_in, y_out, t_in, t_out = (table(tables_ref, name) for name in ("y_in", "y_out", "t_in", "t_out"))

    @pl.loop(0, CX)
    def _(x):
        t_synthesis(w_ref, t_out, syn, x)

        @pl.loop(0, TP // Y_TILES)
        def _(step):
            at = lane_slice(step, Y_TILES)
            spec = y_synthesis(syn, step * Y_TILES, Y_TILES, y_out)
            z = spec + channel_map(field_ref[x, :, at], map_ref[...], Y_TILES) + lanes([bias_ref[...]] * Y_TILES)
            gz = (cot_ref[x, :, at].astype(F32) * gelu_slope(z)).astype(BF)
            gz_ref[x, :, at] = gz
            y_analysis_store(gz, step * Y_TILES, Y_TILES, y_in, ana)

        t_analysis(ana, t_in, out_ref, x)


def final_kernel(w_ref, gz_ref, map_ref, tables_ref, out_ref, syn):
    y_out, t_out = table(tables_ref, "y_out"), table(tables_ref, "t_out")

    @pl.loop(0, CX)
    def _(x):
        t_synthesis(w_ref, t_out, syn, x)

        @pl.loop(0, TP // Y_TILES)
        def _(step):
            at = lane_slice(step, Y_TILES)
            spec = y_synthesis(syn, step * Y_TILES, Y_TILES, y_out)
            out_ref[x, :, at] = (spec + channel_map(gz_ref[x, :, at], map_ref[...], Y_TILES, 1)).astype(BF)


M = 8


def x_analysis(in_ref, x_in):
    data = lanes([in_ref[pl.ds(m, N, stride=M), :] for m in range(M)])
    res = dot(x_in, stack3(data))
    out = []
    for m in range(M):
        cos_part = res[:K, m * 128 : (m + 1) * 128]
        sin_part = res[K:, m * 128 : (m + 1) * 128]
        out.append(cos_part - turned(sin_part))
    return out


def x_synthesis(blocks, x_out, out_ref):
    data = lanes([jnp.concatenate([v, turned(v)], 0) for v in blocks])
    res = dot(x_out, stack3(data))
    for m in range(M):
        out_ref[pl.ds(m, N, stride=M), :] = res[:, m * 128 : (m + 1) * 128]


def mix(u, weights):
    low = low_lanes((K, 128))
    other = swap(u)
    rows = jnp.concatenate([jnp.where(low, u, other), jnp.where(low, other, u)], 0)
    parts = jnp.concatenate(split(rows), 0).astype(F32)
    row = lax.broadcasted_iota(jnp.int32, (4 * K, 128), 0) % K
    half = lax.broadcasted_iota(jnp.int32, (4 * K, 128), 1) // C
    left = lanes([jnp.where(row == 2 * j + half, parts, 0.0).astype(BF) for j in range(K // 2)])
    res = dot(left, weights)
    res = res[: 2 * K] + res[2 * K :]
    return res[:K] + turned(res[K:])


def mix_adjoint(g, weights):
    rows = jnp.concatenate([g, -turned(g)], 0)
    parts = jnp.concatenate(split(rows), 0)
    res = lax.dot_general(parts, weights, (((1,), (1,)), ((), ())), preferred_element_type=F32)
    res = res[: 2 * K] + res[2 * K :]
    row = lax.broadcasted_iota(jnp.int32, (2 * K, 128), 0) % K
    half = lax.broadcasted_iota(jnp.int32, (2 * K, 128), 1) // C
    total = jnp.zeros((2 * K, 128), F32)
    for j in range(K // 2):
        total = total + jnp.where(row == 2 * j + half, res[:, j * 128 : (j + 1) * 128], 0.0)
    total = total + swap(total)
    return jnp.where(low_lanes((K, 128)), total[:K], total[K:])


def spectral_kernel(adjoint, in_ref, w_ref, tables_ref, hat_ref, out_ref):
    spectra = x_analysis(in_ref, table(tables_ref, "x_in"))
    mixed = []
    for m in range(M):
        hat_ref[m] = spectra[m]
        weights = w_ref[m]
        mixed.append(mix_adjoint(spectra[m], weights) if adjoint else mix(spectra[m], weights))
    x_synthesis(mixed, table(tables_ref, "x_out"), out_ref)


G_MODES = 2


def grads_kernel(u_near, u_far, g_near, g_far, out_ref):
    own = lax.broadcasted_iota(jnp.int32, (C, 2 * DP * K), 1) % K
    for j in range(G_MODES):
        m = pl.program_id(0) * G_MODES + j
        u = jnp.concatenate([ref[b, m] for ref in (u_near, u_far) for b in range(DP // 2)], 0)
        g = jnp.concatenate([ref[b, m] for ref in (g_near, g_far) for b in range(DP // 2)], 0)
        u_t = u.T.astype(BF)
        left = lanes([u_t[:C], u_t[C:]])
        right = jnp.concatenate([g, -turned(g)], 0).astype(BF)
        tall = jnp.concatenate([jnp.where(own == kx, left, jnp.zeros_like(left)) for kx in range(K)], 0)
        out_ref[j] = dot(tall, right).reshape(K, C, 2 * C)


PARAMS = pltpu.CompilerParams(vmem_limit_bytes=32 * 1024 * 1024)
IN_VMEM = pl.BlockSpec(memory_space=pltpu.VMEM)
IN_HBM = pl.BlockSpec(memory_space=pltpu.HBM)


def vmem_call(kernel, name, out_shapes, scratch, *operands, specs=None):
    return pl.pallas_call(
        kernel,
        name=name,
        out_shape=out_shapes,
        in_specs=specs or [IN_VMEM] * len(operands),
        out_specs=jax.tree.map(lambda _: IN_VMEM, out_shapes),
        scratch_shapes=scratch,
        compiler_params=PARAMS,
    )(*operands)


def shape(dims, kind=F32):
    return jax.ShapeDtypeStruct(dims, kind)


SPECTRA = shape((SLABS, CX, M, 128))
ROWS = pltpu.VMEM((TP * 2 * K, 128), F32)
Y_RING = 4


def exchange(data):
    return lax.all_to_all(data, "slab", 0, 0, tiled=True)


def gather_samples(data):
    def moved(by):
        return lax.ppermute(
            data, "dp", [(i, i // Y_RING * Y_RING + (i + by) % Y_RING) for i in range(DP)]
        )

    near = jnp.stack([data, moved(1), moved(3), moved(2)], 0)
    return near, lax.ppermute(near, "dp", [(i, (i + Y_RING) % DP) for i in range(DP)])


def body(field, cotangent, mode_weights, w_local, bias):
    grid_shape = (CX, N, N * C)

    def spectral(adjoint, data):
        return vmem_call(
            lambda *refs: spectral_kernel(adjoint, *refs),
            "adjoint" if adjoint else "mix",
            (shape((M, K, 128)), shape((N * M, 128))),
            [],
            data.reshape(N * M, 128),
            weights,
            tables,
        )

    first, values, cot, weights, tables, wide_map, wide_bias = vmem_call(
        analyse_kernel,
        "analyse",
        (
            SPECTRA,
            shape(grid_shape, BF),
            shape(grid_shape, BF),
            shape((M, K * C, 2 * C), BF),
            shape(PACKED.shape, BF),
            shape((2 * C, 2 * C), BF),
            shape((1, 2 * C)),
        ),
        [ROWS, pltpu.VMEM((C, C), BF), pltpu.VMEM((1, C), F32), pltpu.SemaphoreType.DMA((7,))],
        field.reshape(grid_shape),
        cotangent.reshape(grid_shape),
        mode_weights.reshape(M, K * C, 2 * C),
        jnp.asarray(PACKED),
        w_local,
        bias.reshape(1, C),
        specs=[IN_HBM] * 6,
    )
    u_hat, mixed = spectral(False, exchange(first))
    u_near, u_far = gather_samples(u_hat)
    gz, second = vmem_call(
        middle_kernel,
        "middle",
        (shape(grid_shape, BF), SPECTRA),
        [ROWS, ROWS],
        exchange(mixed.reshape(SPECTRA.shape)),
        values,
        cot,
        wide_map,
        wide_bias,
        tables,
    )
    g_hat, back = spectral(True, exchange(second))
    g_near, g_far = gather_samples(g_hat)
    grad_field = vmem_call(
        final_kernel,
        "final",
        shape(grid_shape, BF),
        [ROWS],
        exchange(back.reshape(SPECTRA.shape)),
        gz,
        wide_map,
        tables,
    )
    grad_modes = pl.pallas_call(
        grads_kernel,
        name="weight_grads",
        grid=(M // G_MODES,),
        out_shape=shape((M, K, C, 2 * C)),
        in_specs=[IN_VMEM] * 4,
        out_specs=pl.BlockSpec((G_MODES, K, C, 2 * C), lambda m: (m, 0, 0, 0)),
        compiler_params=PARAMS,
    )(u_near, u_far, g_near, g_far)
    return grad_field.reshape(field.shape), grad_modes


def solution(mesh):
    placed = (
        P("dp", "slab", None, None),
        P("dp", "slab", None, None),
        P("slab", None, None, None),
        P(),
        P(),
    )
    return jax.shard_map(
        body,
        mesh=mesh,
        in_specs=placed,
        out_specs=(P("dp", "slab", None, None), P("slab", None, None, None)),
        check_vma=False,
    )
```

time: 639 us -> 114 us (0.18); the launches traced: 630 us -> 113 us
  waiting for transfers between devices: 450 us -> 22.1 us
  matrix products: 74.8 us -> 0 us
  local copies, waits for them, and re-layouts: 78.9 us -> 7.29 us
  blocking collectives: 0 us -> 43.5 us
  Pallas kernels: 0 us -> 20 us
  starting transfers between devices: 0.42 us -> 19.8 us
  between operations: 14.6 us -> 0.71 us
  other arithmetic: 11.5 us -> 0.04 us
    reduce_scatter x2 -> x0, waiting for transfers between devices: 228 us -> none  [analyse(): lax.psum_scatter(x_analysis(second, own_cos, own_sin), 'slab', scatter_di...]
    all_gather x2 -> x0, waiting for transfers between devices: 151 us -> none  [synthesise(): lax.all_gather(spectra, 'slab', axis=0, tiled=True)]
    dot_general x46 -> x0, matrix products: 74.8 us -> none  [the longest x8 15.3 us: applied(): return jnp.einsum('ky,ktbxc->bxytc', table, part_in, precision=HIGHEST)]
    psum x1 -> x0, waiting for transfers between devices: 71.1 us -> none  [body(): grad_modes = lax.psum(weight_grads(spectra, grad_spectra), 'dp')]
    all_to_all x0 -> x2, blocking collectives: none -> 43.5 us  [exchange(): return lax.all_to_all(data, 'slab', 0, 0, tiled=True)]
    reshape x8 -> x0, local copies, waits for them, and re-layouts: 22.7 us -> none  [the longest x2 6.39 us: analyse(): values.reshape(-1, NT, C)]
    pallas_call x0 -> x6, Pallas kernels: none -> 20 us  [the longest x5 16.5 us: vmem_call(): pl.pallas_call(kernel, name=name, out_shape=out_shapes, in_specs=specs or...]
    ppermute x0 -> x8, waiting for transfers between devices: none -> 13 us  [the longest x2 9.48 us: gather_samples(): lax.ppermute(near, 'dp', [(i, (i + Y_RING) % DP) for i in range(DP)])]
  transfers between devices with their start and end apart: 5 -> 10, of which waited for: 5 -> 6; matrix products, arithmetic and copies ran while one was open for 9% -> 0% of each run, Pallas kernels for 0% -> 5%
where the time goes in v1:
time: 114 us; the launch traced here: 113 us
  blocking collectives  43.5 us (38%)
  waiting for transfers between devices  22.1 us (19%)
  Pallas kernels  20 us (18%)
  starting transfers between devices  19.8 us (17%)
  local copies, waits for them, and re-layouts  7.29 us (6%)
    all_to_all x2, blocking collectives, exchange(): return lax.all_to_all(data, 'slab', 0, 0, tiled=True)  43.5 us
    pallas_call x5, Pallas kernels, vmem_call(): pl.pallas_call(kernel, name=name, out_shape=out_shapes, in_specs=specs or...  16.5 us
    all_to_all x2, starting transfers between devices, exchange(): return lax.all_to_all(data, 'slab', 0, 0, tiled=True)  10 us
    ppermute x2, waiting for transfers between devices, gather_samples(): lax.ppermute(near, 'dp', [(i, (i + Y_RING) % DP) for i in range(DP)])  9.48 us
    all_to_all x2, waiting for transfers between devices, exchange(): return lax.all_to_all(data, 'slab', 0, 0, tiled=True)  9.08 us
    ppermute x6, starting transfers between devices, moved(): lax.ppermute(data, 'dp', [(i, i // Y_RING * Y_RING + (i + by) % Y_RING) f...  8.92 us
    unnamed x16, local copies, waits for them, and re-layouts  7.29 us
    pallas_call x1, Pallas kernels, body(): pl.pallas_call(grads_kernel, name='weight_grads', grid=(M // G_MODES,), o...  3.56 us
  transfers between devices with their start and end apart: 10, of which 6 were waited for; matrix products, arithmetic and copies ran while one was open for 0% of the time, Pallas kernels for 5%

profile of v1, /device:TPU:1, one launch (start us, length us, event | category | flops | bytes accessed | tf_op | source)
XLA Modules:
  0.0 113.4 jit_solution(18357252689108062844)
XLA Ops:
  0.6 1.6 %copy-done = bf16[8,16,64,128]{3,2,1,0:T(8,128)(2,1)S(1)} copy-done((bf16[8,16,64,128]{3,2,1,0:T(8,128)(2,1)S(1)}, bf16[8,16,64,128]{3,2,1,0:T(8,128)(2,1)}, u32[]{:S(2)}) %copy-start) | copy-done | bytes 2097176
  2.2 1.2 %copy-done.1 = bf16[1,2,64,4096]{3,2,1,0:T(8,128)(2,1)S(1)} copy-done((bf16[1,2,64,4096]{3,2,1,0:T(8,128)(2,1)S(1)}, bf16[1,2,64,4096]{3,2,1,0:T(8,128)(2,1)}, u32[]{:S(2)}) %copy-start.1) | copy-done | bytes 1048600
  3.5 1.2 %copy-done.2 = bf16[1,2,64,4096]{3,2,1,0:T(8,128)(2,1)S(1)} copy-done((bf16[1,2,64,4096]{3,2,1,0:T(8,128)(2,1)S(1)}, bf16[1,2,64,4096]{3,2,1,0:T(8,128)(2,1)}, u32[]{:S(2)}) %copy-start.2) | copy-done | bytes 1048600
  4.7 0.9 copy-done.5
  7.0 2.9 %analyse.1 = (f32[32,2,8,128]{3,2,1,0:T(8,128)S(1)}, bf16[2,64,4096]{2,1,0:T(8,128)(2,1)S(1)}, bf16[2,64,4096]{2,1,0:T(8,128)(2,1)S(1)}, bf16[8,1024,128]{2,1,0:...) custom-call(bf16[2,64,4096]{2,1,0:T(8,128)(2,1)S(1)} %bitcast.18, ...), custom_call_target="tpu_custom_call" | custom-call | tf_op jit(solution)/shard_map/analyse/pallas_call | solution.py:366
  9.9 25.8 %all_to_all.20 = f32[32,2,8,128]{3,2,1,0:T(8,128)S(1)} all-to-all(f32[32,2,8,128]{3,2,1,0:T(8,128)S(1)} %get-tuple-element.15), channel_id=1, replica_groups=mesh['dp'=8,'slab'=32] {'slab'}, dimensions={0} | all-to-all | bytes 524288 | tf_op jit(solution)/shard_map/all_to_all | solution.py:387
  35.7 1.0 mix.1
  36.7 17.7 %all_to_all.21.w_ref = f32[32,2,8,128]{3,2,1,0:T(8,128)S(1)} all-to-all(f32[32,2,8,128]{3,2,1,0:T(8,128)S(1)} %bitcast.22), channel_id=1, replica_groups=mesh['dp'=8,'slab'=32] {'slab'}, dimensions={0} | all-to-all | bytes 524288 | tf_op jit(solution)/shard_map/all_to_all | solution.py:387
  54.4 6.6 %middle.1 = (bf16[2,64,4096]{2,1,0:T(8,128)(2,1)S(1)}, f32[32,2,8,128]{3,2,1,0:T(8,128)}) custom-call(f32[32,2,8,128]{3,2,1,0:T(8,128)S(1)} %all_to_all.21.w_ref, bf16[2,64,4096]{2,1,0:T(8,128)(2,1)S(1)} %get-tuple-element.19.field_ref, bf16[2,64,4096]{2,1,0:T(8,128)(2,1)S(1)} %get-tuple-element.20.cot_ref, bf16[128,128]{1,0:T(8,128)(2,1)S(1)} %get-tuple-element.21.map_ref, ...), custom_call_target="tpu_custom_call" | custom-call | tf_op jit(solution)/shard_map/middle/pallas_call | solution.py:366
  61.0 1.0 copy-done.3
  62.0 5.0 %all-to-all-start.2 = ((f32[32,2,8,128]{3,2,1,0:T(8,128)}), f32[32,2,8,128]{3,2,1,0:T(8,128)S(1)}, u32[]{:S(2)}, u32[]{:S(2)}) async-start(f32[32,2,8,128]{3,2,1,0:T(8,128)} %get-tuple-element.23), calls=%async_computation.2 | async-start | bytes 524288 | tf_op jit(solution)/shard_map/all_to_all | solution.py:387
  67.0 3.0 %collective-permute-start.2 = (f32[8,16,128]{2,1,0:T(8,128)S(1)}, f32[8,16,128]{2,1,0:T(8,128)S(1)}, u32[]{:S(2)}, u32[]{:S(2)}) collective-permute-start(f32[8,16,128]{2,1,0:T(8,128)S(1)} %get-tuple-element.26), channel_id=1, source_target_pairs={{0,64},{32,96},{64,0},{96,32},{128,192},{160,224},{192,128},{224,1... | collective-permute-start | bytes 196616 | tf_op jit(solution)/shard_map/ppermute | solution.py:392
  70.0 0.8 collective-permute-start.1
  71.4 9.1 %all-to-all-done.2 = f32[32,2,8,128]{3,2,1,0:T(8,128)S(1)} async-done(((f32[32,2,8,128]{3,2,1,0:T(8,128)}), f32[32,2,8,128]{3,2,1,0:T(8,128)S(1)}, u32[]{:S(2)}, u32[]{:S(2)}) %all-to-all-start.2) | async-done | bytes 262176 | tf_op jit(solution)/shard_map/all_to_all | solution.py:387
  80.5 2.0 %adjoint.1 = (f32[8,16,128]{2,1,0:T(8,128)S(1)}, f32[512,128]{1,0:T(8,128)}) custom-call(f32[512,128]{1,0:T(8,128)S(1)} %bitcast.20, bf16[8,1024,128]{2,1,0:T(8,128)(2,1)S(1)} %get-tuple-element.16.refs_1_, bf16[320,256]{1,0:T(8,128)(2,1)S(1)} %get-tuple-element.17.refs_2_.tables_ref), custom_call_target="tpu_custom_call" | custom-call | tf_op jit(solution)/shard_map/adjoint/pallas_call | solution.py:366
  82.5 5.0 %all-to-all-start.3 = ((f32[32,2,8,128]{3,2,1,0:T(8,128)}), f32[32,2,8,128]{3,2,1,0:T(8,128)S(1)}, u32[]{:S(2)}, u32[]{:S(2)}) async-start(f32[32,2,8,128]{3,2,1,0:T(8,128)} %bitcast.7), calls=%async_computation.3 | async-start | bytes 524288 | tf_op jit(solution)/shard_map/all_to_all | solution.py:387
  87.6 3.0 %collective-permute-start.6 = (f32[8,16,128]{2,1,0:T(8,128)S(1)}, f32[8,16,128]{2,1,0:T(8,128)S(1)}, u32[]{:S(2)}, u32[]{:S(2)}) collective-permute-start(f32[8,16,128]{2,1,0:T(8,128)S(1)} %get-tuple-element.27), channel_id=1, source_target_pairs={{0,64},{32,96},{64,0},{96,32},{128,192},{160,224},{192,128},{224,1... | collective-permute-start | bytes 196616 | tf_op jit(solution)/shard_map/ppermute | solution.py:392
  90.6 0.8 collective-permute-start.5
  92.6 1.9 %collective-permute-done.5 = f32[8,16,128]{2,1,0:T(8,128)S(1)} collective-permute-done((f32[8,16,128]{2,1,0:T(8,128)S(1)}, f32[8,16,128]{2,1,0:T(8,128)S(1)}, u32[]{:S(2)}, u32[]{:S(2)}) %collective-permute-start.5) | collective-permute-done | bytes 65568 | tf_op jit(solution)/shard_map/ppermute | solution.py:392
  94.4 1.5 %collective-permute-done.4 = f32[8,16,128]{2,1,0:T(8,128)S(1)} collective-permute-done((f32[8,16,128]{2,1,0:T(8,128)S(1)}, f32[8,16,128]{2,1,0:T(8,128)S(1)}, u32[]{:S(2)}, u32[]{:S(2)}) %collective-permute-start.4) | collective-permute-done | bytes 65568 | tf_op jit(solution)/shard_map/ppermute | solution.py:392
  96.4 3.9 %collective-permute-done.3.u_far = f32[4,8,16,128]{3,2,1,0:T(8,128)S(1)} collective-permute-done((f32[4,8,16,128]{3,2,1,0:T(8,128)S(1)}, f32[4,8,16,128]{3,2,1,0:T(8,128)S(1)}, u32[]{:S(2)}, u32[]{:S(2)}) %collective-permute-start.3) | collective-permute-done | bytes 262176 | tf_op jit(solution)/shard_map/ppermute | solution.py:397
  100.3 5.6 %collective-permute-done.7.g_far = f32[4,8,16,128]{3,2,1,0:T(8,128)S(1)} collective-permute-done((f32[4,8,16,128]{3,2,1,0:T(8,128)S(1)}, f32[4,8,16,128]{3,2,1,0:T(8,128)S(1)}, u32[]{:S(2)}, u32[]{:S(2)}) %collective-permute-start.7) | collective-permute-done | bytes 262176 | tf_op jit(solution)/shard_map/ppermute | solution.py:397
  105.9 3.6 %weight_grads.1 = f32[8,16,64,128]{3,2,1,0:T(8,128)} custom-call(f32[4,8,16,128]{3,2,1,0:T(8,128)S(1)} %pad_maximum_fusion.u_near, f32[4,8,16,128]{3,2,1,0:T(8,128)S(1)} %collective-permute-done.3.u_far, f32[4,8,16,128]{3,2,1,0:T(8,128)S(1)} %pad_maximum_fusion.1.g_near, f32[4,8,16,128]{3,2,1,0:T(8,128)S(1)} %collective-permute-done.7.g_far), custom_call_target="tpu_custom_call" | custom-call | tf_op jit(solution)/shard_map/weight_grads/pallas_call | solution.py:461
  109.4 3.9 %final.1 = bf16[2,64,4096]{2,1,0:T(8,128)(2,1)} custom-call(f32[32,2,8,128]{3,2,1,0:T(8,128)S(1)} %all-to-all-done.3.w_ref, bf16[2,64,4096]{2,1,0:T(8,128)(2,1)S(1)} %copy-done.4, bf16[128,128]{1,0:T(8,128)(2,1)S(1)} %get-tuple-element.21.map_ref, bf16[320,256]{1,0:T(8,128)(2,1)S(1)} %get-tuple-element.17.refs_2_.tables_ref), custom_call_target="tpu_custom_call" | custom-call | tf_op jit(solution)/shard_map/final/pallas_call | solution.py:366
  (22 shorter events, 3.7 us)
Async XLA Ops:
  0.6 1.6 %copy-start = (bf16[8,16,64,128]{3,2,1,0:T(8,128)(2,1)S(1)}, bf16[8,16,64,128]{3,2,1,0:T(8,128)(2,1)}, u32[]{:S(2)}) copy-start(bf16[8,16,64,128]{3,2,1,0:T(8,128)(2,1)} %param.8) | copy-start | bytes 6291460
  2.2 1.2 %copy-start.1 = (bf16[1,2,64,4096]{3,2,1,0:T(8,128)(2,1)S(1)}, bf16[1,2,64,4096]{3,2,1,0:T(8,128)(2,1)}, u32[]{:S(2)}) copy-start(bf16[1,2,64,4096]{3,2,1,0:T(8,128)(2,1)} %param.6) | copy-start | bytes 3145732
  3.4 1.2 %copy-start.2 = (bf16[1,2,64,4096]{3,2,1,0:T(8,128)(2,1)S(1)}, bf16[1,2,64,4096]{3,2,1,0:T(8,128)(2,1)}, u32[]{:S(2)}) copy-start(bf16[1,2,64,4096]{3,2,1,0:T(8,128)(2,1)} %param.7) | copy-start | bytes 3145732
  4.7 0.9 copy-start.5
  5.6 0.7 copy-start.6
  6.3 0.7 copy-start.7
  61.0 1.0 copy-start.3
  62.0 18.6 %all-to-all-start.2 = ((f32[32,2,8,128]{3,2,1,0:T(8,128)}), f32[32,2,8,128]{3,2,1,0:T(8,128)S(1)}, u32[]{:S(2)}, u32[]{:S(2)}) async-start(f32[32,2,8,128]{3,2,1,0:T(8,128)} %get-tuple-element.23), calls=%async_computation.2 | async-start | bytes 524288 | tf_op jit(solution)/shard_map/all_to_all | solution.py:387
  67.0 24.3 %collective-permute-start.2 = (f32[8,16,128]{2,1,0:T(8,128)S(1)}, f32[8,16,128]{2,1,0:T(8,128)S(1)}, u32[]{:S(2)}, u32[]{:S(2)}) collective-permute-start(f32[8,16,128]{2,1,0:T(8,128)S(1)} %get-tuple-element.26), channel_id=1, source_target_pairs={{0,64},{32,96},{64,0},{96,32},{128,192},{160,224},{192,128},{224,1... | collective-permute-start | bytes 196616 | tf_op jit(solution)/shard_map/ppermute | solution.py:392
  70.0 22.0 %collective-permute-start.1 = (f32[8,16,128]{2,1,0:T(8,128)S(1)}, f32[8,16,128]{2,1,0:T(8,128)S(1)}, u32[]{:S(2)}, u32[]{:S(2)}) collective-permute-start(f32[8,16,128]{2,1,0:T(8,128)S(1)} %get-tuple-element.26), channel_id=1, source_target_pairs={{0,96},{32,0},{64,32},{96,64},{128,224},{160,128},{192,160},{224,1... | collective-permute-start | bytes 196616 | tf_op jit(solution)/shard_map/ppermute | solution.py:392
  70.8 21.3 %collective-permute-start = (f32[8,16,128]{2,1,0:T(8,128)S(1)}, f32[8,16,128]{2,1,0:T(8,128)S(1)}, u32[]{:S(2)}, u32[]{:S(2)}) collective-permute-start(f32[8,16,128]{2,1,0:T(8,128)S(1)} %get-tuple-element.26), channel_id=1, source_target_pairs={{0,32},{32,64},{64,96},{96,0},{128,160},{160,192},{192,224},{224,1... | collective-permute-start | bytes 196616 | tf_op jit(solution)/shard_map/ppermute | solution.py:392
  82.5 26.9 %all-to-all-start.3 = ((f32[32,2,8,128]{3,2,1,0:T(8,128)}), f32[32,2,8,128]{3,2,1,0:T(8,128)S(1)}, u32[]{:S(2)}, u32[]{:S(2)}) async-start(f32[32,2,8,128]{3,2,1,0:T(8,128)} %bitcast.7), calls=%async_computation.3 | async-start | bytes 524288 | tf_op jit(solution)/shard_map/all_to_all | solution.py:387
  87.6 5.0 %collective-permute-start.6 = (f32[8,16,128]{2,1,0:T(8,128)S(1)}, f32[8,16,128]{2,1,0:T(8,128)S(1)}, u32[]{:S(2)}, u32[]{:S(2)}) collective-permute-start(f32[8,16,128]{2,1,0:T(8,128)S(1)} %get-tuple-element.27), channel_id=1, source_target_pairs={{0,64},{32,96},{64,0},{96,32},{128,192},{160,224},{192,128},{224,1... | collective-permute-start | bytes 196616 | tf_op jit(solution)/shard_map/ppermute | solution.py:392
  90.6 3.9 %collective-permute-start.5 = (f32[8,16,128]{2,1,0:T(8,128)S(1)}, f32[8,16,128]{2,1,0:T(8,128)S(1)}, u32[]{:S(2)}, u32[]{:S(2)}) collective-permute-start(f32[8,16,128]{2,1,0:T(8,128)S(1)} %get-tuple-element.27), channel_id=1, source_target_pairs={{0,96},{32,0},{64,32},{96,64},{128,224},{160,128},{192,160},{224,1... | collective-permute-start | bytes 196616 | tf_op jit(solution)/shard_map/ppermute | solution.py:392
  91.3 4.6 %collective-permute-start.4 = (f32[8,16,128]{2,1,0:T(8,128)S(1)}, f32[8,16,128]{2,1,0:T(8,128)S(1)}, u32[]{:S(2)}, u32[]{:S(2)}) collective-permute-start(f32[8,16,128]{2,1,0:T(8,128)S(1)} %get-tuple-element.27), channel_id=1, source_target_pairs={{0,32},{32,64},{64,96},{96,0},{128,160},{160,192},{192,224},{224,1... | collective-permute-start | bytes 196616 | tf_op jit(solution)/shard_map/ppermute | solution.py:392
  92.1 8.2 %collective-permute-start.3 = (f32[4,8,16,128]{3,2,1,0:T(8,128)S(1)}, f32[4,8,16,128]{3,2,1,0:T(8,128)S(1)}, u32[]{:S(2)}, u32[]{:S(2)}) collective-permute-start(f32[4,8,16,128]{3,2,1,0:T(8,128)S(1)} %pad_maximum_fusion.u_near), channel_id=1, source_target_pairs={{0,128},{32,160},{64,192},{96,224},{128,0},{160,32},{192,64},{224,... | collective-permute-start | bytes 786440 | tf_op jit(solution)/shard_map/ppermute | solution.py:397
  96.0 13.5 %copy-start.4 = (bf16[2,64,4096]{2,1,0:T(8,128)(2,1)S(1)}, bf16[2,64,4096]{2,1,0:T(8,128)(2,1)}, u32[]{:S(2)}) copy-start(bf16[2,64,4096]{2,1,0:T(8,128)(2,1)} %copy-done.3) | copy-start | bytes 3145732
  96.0 9.9 %collective-permute-start.7 = (f32[4,8,16,128]{3,2,1,0:T(8,128)S(1)}, f32[4,8,16,128]{3,2,1,0:T(8,128)S(1)}, u32[]{:S(2)}, u32[]{:S(2)}) collective-permute-start(f32[4,8,16,128]{3,2,1,0:T(8,128)S(1)} %pad_maximum_fusion.1.g_near), channel_id=1, source_target_pairs={{0,128},{32,160},{64,192},{96,224},{128,0},{160,32},{192,64},{224,... | collective-permute-start | bytes 786440 | tf_op jit(solution)/shard_map/ppermute | solution.py:397

commit v2 on v1

--- a/solution.py
+++ b/solution.py
@@ -197,90 +197,111 @@
     return pl.ds(pl.multiple_of(step * tiles * 128, tiles * 128), tiles * 128)
 
 
-def analyse_kernel(
-    field_in, cot_in, w_in, tables_in, map_in, bias_in,
-    out_ref, field_ref, cot_ref, w_ref, tables_ref, map_ref, bias_ref,
-    scratch, small_map, small_bias, sems,
-):
-    copies = [
-        pltpu.make_async_copy(source, target, sems.at[i])
-        for i, (source, target) in enumerate(
-            [
-                (tables_in, tables_ref),
-                (field_in.at[0], field_ref.at[0]),
-                (field_in.at[1], field_ref.at[1]),
-                (map_in, small_map),
-                (bias_in, small_bias),
-                (w_in, w_ref),
-                (cot_in, cot_ref),
-            ]
-        )
-    ]
+HALF = N * C // 2
+
+
+def start_all(sems, *moves):
+    copies = [pltpu.make_async_copy(*move, sems.at[i]) for i, move in enumerate(moves)]
     for copy in copies:
         copy.start()
+    return copies
+
+
+def analyse_kernel(
+    field_in, w_in, tables_in, map_in, bias_in,
+    out_ref, w_ref, tables_ref, map_ref, bias_ref,
+    field, scratch, small_map, small_bias, sems,
+):
+    parts = [(i // 2, slice(None), pl.ds(i % 2 * HALF, HALF)) for i in range(2 * CX)]
+    copies = start_all(
+        sems,
+        (tables_in, tables_ref),
+        *((field_in.at[part], field.at[part]) for part in parts),
+        (map_in, small_map),
+        (bias_in, small_bias),
+        (w_in, w_ref),
+    )
     copies[0].wait()
-    y_in, t_table = table(tables_ref, "y_in"), table(tables_ref, "t_in")
-    for x in range(CX):
-        copies[1 + x].wait()
-
-        @pl.loop(0, TP // Y_TILES)
+    y_in, t_in = table(tables_ref, "y_in"), table(tables_ref, "t_in")
+    for i in range(2 * CX):
+        copies[1 + i].wait()
+
+        @pl.loop(i % 2 * TP // 2 // Y_TILES, (i % 2 + 1) * TP // 2 // Y_TILES)
         def _(step):
             y_analysis_store(
-                field_ref[x, :, lane_slice(step, Y_TILES)], step * Y_TILES, Y_TILES, y_in, scratch
+                field[i // 2, :, lane_slice(step, Y_TILES)], step * Y_TILES, Y_TILES, y_in, scratch
             )
 
-        t_analysis(scratch, t_table, out_ref, x)
-    copies[3].wait()
-    copies[4].wait()
+        if i % 2 == 1:
+            t_analysis(scratch, t_in, out_ref, i // 2)
+    for copy in copies[1 + 2 * CX :]:
+        copy.wait()
     wide_map = jnp.concatenate([small_map[...]] * 2, 1)
     wide_map = jnp.concatenate([wide_map] * 2, 0)
     row = lax.broadcasted_iota(jnp.int32, (2 * C, 2 * C), 0) // C
     lane = lax.broadcasted_iota(jnp.int32, (2 * C, 2 * C), 1) // C
     map_ref[...] = jnp.where(row == lane, wide_map, jnp.zeros_like(wide_map))
     bias_ref[...] = jnp.concatenate([small_bias[...]] * 2, 1)
-    copies[5].wait()
-    copies[6].wait()
 
 
 def gelu_slope(z):
-    inner = SQRT_TWO_PI * (z + 0.044715 * z * z * z)
-    tanh_value = jnp.tanh(inner)
-    return 0.5 * (1.0 + tanh_value) + 0.5 * z * (1.0 - tanh_value * tanh_value) * SQRT_TWO_PI * (
-        1.0 + 3.0 * 0.044715 * z * z
-    )
-
-
-def middle_kernel(w_ref, field_ref, cot_ref, map_ref, bias_ref, tables_ref, gz_ref, out_ref, syn, ana):
+    square = z * z
+    tanh_value = jnp.tanh(z * (SQRT_TWO_PI + SQRT_TWO_PI * 0.044715 * square))
+    inner_slope = z * (0.5 * SQRT_TWO_PI + 1.5 * SQRT_TWO_PI * 0.044715 * square)
+    return 0.5 + 0.5 * tanh_value + inner_slope * (1.0 - tanh_value * tanh_value)
+
+
+def middle_kernel(
+    w_ref, field_in, cot_in, map_ref, bias_ref, tables_ref, gz_out, out_ref, field, cot, gz, syn, ana, sems
+):
+    copies = start_all(
+        sems,
+        (field_in.at[0], field.at[0]),
+        (cot_in.at[0], cot.at[0]),
+        (field_in.at[1], field.at[1]),
+        (cot_in.at[1], cot.at[1]),
+    )
+    backs = [pltpu.make_async_copy(gz.at[x], gz_out.at[x], sems.at[len(copies) + x]) for x in range(CX)]
     y_in, y_out, t_in, t_out = (table(tables_ref, name) for name in ("y_in", "y_out", "t_in", "t_out"))
-
-    @pl.loop(0, CX)
-    def _(x):
+    for x in range(CX):
         t_synthesis(w_ref, t_out, syn, x)
+        copies[2 * x].wait()
+        copies[2 * x + 1].wait()
 
         @pl.loop(0, TP // Y_TILES)
         def _(step):
             at = lane_slice(step, Y_TILES)
             spec = y_synthesis(syn, step * Y_TILES, Y_TILES, y_out)
-            z = spec + channel_map(field_ref[x, :, at], map_ref[...], Y_TILES) + lanes([bias_ref[...]] * Y_TILES)
-            gz = (cot_ref[x, :, at].astype(F32) * gelu_slope(z)).astype(BF)
-            gz_ref[x, :, at] = gz
-            y_analysis_store(gz, step * Y_TILES, Y_TILES, y_in, ana)
-
+            z = spec + channel_map(field[x, :, at], map_ref[...], Y_TILES) + lanes([bias_ref[...]] * Y_TILES)
+            out = (cot[x, :, at].astype(F32) * gelu_slope(z)).astype(BF)
+            gz[x, :, at] = out
+            y_analysis_store(out, step * Y_TILES, Y_TILES, y_in, ana)
+
+        backs[x].start()
         t_analysis(ana, t_in, out_ref, x)
-
-
-def final_kernel(w_ref, gz_ref, map_ref, tables_ref, out_ref, syn):
+    for back in backs:
+        back.wait()
+
+
+def final_kernel(w_ref, gz_in, map_ref, tables_ref, grad_out, gz, grad, syn, sems):
+    copies = start_all(sems, (gz_in.at[0], gz.at[0]), (gz_in.at[1], gz.at[1]))
+    backs = [
+        pltpu.make_async_copy(grad.at[x], grad_out.at[x], sems.at[len(copies) + x]) for x in range(CX)
+    ]
     y_out, t_out = table(tables_ref, "y_out"), table(tables_ref, "t_out")
-
-    @pl.loop(0, CX)
-    def _(x):
+    for x in range(CX):
         t_synthesis(w_ref, t_out, syn, x)
+        copies[x].wait()
 
         @pl.loop(0, TP // Y_TILES)
         def _(step):
             at = lane_slice(step, Y_TILES)
             spec = y_synthesis(syn, step * Y_TILES, Y_TILES, y_out)
-            out_ref[x, :, at] = (spec + channel_map(gz_ref[x, :, at], map_ref[...], Y_TILES, 1)).astype(BF)
+            grad[x, :, at] = (spec + channel_map(gz[x, :, at], map_ref[...], Y_TILES, 1)).astype(BF)
+
+        backs[x].start()
+    for back in backs:
+        back.wait()
 
 
 M = 8
@@ -344,34 +365,49 @@
 G_MODES = 2
 
 
-def grads_kernel(u_near, u_far, g_near, g_far, out_ref):
-    own = lax.broadcasted_iota(jnp.int32, (C, 2 * DP * K), 1) % K
+def grads_kernel(*refs):
+    u_refs, g_refs, out_ref = refs[:Y_RING], refs[Y_RING : 2 * Y_RING], refs[-1]
+    own = lax.broadcasted_iota(jnp.int32, (C, 2 * DP * K), 1) % K // 2
+    odd = lax.broadcasted_iota(jnp.int32, (2 * DP * K, 1), 0) % 2 == 1
     for j in range(G_MODES):
         m = pl.program_id(0) * G_MODES + j
-        u = jnp.concatenate([ref[b, m] for ref in (u_near, u_far) for b in range(DP // 2)], 0)
-        g = jnp.concatenate([ref[b, m] for ref in (g_near, g_far) for b in range(DP // 2)], 0)
+        u, g = (
+            jnp.concatenate([ref[b, m] for ref in part for b in range(DP // Y_RING)], 0)
+            for part in (u_refs, g_refs)
+        )
         u_t = u.T.astype(BF)
         left = lanes([u_t[:C], u_t[C:]])
-        right = jnp.concatenate([g, -turned(g)], 0).astype(BF)
-        tall = jnp.concatenate([jnp.where(own == kx, left, jnp.zeros_like(left)) for kx in range(K)], 0)
-        out_ref[j] = dot(tall, right).reshape(K, C, 2 * C)
-
-
-PARAMS = pltpu.CompilerParams(vmem_limit_bytes=32 * 1024 * 1024)
+        right = jnp.concatenate([g, -turned(g)], 0)
+        right = lanes([jnp.where(odd, 0.0, right), jnp.where(odd, right, 0.0)]).astype(BF)
+        tall = jnp.concatenate([jnp.where(own == q, left, jnp.zeros_like(left)) for q in range(K // 2)], 0)
+        out = dot(tall, right)
+        for kx in range(K):
+            out_ref[j, kx] = out[kx // 2 * C : (kx // 2 + 1) * C, kx % 2 * 128 : (kx % 2 + 1) * 128]
+
+
+LIMIT = 32
 IN_VMEM = pl.BlockSpec(memory_space=pltpu.VMEM)
 IN_HBM = pl.BlockSpec(memory_space=pltpu.HBM)
 
 
-def vmem_call(kernel, name, out_shapes, scratch, *operands, specs=None):
+def call(kernel, name, out_shapes, out_specs, scratch, *operands, specs):
     return pl.pallas_call(
         kernel,
         name=name,
         out_shape=out_shapes,
-        in_specs=specs or [IN_VMEM] * len(operands),
-        out_specs=jax.tree.map(lambda _: IN_VMEM, out_shapes),
+        in_specs=specs,
+        out_specs=out_specs,
         scratch_shapes=scratch,
-        compiler_params=PARAMS,
+        compiler_params=pltpu.CompilerParams(vmem_limit_bytes=LIMIT * 2**20),
     )(*operands)
+
+
+def in_vmem(*arrays):
+    return [pltpu.with_memory_space_constraint(array, pltpu.VMEM) for array in arrays]
+
+
+def in_hbm(*arrays):
+    return [pltpu.with_memory_space_constraint(array, pltpu.HBM) for array in arrays]
 
 
 def shape(dims, kind=F32):
@@ -387,86 +423,92 @@
     return lax.all_to_all(data, "slab", 0, 0, tiled=True)
 
 
-def gather_samples(data):
+def x_pair(data):
+    return jnp.stack([data, lax.ppermute(data, "dp", [(i, (i + Y_RING) % DP) for i in range(DP)])], 0)
+
+
+def y_ring(data):
     def moved(by):
         return lax.ppermute(
             data, "dp", [(i, i // Y_RING * Y_RING + (i + by) % Y_RING) for i in range(DP)]
         )
 
-    near = jnp.stack([data, moved(1), moved(3), moved(2)], 0)
-    return near, lax.ppermute(near, "dp", [(i, (i + Y_RING) % DP) for i in range(DP)])
+    return [data, moved(1), moved(3), moved(2)]
 
 
 def body(field, cotangent, mode_weights, w_local, bias):
     grid_shape = (CX, N, N * C)
+    on_grid = pltpu.VMEM(grid_shape, BF)
+    values, cot = field.reshape(grid_shape), cotangent.reshape(grid_shape)
 
     def spectral(adjoint, data):
-        return vmem_call(
+        return call(
             lambda *refs: spectral_kernel(adjoint, *refs),
             "adjoint" if adjoint else "mix",
             (shape((M, K, 128)), shape((N * M, 128))),
+            [IN_VMEM] * 2,
             [],
             data.reshape(N * M, 128),
-            weights,
-            tables,
+            *in_vmem(weights, tables),
+            specs=[IN_VMEM] * 3,
         )
 
-    first, values, cot, weights, tables, wide_map, wide_bias = vmem_call(
+    first, weights, tables, wide_map, wide_bias = call(
         analyse_kernel,
         "analyse",
         (
             SPECTRA,
-            shape(grid_shape, BF),
-            shape(grid_shape, BF),
-            shape((M, K * C, 2 * C), BF),
-            shape(PACKED.shape, BF),
-            shape((2 * C, 2 * C), BF),
-            shape((1, 2 * C)),
+            pltpu.VMEM((M, K * C, 2 * C), BF),
+            pltpu.VMEM(PACKED.shape, BF),
+            pltpu.VMEM((2 * C, 2 * C), BF),
+            pltpu.VMEM((1, 2 * C), F32),
         ),
-        [ROWS, pltpu.VMEM((C, C), BF), pltpu.VMEM((1, C), F32), pltpu.SemaphoreType.DMA((7,))],
-        field.reshape(grid_shape),
-        cotangent.reshape(grid_shape),
-        mode_weights.reshape(M, K * C, 2 * C),
-        jnp.asarray(PACKED),
-        w_local,
-        bias.reshape(1, C),
-        specs=[IN_HBM] * 6,
+        [IN_VMEM] * 5,
+        [on_grid, ROWS, pltpu.VMEM((C, C), BF), pltpu.VMEM((1, C), F32), pltpu.SemaphoreType.DMA((8,))],
+        *in_hbm(
+            values, mode_weights.reshape(M, K * C, 2 * C), jnp.asarray(PACKED), w_local, bias.reshape(1, C)
+        ),
+        specs=[IN_HBM] * 5,
     )
     u_hat, mixed = spectral(False, exchange(first))
-    u_near, u_far = gather_samples(u_hat)
-    gz, second = vmem_call(
+    u_pair = x_pair(u_hat)
+    arrived, u_pair = lax.optimization_barrier((exchange(mixed.reshape(SPECTRA.shape)), u_pair))
+    gz, second = call(
         middle_kernel,
         "middle",
-        (shape(grid_shape, BF), SPECTRA),
-        [ROWS, ROWS],
-        exchange(mixed.reshape(SPECTRA.shape)),
-        values,
-        cot,
-        wide_map,
-        wide_bias,
-        tables,
-    )
-    g_hat, back = spectral(True, exchange(second))
-    g_near, g_far = gather_samples(g_hat)
-    grad_field = vmem_call(
+        (pltpu.HBM(grid_shape, BF), SPECTRA),
+        [IN_HBM, IN_VMEM],
+        [on_grid, on_grid, on_grid, ROWS, ROWS, pltpu.SemaphoreType.DMA((6,))],
+        arrived,
+        *in_hbm(values, cot),
+        *in_vmem(wide_map, wide_bias, tables),
+        specs=[IN_VMEM] + [IN_HBM] * 2 + [IN_VMEM] * 3,
+    )
+    u_all = y_ring(u_pair)
+    arrived, u_all = lax.optimization_barrier((exchange(second), u_all))
+    g_hat, back = spectral(True, arrived)
+    g_all = y_ring(x_pair(g_hat))
+    grad_field = call(
         final_kernel,
         "final",
-        shape(grid_shape, BF),
-        [ROWS],
+        pltpu.HBM(grid_shape, BF),
+        IN_HBM,
+        [on_grid, on_grid, ROWS, pltpu.SemaphoreType.DMA((4,))],
         exchange(back.reshape(SPECTRA.shape)),
-        gz,
-        wide_map,
-        tables,
-    )
+        *in_hbm(gz),
+        *in_vmem(wide_map, tables),
+        specs=[IN_VMEM, IN_HBM] + [IN_VMEM] * 2,
+    )
+    grad_field, g_all = lax.optimization_barrier((grad_field, g_all))
     grad_modes = pl.pallas_call(
         grads_kernel,
         name="weight_grads",
         grid=(M // G_MODES,),
         out_shape=shape((M, K, C, 2 * C)),
-        in_specs=[IN_VMEM] * 4,
+        in_specs=[IN_VMEM] * 2 * Y_RING,
         out_specs=pl.BlockSpec((G_MODES, K, C, 2 * C), lambda m: (m, 0, 0, 0)),
-        compiler_params=PARAMS,
-    )(u_near, u_far, g_near, g_far)
+        compiler_params=pltpu.CompilerParams(vmem_limit_bytes=LIMIT * 2**20),
+    )(*u_all, *g_all)
     return grad_field.reshape(field.shape), grad_modes
 
 

time: 114 us -> 106 us (0.930)
  blocking collectives: 43.5 us -> 25.8 us
  waiting for transfers between devices: 22.1 us -> 31.3 us
  local copies, waits for them, and re-layouts: 7.29 us -> 0 us
  starting transfers between devices: 19.8 us -> 26.1 us
  Pallas kernels: 20 us -> 22 us
    all_to_all x2 -> x1, blocking collectives: 43.5 us -> 25.8 us  [exchange(): return lax.all_to_all(data, 'slab', 0, 0, tiled=True)]
    all_to_all x2 -> x3, waiting for transfers between devices: 9.08 us -> 19.8 us  [exchange(): return lax.all_to_all(data, 'slab', 0, 0, tiled=True)]
    unnamed x16 -> x0, local copies, waits for them, and re-layouts: 7.29 us -> none
    all_to_all x2 -> x3, starting transfers between devices: 10 us -> 17 us  [exchange(): return lax.all_to_all(data, 'slab', 0, 0, tiled=True)]
    ppermute x2, waiting for transfers between devices: 9.48 us -> 6.5 us  [x_pair(): lax.ppermute(data, 'dp', [(i, (i + Y_RING) % DP) for i in range(DP)])]
    pallas_call x5, Pallas kernels: 16.5 us -> 18.9 us  [call(): pl.pallas_call(kernel, name=name, out_shape=out_shapes, in_specs=specs, o...]
    ppermute x6, waiting for transfers between devices: 3.5 us -> 5.02 us  [moved(): lax.ppermute(data, 'dp', [(i, i // Y_RING * Y_RING + (i + by) % Y_RING) f...]
  transfers between devices with their start and end apart: 10 -> 11, of which waited for: 6 -> 7; matrix products, arithmetic and copies ran while one was open for 0% -> 0% of each run, Pallas kernels for 5% -> 4%
where the time goes in v2:
time: 106 us
  waiting for transfers between devices  31.3 us (30%)
  starting transfers between devices  26.1 us (25%)
  blocking collectives  25.8 us (24%)
  Pallas kernels  22 us (21%)
    all_to_all x1, blocking collectives, exchange(): return lax.all_to_all(data, 'slab', 0, 0, tiled=True)  25.8 us
    all_to_all x3, waiting for transfers between devices, exchange(): return lax.all_to_all(data, 'slab', 0, 0, tiled=True)  19.8 us
    pallas_call x5, Pallas kernels, call(): pl.pallas_call(kernel, name=name, out_shape=out_shapes, in_specs=specs, o...  18.9 us
    all_to_all x3, starting transfers between devices, exchange(): return lax.all_to_all(data, 'slab', 0, 0, tiled=True)  17 us
    ppermute x6, starting transfers between devices, moved(): lax.ppermute(data, 'dp', [(i, i // Y_RING * Y_RING + (i + by) % Y_RING) f...  8.32 us
    ppermute x2, waiting for transfers between devices, x_pair(): lax.ppermute(data, 'dp', [(i, (i + Y_RING) % DP) for i in range(DP)])  6.5 us
    ppermute x6, waiting for transfers between devices, moved(): lax.ppermute(data, 'dp', [(i, i // Y_RING * Y_RING + (i + by) % Y_RING) f...  5.02 us
    pallas_call x1, Pallas kernels, body(): pl.pallas_call(grads_kernel, name='weight_grads', grid=(M // G_MODES,), o...  3.18 us
  transfers between devices with their start and end apart: 11, of which 7 were waited for; matrix products, arithmetic and copies ran while one was open for 0% of the time, Pallas kernels for 4%

profile of v2, /device:TPU:1, one launch (start us, length us, event | category | flops | bytes accessed | tf_op | source)
XLA Modules:
  0.0 106.1 jit_solution(18060791447324180644)
XLA Ops:
  0.6 3.5 %analyse.1 = (f32[32,2,8,128]{3,2,1,0:T(8,128)S(1)}, bf16[8,1024,128]{2,1,0:T(8,128)(2,1)S(1)}, bf16[320,256]{1,0:T(8,128)(2,1)S(1)}, bf16[128,128]{1,0:T(8,128)(2,1)S(1)}, f32[1,128]{1,0:T(1,128)S(1)}) custom-call(bf16[2,64,4096]{2,1,0:T(8,128)(2,1)} %bitcast.17, bf16[8,1024,128]{2,1,0:T(8,128)(2,1)} %bitcast.19, bf16[320,256]{1,0:T(8,128)(2,1)} %constant.2.clone.tables_in, ...), custom_call_target="tpu_custom_call" | custom-call | tf_op jit(solution)/shard_map/analyse/pallas_call | solution.py:394
  4.1 25.8 %all_to_all.20 = f32[32,2,8,128]{3,2,1,0:T(8,128)S(1)} all-to-all(f32[32,2,8,128]{3,2,1,0:T(8,128)S(1)} %get-tuple-element.25), channel_id=1, replica_groups=mesh['dp'=8,'slab'=32] {'slab'}, dimensions={0} | all-to-all | bytes 524288 | tf_op jit(solution)/shard_map/all_to_all | solution.py:423
  29.9 1.7 %mix.1 = (f32[8,16,128]{2,1,0:T(8,128)S(1)}, f32[512,128]{1,0:T(8,128)}) custom-call(f32[512,128]{1,0:T(8,128)S(1)} %bitcast.14, bf16[8,1024,128]{2,1,0:T(8,128)(2,1)S(1)} %get-tuple-element.26.refs_1_, bf16[320,256]{1,0:T(8,128)(2,1)S(1)} %get-tuple-element.27.refs_2_.tables_ref), custom_call_target="tpu_custom_call" | custom-call | tf_op jit(solution)/shard_map/mix/pallas_call | solution.py:394
  31.6 5.0 %all-to-all-start.1 = ((f32[32,2,8,128]{3,2,1,0:T(8,128)}), f32[32,2,8,128]{3,2,1,0:T(8,128)S(1)}, u32[]{:S(2)}, u32[]{:S(2)}) async-start(f32[32,2,8,128]{3,2,1,0:T(8,128)} %bitcast.4), calls=%async_computation.1 | async-start | bytes 524288 | tf_op jit(solution)/shard_map/all_to_all | solution.py:423
  37.1 3.2 %collective-permute-done = f32[8,16,128]{2,1,0:T(8,128)S(1)} collective-permute-done((f32[8,16,128]{2,1,0:T(8,128)S(1)}, f32[8,16,128]{2,1,0:T(8,128)S(1)}, u32[]{:S(2)}, u32[]{:S(2)}) %collective-permute-start) | collective-permute-done | bytes 65568 | tf_op jit(solution)/shard_map/ppermute | solution.py:427
  40.2 9.9 %all-to-all-done.1.w_ref = f32[32,2,8,128]{3,2,1,0:T(8,128)S(1)} async-done(((f32[32,2,8,128]{3,2,1,0:T(8,128)}), f32[32,2,8,128]{3,2,1,0:T(8,128)S(1)}, u32[]{:S(2)}, u32[]{:S(2)}) %all-to-all-start.1) | async-done | bytes 262176 | tf_op jit(solution)/shard_map/all_to_all | solution.py:423
  50.2 7.2 %middle.1 = (bf16[2,64,4096]{2,1,0:T(8,128)(2,1)}, f32[32,2,8,128]{3,2,1,0:T(8,128)}) custom-call(f32[32,2,8,128]{3,2,1,0:T(8,128)S(1)} %all-to-all-done.1.w_ref, bf16[2,64,4096]{2,1,0:T(8,128)(2,1)} %bitcast.18, bf16[2,64,4096]{2,1,0:T(8,128)(2,1)} %bitcast.20, bf16[128,128]{1,0:T(8,128)(2,1)S(1)} %get-tuple-element.31.map_ref, ...), custom_call_target="tpu_custom_call" | custom-call | tf_op jit(solution)/shard_map/middle/pallas_call | solution.py:394
  57.4 5.0 %all-to-all-start.2 = ((f32[32,2,8,128]{3,2,1,0:T(8,128)}), f32[32,2,8,128]{3,2,1,0:T(8,128)S(1)}, u32[]{:S(2)}, u32[]{:S(2)}) async-start(f32[32,2,8,128]{3,2,1,0:T(8,128)} %get-tuple-element.33), calls=%async_computation.2 | async-start | bytes 524288 | tf_op jit(solution)/shard_map/all_to_all | solution.py:423
  62.4 3.0 %collective-permute-start.3 = (f32[2,8,16,128]{3,2,1,0:T(8,128)S(1)}, f32[2,8,16,128]{3,2,1,0:T(8,128)S(1)}, u32[]{:S(2)}, u32[]{:S(2)}) collective-permute-start(f32[2,8,16,128]{3,2,1,0:T(8,128)S(1)} %pad_maximum_fusion.refs_0_), channel_id=1, source_target_pairs={{0,64},{32,96},{64,0},{96,32},{128,192},{160,224},{192,128},{224,1... | collective-permute-start | bytes 393224 | tf_op jit(solution)/shard_map/ppermute | solution.py:432
  65.4 0.8 collective-permute-start.2
  66.2 0.7 collective-permute-start.1
  66.9 1.9 %collective-permute-done.3.refs_3_ = f32[2,8,16,128]{3,2,1,0:T(8,128)S(1)} collective-permute-done((f32[2,8,16,128]{3,2,1,0:T(8,128)S(1)}, f32[2,8,16,128]{3,2,1,0:T(8,128)S(1)}, u32[]{:S(2)}, u32[]{:S(2)}) %collective-permute-start.3) | collective-permute-done | bytes 131104 | tf_op jit(solution)/shard_map/ppermute | solution.py:432
  68.8 3.2 %collective-permute-done.2.refs_2_ = f32[2,8,16,128]{3,2,1,0:T(8,128)S(1)} collective-permute-done((f32[2,8,16,128]{3,2,1,0:T(8,128)S(1)}, f32[2,8,16,128]{3,2,1,0:T(8,128)S(1)}, u32[]{:S(2)}, u32[]{:S(2)}) %collective-permute-start.2) | collective-permute-done | bytes 131104 | tf_op jit(solution)/shard_map/ppermute | solution.py:432
  71.9 4.1 %all-to-all-done.2 = f32[32,2,8,128]{3,2,1,0:T(8,128)S(1)} async-done(((f32[32,2,8,128]{3,2,1,0:T(8,128)}), f32[32,2,8,128]{3,2,1,0:T(8,128)S(1)}, u32[]{:S(2)}, u32[]{:S(2)}) %all-to-all-start.2) | async-done | bytes 262176 | tf_op jit(solution)/shard_map/all_to_all | solution.py:423
  76.0 2.0 %adjoint.1 = (f32[8,16,128]{2,1,0:T(8,128)S(1)}, f32[512,128]{1,0:T(8,128)}) custom-call(f32[512,128]{1,0:T(8,128)S(1)} %bitcast.13, bf16[8,1024,128]{2,1,0:T(8,128)(2,1)S(1)} %get-tuple-element.26.refs_1_, bf16[320,256]{1,0:T(8,128)(2,1)S(1)} %get-tuple-element.27.refs_2_.tables_ref), custom_call_target="tpu_custom_call" | custom-call | tf_op jit(solution)/shard_map/adjoint/pallas_call | solution.py:394
  78.0 7.0 %all-to-all-start.3 = ((f32[32,2,8,128]{3,2,1,0:T(8,128)}), f32[32,2,8,128]{3,2,1,0:T(8,128)S(1)}, u32[]{:S(2)}, u32[]{:S(2)}) async-start(f32[32,2,8,128]{3,2,1,0:T(8,128)} %bitcast.9), calls=%async_computation.3 | async-start | bytes 524288 | tf_op jit(solution)/shard_map/all_to_all | solution.py:423
  85.0 0.4 collective-permute-start.4
  85.4 3.3 %collective-permute-done.4 = f32[8,16,128]{2,1,0:T(8,128)S(1)} collective-permute-done((f32[8,16,128]{2,1,0:T(8,128)S(1)}, f32[8,16,128]{2,1,0:T(8,128)S(1)}, u32[]{:S(2)}, u32[]{:S(2)}) %collective-permute-start.4) | collective-permute-done | bytes 65568 | tf_op jit(solution)/shard_map/ppermute | solution.py:427
  88.7 2.4 %collective-permute-start.7 = (f32[2,8,16,128]{3,2,1,0:T(8,128)S(1)}, f32[2,8,16,128]{3,2,1,0:T(8,128)S(1)}, u32[]{:S(2)}, u32[]{:S(2)}) collective-permute-start(f32[2,8,16,128]{3,2,1,0:T(8,128)S(1)} %pad_maximum_fusion.1.refs_4_), channel_id=1, source_target_pairs={{0,64},{32,96},{64,0},{96,32},{128,192},{160,224},{192,128},{224,1... | collective-permute-start | bytes 393224 | tf_op jit(solution)/shard_map/ppermute | solution.py:432
  91.1 0.9 collective-permute-start.6
  92.0 0.6 collective-permute-start.5
  92.6 5.8 %all-to-all-done.3.w_ref = f32[32,2,8,128]{3,2,1,0:T(8,128)S(1)} async-done(((f32[32,2,8,128]{3,2,1,0:T(8,128)}), f32[32,2,8,128]{3,2,1,0:T(8,128)S(1)}, u32[]{:S(2)}, u32[]{:S(2)}) %all-to-all-start.3) | async-done | bytes 262176 | tf_op jit(solution)/shard_map/all_to_all | solution.py:423
  98.4 4.4 %final.1 = bf16[2,64,4096]{2,1,0:T(8,128)(2,1)} custom-call(f32[32,2,8,128]{3,2,1,0:T(8,128)S(1)} %all-to-all-done.3.w_ref, bf16[2,64,4096]{2,1,0:T(8,128)(2,1)} %get-tuple-element.37.gz_in, bf16[128,128]{1,0:T(8,128)(2,1)S(1)} %get-tuple-element.31.map_ref, bf16[320,256]{1,0:T(8,128)(2,1)S(1)} %get-tuple-element.27.refs_2_.tables_ref), custom_call_target="tpu_custom_call" | custom-call | tf_op jit(solution)/shard_map/final/pallas_call | solution.py:394
  102.9 3.2 %weight_grads.1 = f32[8,16,64,128]{3,2,1,0:T(8,128)} custom-call(f32[2,8,16,128]{3,2,1,0:T(8,128)S(1)} %pad_maximum_fusion.refs_0_, f32[2,8,16,128]{3,2,1,0:T(8,128)S(1)} %collective-permute-done.1.refs_1_, f32[2,8,16,128]{3,2,1,0:T(8,128)S(1)} %collective-permute-done.2.refs_2_, f32[2,8,16,128]{3,2,1,0:T(8,128)S(1)} %collective-permute-done.3.refs_3_, ...), custom_call_target="tpu_custom_call" | custom-call | tf_op jit(solution)/shard_map/weight_grads/pallas_call | solution.py:503
  (7 shorter events, 0.4 us)
Async XLA Ops:
  31.6 18.6 %all-to-all-start.1 = ((f32[32,2,8,128]{3,2,1,0:T(8,128)}), f32[32,2,8,128]{3,2,1,0:T(8,128)S(1)}, u32[]{:S(2)}, u32[]{:S(2)}) async-start(f32[32,2,8,128]{3,2,1,0:T(8,128)} %bitcast.4), calls=%async_computation.1 | async-start | bytes 524288 | tf_op jit(solution)/shard_map/all_to_all | solution.py:423
  36.6 3.6 %collective-permute-start = (f32[8,16,128]{2,1,0:T(8,128)S(1)}, f32[8,16,128]{2,1,0:T(8,128)S(1)}, u32[]{:S(2)}, u32[]{:S(2)}) collective-permute-start(f32[8,16,128]{2,1,0:T(8,128)S(1)} %get-tuple-element.29), channel_id=1, source_target_pairs={{0,128},{32,160},{64,192},{96,224},{128,0},{160,32},{192,64},{224,... | collective-permute-start | bytes 196616 | tf_op jit(solution)/shard_map/ppermute | solution.py:427
  57.4 18.6 %all-to-all-start.2 = ((f32[32,2,8,128]{3,2,1,0:T(8,128)}), f32[32,2,8,128]{3,2,1,0:T(8,128)S(1)}, u32[]{:S(2)}, u32[]{:S(2)}) async-start(f32[32,2,8,128]{3,2,1,0:T(8,128)} %get-tuple-element.33), calls=%async_computation.2 | async-start | bytes 524288 | tf_op jit(solution)/shard_map/all_to_all | solution.py:423
  62.4 6.3 %collective-permute-start.3 = (f32[2,8,16,128]{3,2,1,0:T(8,128)S(1)}, f32[2,8,16,128]{3,2,1,0:T(8,128)S(1)}, u32[]{:S(2)}, u32[]{:S(2)}) collective-permute-start(f32[2,8,16,128]{3,2,1,0:T(8,128)S(1)} %pad_maximum_fusion.refs_0_), channel_id=1, source_target_pairs={{0,64},{32,96},{64,0},{96,32},{128,192},{160,224},{192,128},{224,1... | collective-permute-start | bytes 393224 | tf_op jit(solution)/shard_map/ppermute | solution.py:432
  65.4 6.5 %collective-permute-start.2 = (f32[2,8,16,128]{3,2,1,0:T(8,128)S(1)}, f32[2,8,16,128]{3,2,1,0:T(8,128)S(1)}, u32[]{:S(2)}, u32[]{:S(2)}) collective-permute-start(f32[2,8,16,128]{3,2,1,0:T(8,128)S(1)} %pad_maximum_fusion.refs_0_), channel_id=1, source_target_pairs={{0,96},{32,0},{64,32},{96,64},{128,224},{160,128},{192,160},{224,1... | collective-permute-start | bytes 393224 | tf_op jit(solution)/shard_map/ppermute | solution.py:432
  66.2 5.7 %collective-permute-start.1 = (f32[2,8,16,128]{3,2,1,0:T(8,128)S(1)}, f32[2,8,16,128]{3,2,1,0:T(8,128)S(1)}, u32[]{:S(2)}, u32[]{:S(2)}) collective-permute-start(f32[2,8,16,128]{3,2,1,0:T(8,128)S(1)} %pad_maximum_fusion.refs_0_), channel_id=1, source_target_pairs={{0,32},{32,64},{64,96},{96,0},{128,160},{160,192},{192,224},{224,1... | collective-permute-start | bytes 393224 | tf_op jit(solution)/shard_map/ppermute | solution.py:432
  78.0 20.4 %all-to-all-start.3 = ((f32[32,2,8,128]{3,2,1,0:T(8,128)}), f32[32,2,8,128]{3,2,1,0:T(8,128)S(1)}, u32[]{:S(2)}, u32[]{:S(2)}) async-start(f32[32,2,8,128]{3,2,1,0:T(8,128)} %bitcast.9), calls=%async_computation.3 | async-start | bytes 524288 | tf_op jit(solution)/shard_map/all_to_all | solution.py:423
  85.0 3.7 %collective-permute-start.4 = (f32[8,16,128]{2,1,0:T(8,128)S(1)}, f32[8,16,128]{2,1,0:T(8,128)S(1)}, u32[]{:S(2)}, u32[]{:S(2)}) collective-permute-start(f32[8,16,128]{2,1,0:T(8,128)S(1)} %get-tuple-element.38), channel_id=1, source_target_pairs={{0,128},{32,160},{64,192},{96,224},{128,0},{160,32},{192,64},{224,... | collective-permute-start | bytes 196616 | tf_op jit(solution)/shard_map/ppermute | solution.py:427
  88.7 14.1 %collective-permute-start.7 = (f32[2,8,16,128]{3,2,1,0:T(8,128)S(1)}, f32[2,8,16,128]{3,2,1,0:T(8,128)S(1)}, u32[]{:S(2)}, u32[]{:S(2)}) collective-permute-start(f32[2,8,16,128]{3,2,1,0:T(8,128)S(1)} %pad_maximum_fusion.1.refs_4_), channel_id=1, source_target_pairs={{0,64},{32,96},{64,0},{96,32},{128,192},{160,224},{192,128},{224,1... | collective-permute-start | bytes 393224 | tf_op jit(solution)/shard_map/ppermute | solution.py:432
  91.1 11.8 %collective-permute-start.6 = (f32[2,8,16,128]{3,2,1,0:T(8,128)S(1)}, f32[2,8,16,128]{3,2,1,0:T(8,128)S(1)}, u32[]{:S(2)}, u32[]{:S(2)}) collective-permute-start(f32[2,8,16,128]{3,2,1,0:T(8,128)S(1)} %pad_maximum_fusion.1.refs_4_), channel_id=1, source_target_pairs={{0,96},{32,0},{64,32},{96,64},{128,224},{160,128},{192,160},{224,1... | collective-permute-start | bytes 393224 | tf_op jit(solution)/shard_map/ppermute | solution.py:432
  92.0 10.9 %collective-permute-start.5 = (f32[2,8,16,128]{3,2,1,0:T(8,128)S(1)}, f32[2,8,16,128]{3,2,1,0:T(8,128)S(1)}, u32[]{:S(2)}, u32[]{:S(2)}) collective-permute-start(f32[2,8,16,128]{3,2,1,0:T(8,128)S(1)} %pad_maximum_fusion.1.refs_4_), channel_id=1, source_target_pairs={{0,32},{32,64},{64,96},{96,0},{128,160},{160,192},{192,224},{224,1... | collective-permute-start | bytes 393224 | tf_op jit(solution)/shard_map/ppermute | solution.py:432

commit v3 on v2

--- a/solution.py
+++ b/solution.py
@@ -127,7 +127,15 @@
     return jnp.concatenate(blocks, 1)
 
 
-Y_TILES = 8
+def steps(first, last):
+    def run(step_of):
+        for step in range(first, last):
+            step_of(step)
+
+    return run
+
+
+Y_TILES = 16
 
 
 def y_analysis_store(chunk, first_tile, tiles, y_in, scratch):
@@ -136,7 +144,7 @@
         scratch[pl.ds(first_tile + j, 2 * K, stride=TP), :] = out[:, j * 128 : (j + 1) * 128]
 
 
-def t_analysis(scratch, t_table, out_ref, x, group=4):
+def t_analysis(scratch, t_table, out_ref, x, group=16):
     low = low_lanes((K, 128))
     for first in range(0, K, group):
         data = lanes([scratch[(first + j) * 2 * TP : (first + j + 1) * 2 * TP, :] for j in range(group)])
@@ -148,7 +156,7 @@
             out_ref[2 * (first + j) + 1, x] = both[8:]
 
 
-def t_synthesis(w_ref, t_table, scratch, x, group=4):
+def t_synthesis(w_ref, t_table, scratch, x, group=16):
     low = low_lanes((K, 128))
     zero = jnp.zeros((K, 128), F32)
     for first in range(0, K, group):
@@ -178,7 +186,7 @@
 def y_synthesis(scratch, first_tile, tiles, y_out):
     data = lanes(
         [
-            scratch[pl.ds(pl.multiple_of((first_tile + j) * 2 * K, 2 * K), 2 * K), :]
+            scratch[pl.ds((first_tile + j) * 2 * K, 2 * K), :]
             for j in range(tiles)
         ]
     )
@@ -194,7 +202,7 @@
 
 
 def lane_slice(step, tiles):
-    return pl.ds(pl.multiple_of(step * tiles * 128, tiles * 128), tiles * 128)
+    return pl.ds(step * tiles * 128, tiles * 128)
 
 
 HALF = N * C // 2
@@ -226,7 +234,7 @@
     for i in range(2 * CX):
         copies[1 + i].wait()
 
-        @pl.loop(i % 2 * TP // 2 // Y_TILES, (i % 2 + 1) * TP // 2 // Y_TILES)
+        @steps(i % 2 * TP // 2 // Y_TILES, (i % 2 + 1) * TP // 2 // Y_TILES)
         def _(step):
             y_analysis_store(
                 field[i // 2, :, lane_slice(step, Y_TILES)], step * Y_TILES, Y_TILES, y_in, scratch
@@ -268,7 +276,7 @@
         copies[2 * x].wait()
         copies[2 * x + 1].wait()
 
-        @pl.loop(0, TP // Y_TILES)
+        @steps(0, TP // Y_TILES)
         def _(step):
             at = lane_slice(step, Y_TILES)
             spec = y_synthesis(syn, step * Y_TILES, Y_TILES, y_out)
@@ -293,7 +301,7 @@
         t_synthesis(w_ref, t_out, syn, x)
         copies[x].wait()
 
-        @pl.loop(0, TP // Y_TILES)
+        @steps(0, TP // Y_TILES)
         def _(step):
             at = lane_slice(step, Y_TILES)
             spec = y_synthesis(syn, step * Y_TILES, Y_TILES, y_out)
@@ -352,29 +360,32 @@
     return jnp.where(low_lanes((K, 128)), total[:K], total[K:])
 
 
-def spectral_kernel(adjoint, in_ref, w_ref, tables_ref, hat_ref, out_ref):
+def mix_kernel(in_ref, w_ref, tables_ref, hat_ref, out_ref):
     spectra = x_analysis(in_ref, table(tables_ref, "x_in"))
     mixed = []
     for m in range(M):
         hat_ref[m] = spectra[m]
-        weights = w_ref[m]
-        mixed.append(mix_adjoint(spectra[m], weights) if adjoint else mix(spectra[m], weights))
+        mixed.append(mix(spectra[m], w_ref[m]))
     x_synthesis(mixed, table(tables_ref, "x_out"), out_ref)
 
 
-G_MODES = 2
+def adjoint_kernel(in_ref, u_ref, w_ref, tables_ref, hats_ref, out_ref):
+    spectra = x_analysis(in_ref, table(tables_ref, "x_in"))
+    mixed = []
+    for m in range(M):
+        hats_ref[0, m] = u_ref[m]
+        hats_ref[1, m] = spectra[m]
+        mixed.append(mix_adjoint(spectra[m], w_ref[m]))
+    x_synthesis(mixed, table(tables_ref, "x_out"), out_ref)
 
 
 def grads_kernel(*refs):
-    u_refs, g_refs, out_ref = refs[:Y_RING], refs[Y_RING : 2 * Y_RING], refs[-1]
+    hats, (grads_out, grads, sems) = refs[:DP], refs[DP:]
     own = lax.broadcasted_iota(jnp.int32, (C, 2 * DP * K), 1) % K // 2
     odd = lax.broadcasted_iota(jnp.int32, (2 * DP * K, 1), 0) % 2 == 1
-    for j in range(G_MODES):
-        m = pl.program_id(0) * G_MODES + j
-        u, g = (
-            jnp.concatenate([ref[b, m] for ref in part for b in range(DP // Y_RING)], 0)
-            for part in (u_refs, g_refs)
-        )
+    copies = [pltpu.make_async_copy(grads.at[m], grads_out.at[m], sems.at[m]) for m in range(M)]
+    for m in range(M):
+        u, g = (jnp.concatenate([hat[i, m] for hat in hats], 0) for i in range(2))
         u_t = u.T.astype(BF)
         left = lanes([u_t[:C], u_t[C:]])
         right = jnp.concatenate([g, -turned(g)], 0)
@@ -382,7 +393,10 @@
         tall = jnp.concatenate([jnp.where(own == q, left, jnp.zeros_like(left)) for q in range(K // 2)], 0)
         out = dot(tall, right)
         for kx in range(K):
-            out_ref[j, kx] = out[kx // 2 * C : (kx // 2 + 1) * C, kx % 2 * 128 : (kx % 2 + 1) * 128]
+            grads[m, kx] = out[kx // 2 * C : (kx // 2 + 1) * C, kx % 2 * 128 : (kx % 2 + 1) * 128]
+        copies[m].start()
+    for copy in copies:
+        copy.wait()
 
 
 LIMIT = 32
@@ -416,42 +430,30 @@
 
 SPECTRA = shape((SLABS, CX, M, 128))
 ROWS = pltpu.VMEM((TP * 2 * K, 128), F32)
-Y_RING = 4
 
 
 def exchange(data):
     return lax.all_to_all(data, "slab", 0, 0, tiled=True)
 
 
-def x_pair(data):
-    return jnp.stack([data, lax.ppermute(data, "dp", [(i, (i + Y_RING) % DP) for i in range(DP)])], 0)
-
-
-def y_ring(data):
-    def moved(by):
-        return lax.ppermute(
-            data, "dp", [(i, i // Y_RING * Y_RING + (i + by) % Y_RING) for i in range(DP)]
-        )
-
-    return [data, moved(1), moved(3), moved(2)]
+Y_RING = 4
+
+
+def x_partner(data):
+    return lax.ppermute(data, "dp", [(i, (i + Y_RING) % DP) for i in range(DP)])
+
+
+def y_neighbours(data):
+    return [
+        lax.ppermute(data, "dp", [(i, i // Y_RING * Y_RING + (i + by) % Y_RING) for i in range(DP)])
+        for by in (1, 3, 2)
+    ]
 
 
 def body(field, cotangent, mode_weights, w_local, bias):
     grid_shape = (CX, N, N * C)
     on_grid = pltpu.VMEM(grid_shape, BF)
     values, cot = field.reshape(grid_shape), cotangent.reshape(grid_shape)
-
-    def spectral(adjoint, data):
-        return call(
-            lambda *refs: spectral_kernel(adjoint, *refs),
-            "adjoint" if adjoint else "mix",
-            (shape((M, K, 128)), shape((N * M, 128))),
-            [IN_VMEM] * 2,
-            [],
-            data.reshape(N * M, 128),
-            *in_vmem(weights, tables),
-            specs=[IN_VMEM] * 3,
-        )
 
     first, weights, tables, wide_map, wide_bias = call(
         analyse_kernel,
@@ -470,9 +472,17 @@
         ),
         specs=[IN_HBM] * 5,
     )
-    u_hat, mixed = spectral(False, exchange(first))
-    u_pair = x_pair(u_hat)
-    arrived, u_pair = lax.optimization_barrier((exchange(mixed.reshape(SPECTRA.shape)), u_pair))
+    u_hat, mixed = call(
+        mix_kernel,
+        "mix",
+        (shape((M, K, 128)), shape((N * M, 128))),
+        [IN_VMEM] * 2,
+        [],
+        exchange(first).reshape(N * M, 128),
+        *in_vmem(weights, tables),
+        specs=[IN_VMEM] * 3,
+    )
+    arrived = exchange(mixed.reshape(SPECTRA.shape))
     gz, second = call(
         middle_kernel,
         "middle",
@@ -484,10 +494,19 @@
         *in_vmem(wide_map, wide_bias, tables),
         specs=[IN_VMEM] + [IN_HBM] * 2 + [IN_VMEM] * 3,
     )
-    u_all = y_ring(u_pair)
-    arrived, u_all = lax.optimization_barrier((exchange(second), u_all))
-    g_hat, back = spectral(True, arrived)
-    g_all = y_ring(x_pair(g_hat))
+    hats, back = call(
+        adjoint_kernel,
+        "adjoint",
+        (shape((2, M, K, 128)), shape((N * M, 128))),
+        [IN_VMEM] * 2,
+        [],
+        exchange(second).reshape(N * M, 128),
+        u_hat,
+        *in_vmem(weights, tables),
+        specs=[IN_VMEM] * 4,
+    )
+    partner = x_partner(hats)
+    others = [*y_neighbours(hats), partner, *y_neighbours(partner)]
     grad_field = call(
         final_kernel,
         "final",
@@ -499,16 +518,17 @@
         *in_vmem(wide_map, tables),
         specs=[IN_VMEM, IN_HBM] + [IN_VMEM] * 2,
     )
-    grad_field, g_all = lax.optimization_barrier((grad_field, g_all))
-    grad_modes = pl.pallas_call(
+    grad_field, *others = lax.optimization_barrier((grad_field, *others))
+    grad_modes = call(
         grads_kernel,
-        name="weight_grads",
-        grid=(M // G_MODES,),
-        out_shape=shape((M, K, C, 2 * C)),
-        in_specs=[IN_VMEM] * 2 * Y_RING,
-        out_specs=pl.BlockSpec((G_MODES, K, C, 2 * C), lambda m: (m, 0, 0, 0)),
-        compiler_params=pltpu.CompilerParams(vmem_limit_bytes=LIMIT * 2**20),
-    )(*u_all, *g_all)
+        "weight_grads",
+        pltpu.HBM((M, K, C, 2 * C), F32),
+        IN_HBM,
+        [pltpu.VMEM((M, K, C, 2 * C), F32), pltpu.SemaphoreType.DMA((M,))],
+        hats,
+        *others,
+        specs=[IN_VMEM] * DP,
+    )
     return grad_field.reshape(field.shape), grad_modes
 
 

time: 106 us -> 97.7 us (0.922)
  blocking collectives: 25.8 us -> 61.1 us
  waiting for transfers between devices: 31.3 us -> 4.37 us
  starting transfers between devices: 26.1 us -> 14.2 us
  Pallas kernels: 22 us -> 16.8 us
    all_to_all x1 -> x3, blocking collectives: 25.8 us -> 61.1 us  [exchange(): return lax.all_to_all(data, 'slab', 0, 0, tiled=True)]
    all_to_all x3 -> x1, waiting for transfers between devices: 19.8 us -> 3.45 us  [exchange(): return lax.all_to_all(data, 'slab', 0, 0, tiled=True)]
    all_to_all x3 -> x1, starting transfers between devices: 17 us -> 5.01 us  [exchange(): return lax.all_to_all(data, 'slab', 0, 0, tiled=True)]
    ppermute x8 -> x7, waiting for transfers between devices: 11.5 us -> 0.92 us  [the longest x1 0.9 us: x_partner(): return lax.ppermute(data, 'dp', [(i, (i + Y_RING) % DP) for i in range(DP)])]
    pallas_call x1 -> x0, Pallas kernels: 3.18 us -> none  [body(): pl.pallas_call(grads_kernel, name='weight_grads', grid=(M // G_MODES,), o...]
    pallas_call x5 -> x6, Pallas kernels: 18.9 us -> 16.8 us  [call(): pl.pallas_call(kernel, name=name, out_shape=out_shapes, in_specs=specs, o...]
    ppermute x8 -> x7, starting transfers between devices: 9.13 us -> 9.18 us  [the longest x6 8.77 us: y_neighbours(): lax.ppermute(data, 'dp', [(i, i // Y_RING * Y_RING + (i + by) % Y_RING) f...]
  transfers between devices with their start and end apart: 11 -> 8, of which waited for: 7 -> 2; matrix products, arithmetic and copies ran while one was open for 0% -> 0% of each run, Pallas kernels for 4% -> 3%
where the time goes in v3:
time: 97.7 us; the launch traced here: 97.4 us
  blocking collectives  61.1 us (63%)
  Pallas kernels  16.8 us (17%)
  starting transfers between devices  14.2 us (15%)
  waiting for transfers between devices  4.37 us (4%)
    all_to_all x3, blocking collectives, exchange(): return lax.all_to_all(data, 'slab', 0, 0, tiled=True)  61.1 us
    pallas_call x6, Pallas kernels, call(): pl.pallas_call(kernel, name=name, out_shape=out_shapes, in_specs=specs, o...  16.8 us
    ppermute x6, starting transfers between devices, y_neighbours(): lax.ppermute(data, 'dp', [(i, i // Y_RING * Y_RING + (i + by) % Y_RING) f...  8.77 us
    all_to_all x1, starting transfers between devices, exchange(): return lax.all_to_all(data, 'slab', 0, 0, tiled=True)  5.01 us
    all_to_all x1, waiting for transfers between devices, exchange(): return lax.all_to_all(data, 'slab', 0, 0, tiled=True)  3.45 us
  transfers between devices with their start and end apart: 8, of which 2 were waited for; matrix products, arithmetic and copies ran while one was open for 0% of the time, Pallas kernels for 3%

profile of v3, /device:TPU:1, one launch (start us, length us, event | category | flops | bytes accessed | tf_op | source)
XLA Modules:
  0.0 97.4 jit_solution(15364165791795592494)
XLA Ops:
  0.6 2.9 %analyse.1 = (f32[32,2,8,128]{3,2,1,0:T(8,128)S(1)}, bf16[8,1024,128]{2,1,0:T(8,128)(2,1)S(1)}, bf16[320,256]{1,0:T(8,128)(2,1)S(1)}, bf16[128,128]{1,0:T(8,128)(2,1)S(1)}, f32[1,128]{1,0:T(1,128)S(1)}) custom-call(bf16[2,64,4096]{2,1,0:T(8,128)(2,1)} %bitcast.12, bf16[8,1024,128]{2,1,0:T(8,128)(2,1)} %bitcast.14, bf16[320,256]{1,0:T(8,128)(2,1)} %constant.2.clone.tables_in, ...), custom_call_target="tpu_custom_call" | custom-call | tf_op jit(solution)/shard_map/analyse/pallas_call | solution.py:408
  3.6 25.8 %all_to_all.20 = f32[32,2,8,128]{3,2,1,0:T(8,128)S(1)} all-to-all(f32[32,2,8,128]{3,2,1,0:T(8,128)S(1)} %get-tuple-element.21), channel_id=1, replica_groups=mesh['dp'=8,'slab'=32] {'slab'}, dimensions={0} | all-to-all | bytes 524288 | tf_op jit(solution)/shard_map/all_to_all | solution.py:436
  29.4 1.0 %mix.1 = (f32[8,16,128]{2,1,0:T(8,128)S(1)}, f32[512,128]{1,0:T(8,128)S(1)}) custom-call(f32[512,128]{1,0:T(8,128)S(1)} %bitcast.10, bf16[8,1024,128]{2,1,0:T(8,128)(2,1)S(1)} %get-tuple-element.22.w_ref, bf16[320,256]{1,0:T(8,128)(2,1)S(1)} %get-tuple-element.23.tables_ref), custom_call_target="tpu_custom_call" | custom-call | tf_op jit(solution)/shard_map/mix/pallas_call | solution.py:408
  30.4 17.7 %all_to_all.21.w_ref = f32[32,2,8,128]{3,2,1,0:T(8,128)S(1)} all-to-all(f32[32,2,8,128]{3,2,1,0:T(8,128)S(1)} %bitcast.11), channel_id=1, replica_groups=mesh['dp'=8,'slab'=32] {'slab'}, dimensions={0} | all-to-all | bytes 524288 | tf_op jit(solution)/shard_map/all_to_all | solution.py:436
  48.1 5.1 %middle.1 = (bf16[2,64,4096]{2,1,0:T(8,128)(2,1)}, f32[32,2,8,128]{3,2,1,0:T(8,128)S(1)}) custom-call(f32[32,2,8,128]{3,2,1,0:T(8,128)S(1)} %all_to_all.21.w_ref, bf16[2,64,4096]{2,1,0:T(8,128)(2,1)} %bitcast.13, bf16[2,64,4096]{2,1,0:T(8,128)(2,1)} %bitcast.15, bf16[128,128]{1,0:T(8,128)(2,1)S(1)} %get-tuple-element.25.map_ref, ...), custom_call_target="tpu_custom_call" | custom-call | tf_op jit(solution)/shard_map/middle/pallas_call | solution.py:408
  53.2 17.7 %all_to_all.22 = f32[32,2,8,128]{3,2,1,0:T(8,128)S(1)} all-to-all(f32[32,2,8,128]{3,2,1,0:T(8,128)S(1)} %get-tuple-element.27), channel_id=1, replica_groups=mesh['dp'=8,'slab'=32] {'slab'}, dimensions={0} | all-to-all | bytes 524288 | tf_op jit(solution)/shard_map/all_to_all | solution.py:436
  70.9 2.0 %adjoint.1 = (f32[2,8,16,128]{3,2,1,0:T(8,128)S(1)}, f32[512,128]{1,0:T(8,128)}) custom-call(f32[512,128]{1,0:T(8,128)S(1)} %bitcast.9, f32[8,16,128]{2,1,0:T(8,128)S(1)} %get-tuple-element.28.u_ref, bf16[8,1024,128]{2,1,0:T(8,128)(2,1)S(1)} %get-tuple-element.22.w_ref, bf16[320,256]{1,0:T(8,128)(2,1)S(1)} %get-tuple-element.23.tables_ref), custom_call_target="tpu_custom_call" | custom-call | tf_op jit(solution)/shard_map/adjoint/pallas_call | solution.py:408
  72.9 5.0 %all-to-all-start.3 = ((f32[32,2,8,128]{3,2,1,0:T(8,128)}), f32[32,2,8,128]{3,2,1,0:T(8,128)S(1)}, u32[]{:S(2)}, u32[]{:S(2)}) async-start(f32[32,2,8,128]{3,2,1,0:T(8,128)} %bitcast.7), calls=%async_computation.3 | async-start | bytes 524288 | tf_op jit(solution)/shard_map/all_to_all | solution.py:436
  77.9 0.4 collective-permute-start.3
  78.3 2.9 %collective-permute-start.2 = (f32[2,8,16,128]{3,2,1,0:T(8,128)S(1)}, f32[2,8,16,128]{3,2,1,0:T(8,128)S(1)}, u32[]{:S(2)}, u32[]{:S(2)}) collective-permute-start(f32[2,8,16,128]{3,2,1,0:T(8,128)S(1)} %get-tuple-element.31.refs_0_), channel_id=1, source_target_pairs={{0,64},{32,96},{64,0},{96,32},{128,192},{160,224},{192,128},{224,1... | collective-permute-start | bytes 393224 | tf_op jit(solution)/shard_map/ppermute | solution.py:448
  81.2 0.8 collective-permute-start.1
  82.0 0.7 collective-permute-start
  82.7 0.9 collective-permute-done.3.refs_4_
  83.6 2.9 %collective-permute-start.6 = (f32[2,8,16,128]{3,2,1,0:T(8,128)S(1)}, f32[2,8,16,128]{3,2,1,0:T(8,128)S(1)}, u32[]{:S(2)}, u32[]{:S(2)}) collective-permute-start(f32[2,8,16,128]{3,2,1,0:T(8,128)S(1)} %collective-permute-done.3.refs_4_), channel_id=1, source_target_pairs={{0,64},{32,96},{64,0},{96,32},{128,192},{160,224},{192,128},{224,1... | collective-permute-start | bytes 393224 | tf_op jit(solution)/shard_map/ppermute | solution.py:448
  86.5 0.8 collective-permute-start.5
  87.3 0.0 collective-permute-done.2.refs_3_
  87.3 0.7 collective-permute-start.4
  88.0 3.5 %all-to-all-done.3.w_ref = f32[32,2,8,128]{3,2,1,0:T(8,128)S(1)} async-done(((f32[32,2,8,128]{3,2,1,0:T(8,128)}), f32[32,2,8,128]{3,2,1,0:T(8,128)S(1)}, u32[]{:S(2)}, u32[]{:S(2)}) %all-to-all-start.3) | async-done | bytes 262176 | tf_op jit(solution)/shard_map/all_to_all | solution.py:436
  91.5 3.3 %final.1 = bf16[2,64,4096]{2,1,0:T(8,128)(2,1)} custom-call(f32[32,2,8,128]{3,2,1,0:T(8,128)S(1)} %all-to-all-done.3.w_ref, bf16[2,64,4096]{2,1,0:T(8,128)(2,1)} %get-tuple-element.30.gz_in, bf16[128,128]{1,0:T(8,128)(2,1)S(1)} %get-tuple-element.25.map_ref, bf16[320,256]{1,0:T(8,128)(2,1)S(1)} %get-tuple-element.23.tables_ref), custom_call_target="tpu_custom_call" | custom-call | tf_op jit(solution)/shard_map/final/pallas_call | solution.py:408
  94.7 0.0 collective-permute-done.1.refs_2_
  94.7 0.0 collective-permute-done.refs_1_
  94.7 0.0 collective-permute-done.5.refs_6_
  94.8 0.0 collective-permute-done.4.refs_5_
  94.8 2.5 %weight_grads.1 = f32[8,16,64,128]{3,2,1,0:T(8,128)} custom-call(f32[2,8,16,128]{3,2,1,0:T(8,128)S(1)} %get-tuple-element.31.refs_0_, f32[2,8,16,128]{3,2,1,0:T(8,128)S(1)} %collective-permute-done.refs_1_, f32[2,8,16,128]{3,2,1,0:T(8,128)S(1)} %collective-permute-done.1.refs_2_, f32[2,8,16,128]{3,2,1,0:T(8,128)S(1)} %collective-permute-done.2.refs_3_, ...), custom_call_target="tpu_custom_call" | custom-call | tf_op jit(solution)/shard_map/weight_grads/pallas_call | solution.py:408
  (1 shorter events, 0.0 us)
Async XLA Ops:
  72.9 18.6 %all-to-all-start.3 = ((f32[32,2,8,128]{3,2,1,0:T(8,128)}), f32[32,2,8,128]{3,2,1,0:T(8,128)S(1)}, u32[]{:S(2)}, u32[]{:S(2)}) async-start(f32[32,2,8,128]{3,2,1,0:T(8,128)} %bitcast.7), calls=%async_computation.3 | async-start | bytes 524288 | tf_op jit(solution)/shard_map/all_to_all | solution.py:436
  77.9 5.7 %collective-permute-start.3 = (f32[2,8,16,128]{3,2,1,0:T(8,128)S(1)}, f32[2,8,16,128]{3,2,1,0:T(8,128)S(1)}, u32[]{:S(2)}, u32[]{:S(2)}) collective-permute-start(f32[2,8,16,128]{3,2,1,0:T(8,128)S(1)} %get-tuple-element.31.refs_0_), channel_id=1, source_target_pairs={{0,128},{32,160},{64,192},{96,224},{128,0},{160,32},{192,64},{224,... | collective-permute-start | bytes 393224 | tf_op jit(solution)/shard_map/ppermute | solution.py:443
  78.3 9.0 %collective-permute-start.2 = (f32[2,8,16,128]{3,2,1,0:T(8,128)S(1)}, f32[2,8,16,128]{3,2,1,0:T(8,128)S(1)}, u32[]{:S(2)}, u32[]{:S(2)}) collective-permute-start(f32[2,8,16,128]{3,2,1,0:T(8,128)S(1)} %get-tuple-element.31.refs_0_), channel_id=1, source_target_pairs={{0,64},{32,96},{64,0},{96,32},{128,192},{160,224},{192,128},{224,1... | collective-permute-start | bytes 393224 | tf_op jit(solution)/shard_map/ppermute | solution.py:448
  81.2 13.5 %collective-permute-start.1 = (f32[2,8,16,128]{3,2,1,0:T(8,128)S(1)}, f32[2,8,16,128]{3,2,1,0:T(8,128)S(1)}, u32[]{:S(2)}, u32[]{:S(2)}) collective-permute-start(f32[2,8,16,128]{3,2,1,0:T(8,128)S(1)} %get-tuple-element.31.refs_0_), channel_id=1, source_target_pairs={{0,96},{32,0},{64,32},{96,64},{128,224},{160,128},{192,160},{224,1... | collective-permute-start | bytes 393224 | tf_op jit(solution)/shard_map/ppermute | solution.py:448
  82.0 12.7 %collective-permute-start = (f32[2,8,16,128]{3,2,1,0:T(8,128)S(1)}, f32[2,8,16,128]{3,2,1,0:T(8,128)S(1)}, u32[]{:S(2)}, u32[]{:S(2)}) collective-permute-start(f32[2,8,16,128]{3,2,1,0:T(8,128)S(1)} %get-tuple-element.31.refs_0_), channel_id=1, source_target_pairs={{0,32},{32,64},{64,96},{96,0},{128,160},{160,192},{192,224},{224,1... | collective-permute-start | bytes 393224 | tf_op jit(solution)/shard_map/ppermute | solution.py:448
  83.6 11.1 %collective-permute-start.6 = (f32[2,8,16,128]{3,2,1,0:T(8,128)S(1)}, f32[2,8,16,128]{3,2,1,0:T(8,128)S(1)}, u32[]{:S(2)}, u32[]{:S(2)}) collective-permute-start(f32[2,8,16,128]{3,2,1,0:T(8,128)S(1)} %collective-permute-done.3.refs_4_), channel_id=1, source_target_pairs={{0,64},{32,96},{64,0},{96,32},{128,192},{160,224},{192,128},{224,1... | collective-permute-start | bytes 393224 | tf_op jit(solution)/shard_map/ppermute | solution.py:448
  86.5 8.2 %collective-permute-start.5 = (f32[2,8,16,128]{3,2,1,0:T(8,128)S(1)}, f32[2,8,16,128]{3,2,1,0:T(8,128)S(1)}, u32[]{:S(2)}, u32[]{:S(2)}) collective-permute-start(f32[2,8,16,128]{3,2,1,0:T(8,128)S(1)} %collective-permute-done.3.refs_4_), channel_id=1, source_target_pairs={{0,96},{32,0},{64,32},{96,64},{128,224},{160,128},{192,160},{224,1... | collective-permute-start | bytes 393224 | tf_op jit(solution)/shard_map/ppermute | solution.py:448
  87.3 7.5 %collective-permute-start.4 = (f32[2,8,16,128]{3,2,1,0:T(8,128)S(1)}, f32[2,8,16,128]{3,2,1,0:T(8,128)S(1)}, u32[]{:S(2)}, u32[]{:S(2)}) collective-permute-start(f32[2,8,16,128]{3,2,1,0:T(8,128)S(1)} %collective-permute-done.3.refs_4_), channel_id=1, source_target_pairs={{0,32},{32,64},{64,96},{96,0},{128,160},{160,192},{192,224},{224,1... | collective-permute-start | bytes 393224 | tf_op jit(solution)/shard_map/ppermute | solution.py:448

commit v4 on v3

--- a/solution.py
+++ b/solution.py
@@ -127,27 +127,18 @@
     return jnp.concatenate(blocks, 1)
 
 
-def steps(first, last):
-    def run(step_of):
-        for step in range(first, last):
-            step_of(step)
-
-    return run
-
-
-Y_TILES = 16
+Y_TILES = 32
 
 
 def y_analysis_store(chunk, first_tile, tiles, y_in, scratch):
     out = dot(y_in, jnp.concatenate([chunk, chunk], 0))
-    for j in range(tiles):
-        scratch[pl.ds(first_tile + j, 2 * K, stride=TP), :] = out[:, j * 128 : (j + 1) * 128]
+    scratch[:, first_tile : first_tile + tiles, :] = out.reshape(2 * K, tiles, 128)
 
 
 def t_analysis(scratch, t_table, out_ref, x, group=16):
     low = low_lanes((K, 128))
     for first in range(0, K, group):
-        data = lanes([scratch[(first + j) * 2 * TP : (first + j + 1) * 2 * TP, :] for j in range(group)])
+        data = lanes([scratch[2 * (first + j) : 2 * (first + j + 1)].reshape(2 * TP, 128) for j in range(group)])
         res = dot(t_table, stack2(data))
         for j in range(group):
             re0, re1, im0, im1 = (res[q * K : (q + 1) * K, j * 128 : (j + 1) * 128] for q in range(4))
@@ -176,17 +167,16 @@
                 )
             )
         res = dot(t_table, stack3(lanes(blocks)))
-        for j in range(group):
-            for cs in range(2):
-                scratch[pl.ds(cs * K + first + j, TP, stride=2 * K), :] = res[
-                    cs * TP : (cs + 1) * TP, j * 128 : (j + 1) * 128
-                ]
+        for cs in range(2):
+            scratch[:, cs * K + first : cs * K + first + group, :] = res[cs * TP : (cs + 1) * TP].reshape(
+                TP, group, 128
+            )
 
 
 def y_synthesis(scratch, first_tile, tiles, y_out):
     data = lanes(
         [
-            scratch[pl.ds((first_tile + j) * 2 * K, 2 * K), :]
+            scratch[first_tile + j]
             for j in range(tiles)
         ]
     )
@@ -231,17 +221,11 @@
     )
     copies[0].wait()
     y_in, t_in = table(tables_ref, "y_in"), table(tables_ref, "t_in")
-    for i in range(2 * CX):
-        copies[1 + i].wait()
-
-        @steps(i % 2 * TP // 2 // Y_TILES, (i % 2 + 1) * TP // 2 // Y_TILES)
-        def _(step):
-            y_analysis_store(
-                field[i // 2, :, lane_slice(step, Y_TILES)], step * Y_TILES, Y_TILES, y_in, scratch
-            )
-
-        if i % 2 == 1:
-            t_analysis(scratch, t_in, out_ref, i // 2)
+    for x in range(CX):
+        copies[1 + 2 * x].wait()
+        copies[2 + 2 * x].wait()
+        y_analysis_store(field[x], 0, TP, y_in, scratch)
+        t_analysis(scratch, t_in, out_ref, x)
     for copy in copies[1 + 2 * CX :]:
         copy.wait()
     wide_map = jnp.concatenate([small_map[...]] * 2, 1)
@@ -255,8 +239,8 @@
 def gelu_slope(z):
     square = z * z
     tanh_value = jnp.tanh(z * (SQRT_TWO_PI + SQRT_TWO_PI * 0.044715 * square))
-    inner_slope = z * (0.5 * SQRT_TWO_PI + 1.5 * SQRT_TWO_PI * 0.044715 * square)
-    return 0.5 + 0.5 * tanh_value + inner_slope * (1.0 - tanh_value * tanh_value)
+    half_rise = z * (0.5 * SQRT_TWO_PI + 1.5 * SQRT_TWO_PI * 0.044715 * square)
+    return (1.0 + tanh_value) * (0.5 + half_rise * (1.0 - tanh_value))
 
 
 def middle_kernel(
@@ -272,21 +256,22 @@
     backs = [pltpu.make_async_copy(gz.at[x], gz_out.at[x], sems.at[len(copies) + x]) for x in range(CX)]
     y_in, y_out, t_in, t_out = (table(tables_ref, name) for name in ("y_in", "y_out", "t_in", "t_out"))
     for x in range(CX):
-        t_synthesis(w_ref, t_out, syn, x)
+        t_synthesis(w_ref, t_out, syn.at[x], x)
+    for x in range(CX):
         copies[2 * x].wait()
         copies[2 * x + 1].wait()
 
-        @steps(0, TP // Y_TILES)
-        def _(step):
+        for step in range(TP // Y_TILES):
             at = lane_slice(step, Y_TILES)
-            spec = y_synthesis(syn, step * Y_TILES, Y_TILES, y_out)
+            spec = y_synthesis(syn.at[x], step * Y_TILES, Y_TILES, y_out)
             z = spec + channel_map(field[x, :, at], map_ref[...], Y_TILES) + lanes([bias_ref[...]] * Y_TILES)
             out = (cot[x, :, at].astype(F32) * gelu_slope(z)).astype(BF)
             gz[x, :, at] = out
-            y_analysis_store(out, step * Y_TILES, Y_TILES, y_in, ana)
+            y_analysis_store(out, step * Y_TILES, Y_TILES, y_in, ana.at[x])
 
         backs[x].start()
-        t_analysis(ana, t_in, out_ref, x)
+    for x in range(CX):
+        t_analysis(ana.at[x], t_in, out_ref, x)
     for back in backs:
         back.wait()
 
@@ -298,13 +283,13 @@
     ]
     y_out, t_out = table(tables_ref, "y_out"), table(tables_ref, "t_out")
     for x in range(CX):
-        t_synthesis(w_ref, t_out, syn, x)
+        t_synthesis(w_ref, t_out, syn.at[x], x)
+    for x in range(CX):
         copies[x].wait()
 
-        @steps(0, TP // Y_TILES)
-        def _(step):
+        for step in range(TP // Y_TILES):
             at = lane_slice(step, Y_TILES)
-            spec = y_synthesis(syn, step * Y_TILES, Y_TILES, y_out)
+            spec = y_synthesis(syn.at[x], step * Y_TILES, Y_TILES, y_out)
             grad[x, :, at] = (spec + channel_map(gz[x, :, at], map_ref[...], Y_TILES, 1)).astype(BF)
 
         backs[x].start()
@@ -316,7 +301,7 @@
 
 
 def x_analysis(in_ref, x_in):
-    data = lanes([in_ref[pl.ds(m, N, stride=M), :] for m in range(M)])
+    data = in_ref[...].reshape(N, M * 128)
     res = dot(x_in, stack3(data))
     out = []
     for m in range(M):
@@ -329,8 +314,7 @@
 def x_synthesis(blocks, x_out, out_ref):
     data = lanes([jnp.concatenate([v, turned(v)], 0) for v in blocks])
     res = dot(x_out, stack3(data))
-    for m in range(M):
-        out_ref[pl.ds(m, N, stride=M), :] = res[:, m * 128 : (m + 1) * 128]
+    out_ref[...] = res.reshape(N, M, 128)
 
 
 def mix(u, weights):
@@ -429,7 +413,8 @@
 
 
 SPECTRA = shape((SLABS, CX, M, 128))
-ROWS = pltpu.VMEM((TP * 2 * K, 128), F32)
+BOTH_ROWS = pltpu.VMEM((CX, 2 * K, TP, 128), F32)
+ROWS = pltpu.VMEM((2 * K, TP, 128), F32)
 
 
 def exchange(data):
@@ -446,7 +431,7 @@
 def y_neighbours(data):
     return [
         lax.ppermute(data, "dp", [(i, i // Y_RING * Y_RING + (i + by) % Y_RING) for i in range(DP)])
-        for by in (1, 3, 2)
+        for by in (2, 3, 1)
     ]
 
 
@@ -475,10 +460,10 @@
     u_hat, mixed = call(
         mix_kernel,
         "mix",
-        (shape((M, K, 128)), shape((N * M, 128))),
+        (shape((M, K, 128)), shape((N, M, 128))),
         [IN_VMEM] * 2,
         [],
-        exchange(first).reshape(N * M, 128),
+        exchange(first).reshape(N, M, 128),
         *in_vmem(weights, tables),
         specs=[IN_VMEM] * 3,
     )
@@ -488,7 +473,7 @@
         "middle",
         (pltpu.HBM(grid_shape, BF), SPECTRA),
         [IN_HBM, IN_VMEM],
-        [on_grid, on_grid, on_grid, ROWS, ROWS, pltpu.SemaphoreType.DMA((6,))],
+        [on_grid, on_grid, on_grid, BOTH_ROWS, BOTH_ROWS, pltpu.SemaphoreType.DMA((6,))],
         arrived,
         *in_hbm(values, cot),
         *in_vmem(wide_map, wide_bias, tables),
@@ -497,22 +482,23 @@
     hats, back = call(
         adjoint_kernel,
         "adjoint",
-        (shape((2, M, K, 128)), shape((N * M, 128))),
+        (shape((2, M, K, 128)), shape((N, M, 128))),
         [IN_VMEM] * 2,
         [],
-        exchange(second).reshape(N * M, 128),
+        exchange(second).reshape(N, M, 128),
         u_hat,
         *in_vmem(weights, tables),
         specs=[IN_VMEM] * 4,
     )
     partner = x_partner(hats)
-    others = [*y_neighbours(hats), partner, *y_neighbours(partner)]
+    opposite, back_one, next_one = y_neighbours(hats)
+    others = [opposite, back_one, next_one, partner, x_partner(opposite), *y_neighbours(partner)[1:]]
     grad_field = call(
         final_kernel,
         "final",
         pltpu.HBM(grid_shape, BF),
         IN_HBM,
-        [on_grid, on_grid, ROWS, pltpu.SemaphoreType.DMA((4,))],
+        [on_grid, on_grid, BOTH_ROWS, pltpu.SemaphoreType.DMA((4,))],
         exchange(back.reshape(SPECTRA.shape)),
         *in_hbm(gz),
         *in_vmem(wide_map, tables),

time: 97.7 us -> 96 us (0.983)
  Pallas kernels: 16.8 us -> 15.3 us
    pallas_call x6, Pallas kernels: 16.8 us -> 15.3 us  [call(): pl.pallas_call(kernel, name=name, out_shape=out_shapes, in_specs=specs, o...]
    ppermute x1 -> x2, starting transfers between devices: 0.41 us -> 1.54 us  [x_partner(): return lax.ppermute(data, 'dp', [(i, (i + Y_RING) % DP) for i in range(DP)])]
    ppermute x6 -> x5, starting transfers between devices: 8.77 us -> 8.27 us  [y_neighbours(): lax.ppermute(data, 'dp', [(i, i // Y_RING * Y_RING + (i + by) % Y_RING) f...]
  transfers between devices with their start and end apart: 8 -> 8, of which waited for: 2 -> 1; matrix products, arithmetic and copies ran while one was open for 0% -> 0% of each run, Pallas kernels for 3% -> 3%
where the time goes in v4:
time: 96 us; the launch traced here: 95.7 us
  blocking collectives  61.1 us (64%)
  Pallas kernels  15.3 us (16%)
  starting transfers between devices  14.8 us (15%)
  waiting for transfers between devices  3.73 us (4%)
    all_to_all x3, blocking collectives, exchange(): return lax.all_to_all(data, 'slab', 0, 0, tiled=True)  61.1 us
    pallas_call x6, Pallas kernels, call(): pl.pallas_call(kernel, name=name, out_shape=out_shapes, in_specs=specs, o...  15.3 us
    ppermute x5, starting transfers between devices, y_neighbours(): lax.ppermute(data, 'dp', [(i, i // Y_RING * Y_RING + (i + by) % Y_RING) f...  8.27 us
    all_to_all x1, starting transfers between devices, exchange(): return lax.all_to_all(data, 'slab', 0, 0, tiled=True)  5.01 us
    all_to_all x1, waiting for transfers between devices, exchange(): return lax.all_to_all(data, 'slab', 0, 0, tiled=True)  3.71 us
  transfers between devices with their start and end apart: 8, of which 1 were waited for; matrix products, arithmetic and copies ran while one was open for 0% of the time, Pallas kernels for 3%

profile of v4, /device:TPU:1, one launch (start us, length us, event | category | flops | bytes accessed | tf_op | source)
XLA Modules:
  0.0 95.7 jit_solution(17981451929050314895)
XLA Ops:
  0.6 2.4 %analyse.1 = (f32[32,2,8,128]{3,2,1,0:T(8,128)S(1)}, bf16[8,1024,128]{2,1,0:T(8,128)(2,1)S(1)}, bf16[320,256]{1,0:T(8,128)(2,1)S(1)}, bf16[128,128]{1,0:T(8,128)(2,1)S(1)}, f32[1,128]{1,0:T(1,128)S(1)}) custom-call(bf16[2,64,4096]{2,1,0:T(8,128)(2,1)} %bitcast.12, bf16[8,1024,128]{2,1,0:T(8,128)(2,1)} %bitcast.14, bf16[320,256]{1,0:T(8,128)(2,1)} %constant.2.clone.tables_in, ...), custom_call_target="tpu_custom_call" | custom-call | tf_op jit(solution)/shard_map/analyse/pallas_call | solution.py:392
  3.1 25.8 %all_to_all.20 = f32[32,2,8,128]{3,2,1,0:T(8,128)S(1)} all-to-all(f32[32,2,8,128]{3,2,1,0:T(8,128)S(1)} %get-tuple-element.21), channel_id=1, replica_groups=mesh['dp'=8,'slab'=32] {'slab'}, dimensions={0} | all-to-all | bytes 524288 | tf_op jit(solution)/shard_map/all_to_all | solution.py:421
  28.9 1.0 %mix.1 = (f32[8,16,128]{2,1,0:T(8,128)S(1)}, f32[64,8,128]{2,1,0:T(8,128)S(1)}) custom-call(f32[64,8,128]{2,1,0:T(8,128)S(1)} %bitcast.10, bf16[8,1024,128]{2,1,0:T(8,128)(2,1)S(1)} %get-tuple-element.22.w_ref, bf16[320,256]{1,0:T(8,128)(2,1)S(1)} %get-tuple-element.23.tables_ref), custom_call_target="tpu_custom_call" | custom-call | tf_op jit(solution)/shard_map/mix/pallas_call | solution.py:392
  29.9 17.7 %all_to_all.21.w_ref = f32[32,2,8,128]{3,2,1,0:T(8,128)S(1)} all-to-all(f32[32,2,8,128]{3,2,1,0:T(8,128)S(1)} %bitcast.11), channel_id=1, replica_groups=mesh['dp'=8,'slab'=32] {'slab'}, dimensions={0} | all-to-all | bytes 524288 | tf_op jit(solution)/shard_map/all_to_all | solution.py:421
  47.5 4.2 %middle.1 = (bf16[2,64,4096]{2,1,0:T(8,128)(2,1)}, f32[32,2,8,128]{3,2,1,0:T(8,128)S(1)}) custom-call(f32[32,2,8,128]{3,2,1,0:T(8,128)S(1)} %all_to_all.21.w_ref, bf16[2,64,4096]{2,1,0:T(8,128)(2,1)} %bitcast.13, bf16[2,64,4096]{2,1,0:T(8,128)(2,1)} %bitcast.15, bf16[128,128]{1,0:T(8,128)(2,1)S(1)} %get-tuple-element.25.map_ref, ...), custom_call_target="tpu_custom_call" | custom-call | tf_op jit(solution)/shard_map/middle/pallas_call | solution.py:392
  51.8 17.7 %all_to_all.22 = f32[32,2,8,128]{3,2,1,0:T(8,128)S(1)} all-to-all(f32[32,2,8,128]{3,2,1,0:T(8,128)S(1)} %get-tuple-element.27), channel_id=1, replica_groups=mesh['dp'=8,'slab'=32] {'slab'}, dimensions={0} | all-to-all | bytes 524288 | tf_op jit(solution)/shard_map/all_to_all | solution.py:421
  69.4 2.0 %adjoint.1 = (f32[2,8,16,128]{3,2,1,0:T(8,128)S(1)}, f32[64,8,128]{2,1,0:T(8,128)}) custom-call(f32[64,8,128]{2,1,0:T(8,128)S(1)} %bitcast.9, f32[8,16,128]{2,1,0:T(8,128)S(1)} %get-tuple-element.28.u_ref, bf16[8,1024,128]{2,1,0:T(8,128)(2,1)S(1)} %get-tuple-element.22.w_ref, bf16[320,256]{1,0:T(8,128)(2,1)S(1)} %get-tuple-element.23.tables_ref), custom_call_target="tpu_custom_call" | custom-call | tf_op jit(solution)/shard_map/adjoint/pallas_call | solution.py:392
  71.5 5.0 %all-to-all-start.3 = ((f32[32,2,8,128]{3,2,1,0:T(8,128)}), f32[32,2,8,128]{3,2,1,0:T(8,128)S(1)}, u32[]{:S(2)}, u32[]{:S(2)}) async-start(f32[32,2,8,128]{3,2,1,0:T(8,128)} %bitcast.7), calls=%async_computation.3 | async-start | bytes 524288 | tf_op jit(solution)/shard_map/all_to_all | solution.py:421
  76.5 0.4 collective-permute-start.3
  76.9 2.9 %collective-permute-start = (f32[2,8,16,128]{3,2,1,0:T(8,128)S(1)}, f32[2,8,16,128]{3,2,1,0:T(8,128)S(1)}, u32[]{:S(2)}, u32[]{:S(2)}) collective-permute-start(f32[2,8,16,128]{3,2,1,0:T(8,128)S(1)} %get-tuple-element.31.refs_0_), channel_id=1, source_target_pairs={{0,64},{32,96},{64,0},{96,32},{128,192},{160,224},{192,128},{224,1... | collective-permute-start | bytes 393224 | tf_op jit(solution)/shard_map/ppermute | solution.py:433
  79.8 0.4 collective-permute-start.2
  80.2 2.3 %collective-permute-start.1 = (f32[2,8,16,128]{3,2,1,0:T(8,128)S(1)}, f32[2,8,16,128]{3,2,1,0:T(8,128)S(1)}, u32[]{:S(2)}, u32[]{:S(2)}) collective-permute-start(f32[2,8,16,128]{3,2,1,0:T(8,128)S(1)} %get-tuple-element.31.refs_0_), channel_id=1, source_target_pairs={{0,96},{32,0},{64,32},{96,64},{128,224},{160,128},{192,160},{224,1... | collective-permute-start | bytes 393224 | tf_op jit(solution)/shard_map/ppermute | solution.py:433
  82.5 0.0 collective-permute-done.3.refs_4_
  82.5 1.0 %collective-permute-start.6 = (f32[2,8,16,128]{3,2,1,0:T(8,128)S(1)}, f32[2,8,16,128]{3,2,1,0:T(8,128)S(1)}, u32[]{:S(2)}, u32[]{:S(2)}) collective-permute-start(f32[2,8,16,128]{3,2,1,0:T(8,128)S(1)} %collective-permute-done.3.refs_4_), channel_id=1, source_target_pairs={{0,32},{32,64},{64,96},{96,0},{128,160},{160,192},{192,224},{224,1... | collective-permute-start | bytes 393224 | tf_op jit(solution)/shard_map/ppermute | solution.py:433
  83.5 1.7 %collective-permute-start.5 = (f32[2,8,16,128]{3,2,1,0:T(8,128)S(1)}, f32[2,8,16,128]{3,2,1,0:T(8,128)S(1)}, u32[]{:S(2)}, u32[]{:S(2)}) collective-permute-start(f32[2,8,16,128]{3,2,1,0:T(8,128)S(1)} %collective-permute-done.3.refs_4_), channel_id=1, source_target_pairs={{0,96},{32,0},{64,32},{96,64},{128,224},{160,128},{192,160},{224,1... | collective-permute-start | bytes 393224 | tf_op jit(solution)/shard_map/ppermute | solution.py:433
  85.2 0.0 collective-permute-done.refs_1_
  85.2 1.1 %collective-permute-start.4 = (f32[2,8,16,128]{3,2,1,0:T(8,128)S(1)}, f32[2,8,16,128]{3,2,1,0:T(8,128)S(1)}, u32[]{:S(2)}, u32[]{:S(2)}) collective-permute-start(f32[2,8,16,128]{3,2,1,0:T(8,128)S(1)} %collective-permute-done.refs_1_), channel_id=1, source_target_pairs={{0,128},{32,160},{64,192},{96,224},{128,0},{160,32},{192,64},{224,... | collective-permute-start | bytes 393224 | tf_op jit(solution)/shard_map/ppermute | solution.py:428
  86.3 3.7 %all-to-all-done.3.w_ref = f32[32,2,8,128]{3,2,1,0:T(8,128)S(1)} async-done(((f32[32,2,8,128]{3,2,1,0:T(8,128)}), f32[32,2,8,128]{3,2,1,0:T(8,128)S(1)}, u32[]{:S(2)}, u32[]{:S(2)}) %all-to-all-start.3) | async-done | bytes 262176 | tf_op jit(solution)/shard_map/all_to_all | solution.py:421
  90.0 3.1 %final.1 = bf16[2,64,4096]{2,1,0:T(8,128)(2,1)} custom-call(f32[32,2,8,128]{3,2,1,0:T(8,128)S(1)} %all-to-all-done.3.w_ref, bf16[2,64,4096]{2,1,0:T(8,128)(2,1)} %get-tuple-element.30.gz_in, bf16[128,128]{1,0:T(8,128)(2,1)S(1)} %get-tuple-element.25.map_ref, bf16[320,256]{1,0:T(8,128)(2,1)S(1)} %get-tuple-element.23.tables_ref), custom_call_target="tpu_custom_call" | custom-call | tf_op jit(solution)/shard_map/final/pallas_call | solution.py:392
  93.1 0.0 collective-permute-done.2.refs_3_
  93.1 0.0 collective-permute-done.1.refs_2_
  93.2 0.0 collective-permute-done.6.refs_7_
  93.2 0.0 collective-permute-done.4.refs_5_
  93.2 2.5 %weight_grads.1 = f32[8,16,64,128]{3,2,1,0:T(8,128)} custom-call(f32[2,8,16,128]{3,2,1,0:T(8,128)S(1)} %get-tuple-element.31.refs_0_, f32[2,8,16,128]{3,2,1,0:T(8,128)S(1)} %collective-permute-done.refs_1_, f32[2,8,16,128]{3,2,1,0:T(8,128)S(1)} %collective-permute-done.1.refs_2_, f32[2,8,16,128]{3,2,1,0:T(8,128)S(1)} %collective-permute-done.2.refs_3_, ...), custom_call_target="tpu_custom_call" | custom-call | tf_op jit(solution)/shard_map/weight_grads/pallas_call | solution.py:392
  (1 shorter events, 0.0 us)
Async XLA Ops:
  71.5 18.6 %all-to-all-start.3 = ((f32[32,2,8,128]{3,2,1,0:T(8,128)}), f32[32,2,8,128]{3,2,1,0:T(8,128)S(1)}, u32[]{:S(2)}, u32[]{:S(2)}) async-start(f32[32,2,8,128]{3,2,1,0:T(8,128)} %bitcast.7), calls=%async_computation.3 | async-start | bytes 524288 | tf_op jit(solution)/shard_map/all_to_all | solution.py:421
  76.5 6.0 %collective-permute-start.3 = (f32[2,8,16,128]{3,2,1,0:T(8,128)S(1)}, f32[2,8,16,128]{3,2,1,0:T(8,128)S(1)}, u32[]{:S(2)}, u32[]{:S(2)}) collective-permute-start(f32[2,8,16,128]{3,2,1,0:T(8,128)S(1)} %get-tuple-element.31.refs_0_), channel_id=1, source_target_pairs={{0,128},{32,160},{64,192},{96,224},{128,0},{160,32},{192,64},{224,... | collective-permute-start | bytes 393224 | tf_op jit(solution)/shard_map/ppermute | solution.py:428
  76.9 8.3 %collective-permute-start = (f32[2,8,16,128]{3,2,1,0:T(8,128)S(1)}, f32[2,8,16,128]{3,2,1,0:T(8,128)S(1)}, u32[]{:S(2)}, u32[]{:S(2)}) collective-permute-start(f32[2,8,16,128]{3,2,1,0:T(8,128)S(1)} %get-tuple-element.31.refs_0_), channel_id=1, source_target_pairs={{0,64},{32,96},{64,0},{96,32},{128,192},{160,224},{192,128},{224,1... | collective-permute-start | bytes 393224 | tf_op jit(solution)/shard_map/ppermute | solution.py:433
  79.8 13.3 %collective-permute-start.2 = (f32[2,8,16,128]{3,2,1,0:T(8,128)S(1)}, f32[2,8,16,128]{3,2,1,0:T(8,128)S(1)}, u32[]{:S(2)}, u32[]{:S(2)}) collective-permute-start(f32[2,8,16,128]{3,2,1,0:T(8,128)S(1)} %get-tuple-element.31.refs_0_), channel_id=1, source_target_pairs={{0,32},{32,64},{64,96},{96,0},{128,160},{160,192},{192,224},{224,1... | collective-permute-start | bytes 393224 | tf_op jit(solution)/shard_map/ppermute | solution.py:433
  80.2 13.0 %collective-permute-start.1 = (f32[2,8,16,128]{3,2,1,0:T(8,128)S(1)}, f32[2,8,16,128]{3,2,1,0:T(8,128)S(1)}, u32[]{:S(2)}, u32[]{:S(2)}) collective-permute-start(f32[2,8,16,128]{3,2,1,0:T(8,128)S(1)} %get-tuple-element.31.refs_0_), channel_id=1, source_target_pairs={{0,96},{32,0},{64,32},{96,64},{128,224},{160,128},{192,160},{224,1... | collective-permute-start | bytes 393224 | tf_op jit(solution)/shard_map/ppermute | solution.py:433
  82.5 10.7 %collective-permute-start.6 = (f32[2,8,16,128]{3,2,1,0:T(8,128)S(1)}, f32[2,8,16,128]{3,2,1,0:T(8,128)S(1)}, u32[]{:S(2)}, u32[]{:S(2)}) collective-permute-start(f32[2,8,16,128]{3,2,1,0:T(8,128)S(1)} %collective-permute-done.3.refs_4_), channel_id=1, source_target_pairs={{0,32},{32,64},{64,96},{96,0},{128,160},{160,192},{192,224},{224,1... | collective-permute-start | bytes 393224 | tf_op jit(solution)/shard_map/ppermute | solution.py:433
  83.5 9.7 %collective-permute-start.5 = (f32[2,8,16,128]{3,2,1,0:T(8,128)S(1)}, f32[2,8,16,128]{3,2,1,0:T(8,128)S(1)}, u32[]{:S(2)}, u32[]{:S(2)}) collective-permute-start(f32[2,8,16,128]{3,2,1,0:T(8,128)S(1)} %collective-permute-done.3.refs_4_), channel_id=1, source_target_pairs={{0,96},{32,0},{64,32},{96,64},{128,224},{160,128},{192,160},{224,1... | collective-permute-start | bytes 393224 | tf_op jit(solution)/shard_map/ppermute | solution.py:433
  85.2 8.0 %collective-permute-start.4 = (f32[2,8,16,128]{3,2,1,0:T(8,128)S(1)}, f32[2,8,16,128]{3,2,1,0:T(8,128)S(1)}, u32[]{:S(2)}, u32[]{:S(2)}) collective-permute-start(f32[2,8,16,128]{3,2,1,0:T(8,128)S(1)} %collective-permute-done.refs_1_), channel_id=1, source_target_pairs={{0,128},{32,160},{64,192},{96,224},{128,0},{160,32},{192,64},{224,... | collective-permute-start | bytes 393224 | tf_op jit(solution)/shard_map/ppermute | solution.py:428

commit v5 on v4

--- a/solution.py
+++ b/solution.py
@@ -244,22 +244,13 @@
 
 
 def middle_kernel(
-    w_ref, field_in, cot_in, map_ref, bias_ref, tables_ref, gz_out, out_ref, field, cot, gz, syn, ana, sems
+    w_ref, field, cot, map_ref, bias_ref, tables_ref, gz_out, out_ref, gz, syn, ana, sems
 ):
-    copies = start_all(
-        sems,
-        (field_in.at[0], field.at[0]),
-        (cot_in.at[0], cot.at[0]),
-        (field_in.at[1], field.at[1]),
-        (cot_in.at[1], cot.at[1]),
-    )
-    backs = [pltpu.make_async_copy(gz.at[x], gz_out.at[x], sems.at[len(copies) + x]) for x in range(CX)]
+    backs = [pltpu.make_async_copy(gz.at[x], gz_out.at[x], sems.at[x]) for x in range(CX)]
     y_in, y_out, t_in, t_out = (table(tables_ref, name) for name in ("y_in", "y_out", "t_in", "t_out"))
     for x in range(CX):
         t_synthesis(w_ref, t_out, syn.at[x], x)
     for x in range(CX):
-        copies[2 * x].wait()
-        copies[2 * x + 1].wait()
 
         for step in range(TP // Y_TILES):
             at = lane_slice(step, Y_TILES)
@@ -276,16 +267,12 @@
         back.wait()
 
 
-def final_kernel(w_ref, gz_in, map_ref, tables_ref, grad_out, gz, grad, syn, sems):
-    copies = start_all(sems, (gz_in.at[0], gz.at[0]), (gz_in.at[1], gz.at[1]))
-    backs = [
-        pltpu.make_async_copy(grad.at[x], grad_out.at[x], sems.at[len(copies) + x]) for x in range(CX)
-    ]
+def final_kernel(w_ref, gz, map_ref, tables_ref, grad_out, grad, syn, sems):
+    backs = [pltpu.make_async_copy(grad.at[x], grad_out.at[x], sems.at[x]) for x in range(CX)]
     y_out, t_out = table(tables_ref, "y_out"), table(tables_ref, "t_out")
     for x in range(CX):
         t_synthesis(w_ref, t_out, syn.at[x], x)
     for x in range(CX):
-        copies[x].wait()
 
         for step in range(TP // Y_TILES):
             at = lane_slice(step, Y_TILES)
@@ -473,11 +460,10 @@
         "middle",
         (pltpu.HBM(grid_shape, BF), SPECTRA),
         [IN_HBM, IN_VMEM],
-        [on_grid, on_grid, on_grid, BOTH_ROWS, BOTH_ROWS, pltpu.SemaphoreType.DMA((6,))],
+        [on_grid, BOTH_ROWS, BOTH_ROWS, pltpu.SemaphoreType.DMA((2,))],
         arrived,
-        *in_hbm(values, cot),
-        *in_vmem(wide_map, wide_bias, tables),
-        specs=[IN_VMEM] + [IN_HBM] * 2 + [IN_VMEM] * 3,
+        *in_vmem(values, cot, wide_map, wide_bias, tables),
+        specs=[IN_VMEM] * 6,
     )
     hats, back = call(
         adjoint_kernel,
@@ -498,11 +484,10 @@
         "final",
         pltpu.HBM(grid_shape, BF),
         IN_HBM,
-        [on_grid, on_grid, BOTH_ROWS, pltpu.SemaphoreType.DMA((4,))],
+        [on_grid, BOTH_ROWS, pltpu.SemaphoreType.DMA((2,))],
         exchange(back.reshape(SPECTRA.shape)),
-        *in_hbm(gz),
-        *in_vmem(wide_map, tables),
-        specs=[IN_VMEM, IN_HBM] + [IN_VMEM] * 2,
+        *in_vmem(gz, wide_map, tables),
+        specs=[IN_VMEM] * 4,
     )
     grad_field, *others = lax.optimization_barrier((grad_field, *others))
     grad_modes = call(

time: 96 us -> 93.8 us (0.977)
  Pallas kernels: 15.3 us -> 12.8 us
    pallas_call x6, Pallas kernels: 15.3 us -> 12.8 us  [call(): pl.pallas_call(kernel, name=name, out_shape=out_shapes, in_specs=specs, o...]
  transfers between devices with their start and end apart: 8 -> 8, of which waited for: 1 -> 1; matrix products, arithmetic and copies ran while one was open for 0% -> 0% of each run, Pallas kernels for 3% -> 2%
where the time goes in v5:
time: 93.8 us; the launch traced here: 93.5 us
  blocking collectives  61.4 us (65%)
  starting transfers between devices  14.8 us (16%)
  Pallas kernels  12.8 us (14%)
  waiting for transfers between devices  3.72 us (4%)
    all_to_all x3, blocking collectives, exchange(): return lax.all_to_all(data, 'slab', 0, 0, tiled=True)  61.4 us
    pallas_call x6, Pallas kernels, call(): pl.pallas_call(kernel, name=name, out_shape=out_shapes, in_specs=specs, o...  12.8 us
    ppermute x5, starting transfers between devices, y_neighbours(): lax.ppermute(data, 'dp', [(i, i // Y_RING * Y_RING + (i + by) % Y_RING) f...  8.26 us
    all_to_all x1, starting transfers between devices, exchange(): return lax.all_to_all(data, 'slab', 0, 0, tiled=True)  5.01 us
    all_to_all x1, waiting for transfers between devices, exchange(): return lax.all_to_all(data, 'slab', 0, 0, tiled=True)  3.71 us
  transfers between devices with their start and end apart: 8, of which 1 were waited for; matrix products, arithmetic and copies ran while one was open for 0% of the time, Pallas kernels for 2%

profile of v5, /device:TPU:1, one launch (start us, length us, event | category | flops | bytes accessed | tf_op | source)
XLA Modules:
  0.0 93.5 jit_solution(6364982170895490099)
XLA Ops:
  0.6 2.4 %analyse.1 = (f32[32,2,8,128]{3,2,1,0:T(8,128)S(1)}, bf16[8,1024,128]{2,1,0:T(8,128)(2,1)S(1)}, bf16[320,256]{1,0:T(8,128)(2,1)S(1)}, bf16[128,128]{1,0:T(8,128)(2,1)S(1)}, f32[1,128]{1,0:T(1,128)S(1)}) custom-call(bf16[2,64,4096]{2,1,0:T(8,128)(2,1)} %bitcast.9, bf16[8,1024,128]{2,1,0:T(8,128)(2,1)} %bitcast.15, bf16[320,256]{1,0:T(8,128)(2,1)} %constant.2.clone.tables_in, ...), custom_call_target="tpu_custom_call" | custom-call | tf_op jit(solution)/shard_map/analyse/pallas_call | solution.py:379
  3.1 0.0 copy-start
  3.1 0.0 copy-start.1
  3.1 25.9 %all_to_all.20 = f32[32,2,8,128]{3,2,1,0:T(8,128)S(1)} all-to-all(f32[32,2,8,128]{3,2,1,0:T(8,128)S(1)} %get-tuple-element.21), channel_id=1, replica_groups=mesh['dp'=8,'slab'=32] {'slab'}, dimensions={0} | all-to-all | bytes 524288 | tf_op jit(solution)/shard_map/all_to_all | solution.py:408
  29.0 1.0 %mix.1 = (f32[8,16,128]{2,1,0:T(8,128)S(1)}, f32[64,8,128]{2,1,0:T(8,128)S(1)}) custom-call(f32[64,8,128]{2,1,0:T(8,128)S(1)} %bitcast.12, bf16[8,1024,128]{2,1,0:T(8,128)(2,1)S(1)} %get-tuple-element.22.w_ref, bf16[320,256]{1,0:T(8,128)(2,1)S(1)} %get-tuple-element.23.tables_ref), custom_call_target="tpu_custom_call" | custom-call | tf_op jit(solution)/shard_map/mix/pallas_call | solution.py:379
  30.0 17.7 %all_to_all.21.w_ref = f32[32,2,8,128]{3,2,1,0:T(8,128)S(1)} all-to-all(f32[32,2,8,128]{3,2,1,0:T(8,128)S(1)} %bitcast.14), channel_id=1, replica_groups=mesh['dp'=8,'slab'=32] {'slab'}, dimensions={0} | all-to-all | bytes 524288 | tf_op jit(solution)/shard_map/all_to_all | solution.py:408
  47.7 2.9 %middle.1 = (bf16[2,64,4096]{2,1,0:T(8,128)(2,1)}, f32[32,2,8,128]{3,2,1,0:T(8,128)S(1)}) custom-call(f32[32,2,8,128]{3,2,1,0:T(8,128)S(1)} %all_to_all.21.w_ref, bf16[2,64,4096]{2,1,0:T(8,128)(2,1)S(1)} %bitcast.10, bf16[2,64,4096]{2,1,0:T(8,128)(2,1)S(1)} %bitcast.13, bf16[128,128]{1,0:T(8,128)(2,1)S(1)} %get-tuple-element.25.map_ref, ...), custom_call_target="tpu_custom_call" | custom-call | tf_op jit(solution)/shard_map/middle/pallas_call | solution.py:379
  50.6 0.0 copy-start.2
  50.6 17.8 %all_to_all.22 = f32[32,2,8,128]{3,2,1,0:T(8,128)S(1)} all-to-all(f32[32,2,8,128]{3,2,1,0:T(8,128)S(1)} %get-tuple-element.27), channel_id=1, replica_groups=mesh['dp'=8,'slab'=32] {'slab'}, dimensions={0} | all-to-all | bytes 524288 | tf_op jit(solution)/shard_map/all_to_all | solution.py:408
  68.4 2.0 %adjoint.1 = (f32[2,8,16,128]{3,2,1,0:T(8,128)S(1)}, f32[64,8,128]{2,1,0:T(8,128)}) custom-call(f32[64,8,128]{2,1,0:T(8,128)S(1)} %bitcast.11, f32[8,16,128]{2,1,0:T(8,128)S(1)} %get-tuple-element.28.u_ref, bf16[8,1024,128]{2,1,0:T(8,128)(2,1)S(1)} %get-tuple-element.22.w_ref, bf16[320,256]{1,0:T(8,128)(2,1)S(1)} %get-tuple-element.23.tables_ref), custom_call_target="tpu_custom_call" | custom-call | tf_op jit(solution)/shard_map/adjoint/pallas_call | solution.py:379
  70.4 5.0 %all-to-all-start.3 = ((f32[32,2,8,128]{3,2,1,0:T(8,128)}), f32[32,2,8,128]{3,2,1,0:T(8,128)S(1)}, u32[]{:S(2)}, u32[]{:S(2)}) async-start(f32[32,2,8,128]{3,2,1,0:T(8,128)} %bitcast.7), calls=%async_computation.3 | async-start | bytes 524288 | tf_op jit(solution)/shard_map/all_to_all | solution.py:408
  75.4 0.4 collective-permute-start.3
  75.8 2.9 %collective-permute-start = (f32[2,8,16,128]{3,2,1,0:T(8,128)S(1)}, f32[2,8,16,128]{3,2,1,0:T(8,128)S(1)}, u32[]{:S(2)}, u32[]{:S(2)}) collective-permute-start(f32[2,8,16,128]{3,2,1,0:T(8,128)S(1)} %get-tuple-element.31.refs_0_), channel_id=1, source_target_pairs={{0,64},{32,96},{64,0},{96,32},{128,192},{160,224},{192,128},{224,1... | collective-permute-start | bytes 393224 | tf_op jit(solution)/shard_map/ppermute | solution.py:420
  78.7 0.4 collective-permute-start.2
  79.1 2.3 %collective-permute-start.1 = (f32[2,8,16,128]{3,2,1,0:T(8,128)S(1)}, f32[2,8,16,128]{3,2,1,0:T(8,128)S(1)}, u32[]{:S(2)}, u32[]{:S(2)}) collective-permute-start(f32[2,8,16,128]{3,2,1,0:T(8,128)S(1)} %get-tuple-element.31.refs_0_), channel_id=1, source_target_pairs={{0,96},{32,0},{64,32},{96,64},{128,224},{160,128},{192,160},{224,1... | collective-permute-start | bytes 393224 | tf_op jit(solution)/shard_map/ppermute | solution.py:420
  81.4 0.0 collective-permute-done.3.refs_4_
  81.4 1.0 %collective-permute-start.6 = (f32[2,8,16,128]{3,2,1,0:T(8,128)S(1)}, f32[2,8,16,128]{3,2,1,0:T(8,128)S(1)}, u32[]{:S(2)}, u32[]{:S(2)}) collective-permute-start(f32[2,8,16,128]{3,2,1,0:T(8,128)S(1)} %collective-permute-done.3.refs_4_), channel_id=1, source_target_pairs={{0,32},{32,64},{64,96},{96,0},{128,160},{160,192},{192,224},{224,1... | collective-permute-start | bytes 393224 | tf_op jit(solution)/shard_map/ppermute | solution.py:420
  82.4 1.7 %collective-permute-start.5 = (f32[2,8,16,128]{3,2,1,0:T(8,128)S(1)}, f32[2,8,16,128]{3,2,1,0:T(8,128)S(1)}, u32[]{:S(2)}, u32[]{:S(2)}) collective-permute-start(f32[2,8,16,128]{3,2,1,0:T(8,128)S(1)} %collective-permute-done.3.refs_4_), channel_id=1, source_target_pairs={{0,96},{32,0},{64,32},{96,64},{128,224},{160,128},{192,160},{224,1... | collective-permute-start | bytes 393224 | tf_op jit(solution)/shard_map/ppermute | solution.py:420
  84.1 1.2 %collective-permute-start.4 = (f32[2,8,16,128]{3,2,1,0:T(8,128)S(1)}, f32[2,8,16,128]{3,2,1,0:T(8,128)S(1)}, u32[]{:S(2)}, u32[]{:S(2)}) collective-permute-start(f32[2,8,16,128]{3,2,1,0:T(8,128)S(1)} %collective-permute-done.refs_1_), channel_id=1, source_target_pairs={{0,128},{32,160},{64,192},{96,224},{128,0},{160,32},{192,64},{224,... | collective-permute-start | bytes 393224 | tf_op jit(solution)/shard_map/ppermute | solution.py:415
  85.3 3.7 %all-to-all-done.3.w_ref = f32[32,2,8,128]{3,2,1,0:T(8,128)S(1)} async-done(((f32[32,2,8,128]{3,2,1,0:T(8,128)}), f32[32,2,8,128]{3,2,1,0:T(8,128)S(1)}, u32[]{:S(2)}, u32[]{:S(2)}) %all-to-all-start.3) | async-done | bytes 262176 | tf_op jit(solution)/shard_map/all_to_all | solution.py:408
  89.0 1.9 %final.1 = bf16[2,64,4096]{2,1,0:T(8,128)(2,1)} custom-call(f32[32,2,8,128]{3,2,1,0:T(8,128)S(1)} %all-to-all-done.3.w_ref, bf16[2,64,4096]{2,1,0:T(8,128)(2,1)S(1)} %copy-done.2, bf16[128,128]{1,0:T(8,128)(2,1)S(1)} %get-tuple-element.25.map_ref, bf16[320,256]{1,0:T(8,128)(2,1)S(1)} %get-tuple-element.23.tables_ref), custom_call_target="tpu_custom_call" | custom-call | tf_op jit(solution)/shard_map/final/pallas_call | solution.py:379
  90.9 0.0 collective-permute-done.1.refs_2_
  90.9 0.0 collective-permute-done.6.refs_7_
  91.0 2.5 %weight_grads.1 = f32[8,16,64,128]{3,2,1,0:T(8,128)} custom-call(f32[2,8,16,128]{3,2,1,0:T(8,128)S(1)} %get-tuple-element.31.refs_0_, f32[2,8,16,128]{3,2,1,0:T(8,128)S(1)} %collective-permute-done.refs_1_, f32[2,8,16,128]{3,2,1,0:T(8,128)S(1)} %collective-permute-done.1.refs_2_, f32[2,8,16,128]{3,2,1,0:T(8,128)S(1)} %collective-permute-done.2.refs_3_, ...), custom_call_target="tpu_custom_call" | custom-call | tf_op jit(solution)/shard_map/weight_grads/pallas_call | solution.py:379
  (7 shorter events, 0.0 us)
Async XLA Ops:
  3.1 44.6 %copy-start = (bf16[1,2,64,4096]{3,2,1,0:T(8,128)(2,1)S(1)}, bf16[1,2,64,4096]{3,2,1,0:T(8,128)(2,1)}, u32[]{:S(2)}) copy-start(bf16[1,2,64,4096]{3,2,1,0:T(8,128)(2,1)} %param.6) | copy-start | bytes 3145732
  3.1 44.6 %copy-start.1 = (bf16[1,2,64,4096]{3,2,1,0:T(8,128)(2,1)S(1)}, bf16[1,2,64,4096]{3,2,1,0:T(8,128)(2,1)}, u32[]{:S(2)}) copy-start(bf16[1,2,64,4096]{3,2,1,0:T(8,128)(2,1)} %param.7) | copy-start | bytes 3145732
  50.6 38.4 %copy-start.2 = (bf16[2,64,4096]{2,1,0:T(8,128)(2,1)S(1)}, bf16[2,64,4096]{2,1,0:T(8,128)(2,1)}, u32[]{:S(2)}) copy-start(bf16[2,64,4096]{2,1,0:T(8,128)(2,1)} %get-tuple-element.30.gz) | copy-start | bytes 3145732
  70.4 18.6 %all-to-all-start.3 = ((f32[32,2,8,128]{3,2,1,0:T(8,128)}), f32[32,2,8,128]{3,2,1,0:T(8,128)S(1)}, u32[]{:S(2)}, u32[]{:S(2)}) async-start(f32[32,2,8,128]{3,2,1,0:T(8,128)} %bitcast.7), calls=%async_computation.3 | async-start | bytes 524288 | tf_op jit(solution)/shard_map/all_to_all | solution.py:408
  75.4 6.0 %collective-permute-start.3 = (f32[2,8,16,128]{3,2,1,0:T(8,128)S(1)}, f32[2,8,16,128]{3,2,1,0:T(8,128)S(1)}, u32[]{:S(2)}, u32[]{:S(2)}) collective-permute-start(f32[2,8,16,128]{3,2,1,0:T(8,128)S(1)} %get-tuple-element.31.refs_0_), channel_id=1, source_target_pairs={{0,128},{32,160},{64,192},{96,224},{128,0},{160,32},{192,64},{224,... | collective-permute-start | bytes 393224 | tf_op jit(solution)/shard_map/ppermute | solution.py:415
  75.8 8.3 %collective-permute-start = (f32[2,8,16,128]{3,2,1,0:T(8,128)S(1)}, f32[2,8,16,128]{3,2,1,0:T(8,128)S(1)}, u32[]{:S(2)}, u32[]{:S(2)}) collective-permute-start(f32[2,8,16,128]{3,2,1,0:T(8,128)S(1)} %get-tuple-element.31.refs_0_), channel_id=1, source_target_pairs={{0,64},{32,96},{64,0},{96,32},{128,192},{160,224},{192,128},{224,1... | collective-permute-start | bytes 393224 | tf_op jit(solution)/shard_map/ppermute | solution.py:420
  78.7 12.2 %collective-permute-start.2 = (f32[2,8,16,128]{3,2,1,0:T(8,128)S(1)}, f32[2,8,16,128]{3,2,1,0:T(8,128)S(1)}, u32[]{:S(2)}, u32[]{:S(2)}) collective-permute-start(f32[2,8,16,128]{3,2,1,0:T(8,128)S(1)} %get-tuple-element.31.refs_0_), channel_id=1, source_target_pairs={{0,32},{32,64},{64,96},{96,0},{128,160},{160,192},{192,224},{224,1... | collective-permute-start | bytes 393224 | tf_op jit(solution)/shard_map/ppermute | solution.py:420
  79.1 11.8 %collective-permute-start.1 = (f32[2,8,16,128]{3,2,1,0:T(8,128)S(1)}, f32[2,8,16,128]{3,2,1,0:T(8,128)S(1)}, u32[]{:S(2)}, u32[]{:S(2)}) collective-permute-start(f32[2,8,16,128]{3,2,1,0:T(8,128)S(1)} %get-tuple-element.31.refs_0_), channel_id=1, source_target_pairs={{0,96},{32,0},{64,32},{96,64},{128,224},{160,128},{192,160},{224,1... | collective-permute-start | bytes 393224 | tf_op jit(solution)/shard_map/ppermute | solution.py:420
  81.4 9.5 %collective-permute-start.6 = (f32[2,8,16,128]{3,2,1,0:T(8,128)S(1)}, f32[2,8,16,128]{3,2,1,0:T(8,128)S(1)}, u32[]{:S(2)}, u32[]{:S(2)}) collective-permute-start(f32[2,8,16,128]{3,2,1,0:T(8,128)S(1)} %collective-permute-done.3.refs_4_), channel_id=1, source_target_pairs={{0,32},{32,64},{64,96},{96,0},{128,160},{160,192},{192,224},{224,1... | collective-permute-start | bytes 393224 | tf_op jit(solution)/shard_map/ppermute | solution.py:420
  82.4 8.5 %collective-permute-start.5 = (f32[2,8,16,128]{3,2,1,0:T(8,128)S(1)}, f32[2,8,16,128]{3,2,1,0:T(8,128)S(1)}, u32[]{:S(2)}, u32[]{:S(2)}) collective-permute-start(f32[2,8,16,128]{3,2,1,0:T(8,128)S(1)} %collective-permute-done.3.refs_4_), channel_id=1, source_target_pairs={{0,96},{32,0},{64,32},{96,64},{128,224},{160,128},{192,160},{224,1... | collective-permute-start | bytes 393224 | tf_op jit(solution)/shard_map/ppermute | solution.py:420
  84.1 6.9 %collective-permute-start.4 = (f32[2,8,16,128]{3,2,1,0:T(8,128)S(1)}, f32[2,8,16,128]{3,2,1,0:T(8,128)S(1)}, u32[]{:S(2)}, u32[]{:S(2)}) collective-permute-start(f32[2,8,16,128]{3,2,1,0:T(8,128)S(1)} %collective-permute-done.refs_1_), channel_id=1, source_target_pairs={{0,128},{32,160},{64,192},{96,224},{128,0},{160,32},{192,64},{224,... | collective-permute-start | bytes 393224 | tf_op jit(solution)/shard_map/ppermute | solution.py:415

commit v6 on v5

--- a/solution.py
+++ b/solution.py
@@ -224,8 +224,9 @@
     for x in range(CX):
         copies[1 + 2 * x].wait()
         copies[2 + 2 * x].wait()
-        y_analysis_store(field[x], 0, TP, y_in, scratch)
-        t_analysis(scratch, t_in, out_ref, x)
+        y_analysis_store(field[x], 0, TP, y_in, scratch.at[x])
+    for x in range(CX):
+        t_analysis(scratch.at[x], t_in, out_ref, x)
     for copy in copies[1 + 2 * CX :]:
         copy.wait()
     wide_map = jnp.concatenate([small_map[...]] * 2, 1)
@@ -438,7 +439,7 @@
             pltpu.VMEM((1, 2 * C), F32),
         ),
         [IN_VMEM] * 5,
-        [on_grid, ROWS, pltpu.VMEM((C, C), BF), pltpu.VMEM((1, C), F32), pltpu.SemaphoreType.DMA((8,))],
+        [on_grid, BOTH_ROWS, pltpu.VMEM((C, C), BF), pltpu.VMEM((1, C), F32), pltpu.SemaphoreType.DMA((8,))],
         *in_hbm(
             values, mode_weights.reshape(M, K * C, 2 * C), jnp.asarray(PACKED), w_local, bias.reshape(1, C)
         ),

time: 93.8 us -> 93.5 us (level)
  no operation moved by 1% of the time
where the time goes in v6:
time: 93.5 us; the launch traced here: 93.2 us
  blocking collectives  61.4 us (66%)
  starting transfers between devices  14.8 us (16%)
  Pallas kernels  12.5 us (13%)
  waiting for transfers between devices  3.72 us (4%)
    all_to_all x3, blocking collectives, exchange(): return lax.all_to_all(data, 'slab', 0, 0, tiled=True)  61.4 us
    pallas_call x6, Pallas kernels, call(): pl.pallas_call(kernel, name=name, out_shape=out_shapes, in_specs=specs, o...  12.5 us
    ppermute x5, starting transfers between devices, y_neighbours(): lax.ppermute(data, 'dp', [(i, i // Y_RING * Y_RING + (i + by) % Y_RING) f...  8.27 us
    all_to_all x1, starting transfers between devices, exchange(): return lax.all_to_all(data, 'slab', 0, 0, tiled=True)  5.01 us
    all_to_all x1, waiting for transfers between devices, exchange(): return lax.all_to_all(data, 'slab', 0, 0, tiled=True)  3.71 us
  transfers between devices with their start and end apart: 8, of which 1 were waited for; matrix products, arithmetic and copies ran while one was open for 0% of the time, Pallas kernels for 2%

profile of v6, /device:TPU:1, one launch (start us, length us, event | category | flops | bytes accessed | tf_op | source)
XLA Modules:
  0.0 93.2 jit_solution(7243983714585375239)
XLA Ops:
  0.6 2.2 %analyse.1 = (f32[32,2,8,128]{3,2,1,0:T(8,128)S(1)}, bf16[8,1024,128]{2,1,0:T(8,128)(2,1)S(1)}, bf16[320,256]{1,0:T(8,128)(2,1)S(1)}, bf16[128,128]{1,0:T(8,128)(2,1)S(1)}, f32[1,128]{1,0:T(1,128)S(1)}) custom-call(bf16[2,64,4096]{2,1,0:T(8,128)(2,1)} %bitcast.9, bf16[8,1024,128]{2,1,0:T(8,128)(2,1)} %bitcast.15, bf16[320,256]{1,0:T(8,128)(2,1)} %constant.2.clone.tables_in, ...), custom_call_target="tpu_custom_call" | custom-call | tf_op jit(solution)/shard_map/analyse/pallas_call | solution.py:380
  2.8 0.0 copy-start
  2.8 0.0 copy-start.1
  2.8 25.9 %all_to_all.20 = f32[32,2,8,128]{3,2,1,0:T(8,128)S(1)} all-to-all(f32[32,2,8,128]{3,2,1,0:T(8,128)S(1)} %get-tuple-element.21), channel_id=1, replica_groups=mesh['dp'=8,'slab'=32] {'slab'}, dimensions={0} | all-to-all | bytes 524288 | tf_op jit(solution)/shard_map/all_to_all | solution.py:409
  28.8 1.0 %mix.1 = (f32[8,16,128]{2,1,0:T(8,128)S(1)}, f32[64,8,128]{2,1,0:T(8,128)S(1)}) custom-call(f32[64,8,128]{2,1,0:T(8,128)S(1)} %bitcast.12, bf16[8,1024,128]{2,1,0:T(8,128)(2,1)S(1)} %get-tuple-element.22.w_ref, bf16[320,256]{1,0:T(8,128)(2,1)S(1)} %get-tuple-element.23.tables_ref), custom_call_target="tpu_custom_call" | custom-call | tf_op jit(solution)/shard_map/mix/pallas_call | solution.py:380
  29.8 17.7 %all_to_all.21.w_ref = f32[32,2,8,128]{3,2,1,0:T(8,128)S(1)} all-to-all(f32[32,2,8,128]{3,2,1,0:T(8,128)S(1)} %bitcast.14), channel_id=1, replica_groups=mesh['dp'=8,'slab'=32] {'slab'}, dimensions={0} | all-to-all | bytes 524288 | tf_op jit(solution)/shard_map/all_to_all | solution.py:409
  47.5 2.9 %middle.1 = (bf16[2,64,4096]{2,1,0:T(8,128)(2,1)}, f32[32,2,8,128]{3,2,1,0:T(8,128)S(1)}) custom-call(f32[32,2,8,128]{3,2,1,0:T(8,128)S(1)} %all_to_all.21.w_ref, bf16[2,64,4096]{2,1,0:T(8,128)(2,1)S(1)} %bitcast.10, bf16[2,64,4096]{2,1,0:T(8,128)(2,1)S(1)} %bitcast.13, bf16[128,128]{1,0:T(8,128)(2,1)S(1)} %get-tuple-element.25.map_ref, ...), custom_call_target="tpu_custom_call" | custom-call | tf_op jit(solution)/shard_map/middle/pallas_call | solution.py:380
  50.4 0.0 copy-start.2
  50.4 17.8 %all_to_all.22 = f32[32,2,8,128]{3,2,1,0:T(8,128)S(1)} all-to-all(f32[32,2,8,128]{3,2,1,0:T(8,128)S(1)} %get-tuple-element.27), channel_id=1, replica_groups=mesh['dp'=8,'slab'=32] {'slab'}, dimensions={0} | all-to-all | bytes 524288 | tf_op jit(solution)/shard_map/all_to_all | solution.py:409
  68.2 2.0 %adjoint.1 = (f32[2,8,16,128]{3,2,1,0:T(8,128)S(1)}, f32[64,8,128]{2,1,0:T(8,128)}) custom-call(f32[64,8,128]{2,1,0:T(8,128)S(1)} %bitcast.11, f32[8,16,128]{2,1,0:T(8,128)S(1)} %get-tuple-element.28.u_ref, bf16[8,1024,128]{2,1,0:T(8,128)(2,1)S(1)} %get-tuple-element.22.w_ref, bf16[320,256]{1,0:T(8,128)(2,1)S(1)} %get-tuple-element.23.tables_ref), custom_call_target="tpu_custom_call" | custom-call | tf_op jit(solution)/shard_map/adjoint/pallas_call | solution.py:380
  70.2 5.0 %all-to-all-start.3 = ((f32[32,2,8,128]{3,2,1,0:T(8,128)}), f32[32,2,8,128]{3,2,1,0:T(8,128)S(1)}, u32[]{:S(2)}, u32[]{:S(2)}) async-start(f32[32,2,8,128]{3,2,1,0:T(8,128)} %bitcast.7), calls=%async_computation.3 | async-start | bytes 524288 | tf_op jit(solution)/shard_map/all_to_all | solution.py:409
  75.2 0.4 collective-permute-start.3
  75.6 2.9 %collective-permute-start = (f32[2,8,16,128]{3,2,1,0:T(8,128)S(1)}, f32[2,8,16,128]{3,2,1,0:T(8,128)S(1)}, u32[]{:S(2)}, u32[]{:S(2)}) collective-permute-start(f32[2,8,16,128]{3,2,1,0:T(8,128)S(1)} %get-tuple-element.31.refs_0_), channel_id=1, source_target_pairs={{0,64},{32,96},{64,0},{96,32},{128,192},{160,224},{192,128},{224,1... | collective-permute-start | bytes 393224 | tf_op jit(solution)/shard_map/ppermute | solution.py:421
  78.5 0.4 collective-permute-start.2
  78.9 2.3 %collective-permute-start.1 = (f32[2,8,16,128]{3,2,1,0:T(8,128)S(1)}, f32[2,8,16,128]{3,2,1,0:T(8,128)S(1)}, u32[]{:S(2)}, u32[]{:S(2)}) collective-permute-start(f32[2,8,16,128]{3,2,1,0:T(8,128)S(1)} %get-tuple-element.31.refs_0_), channel_id=1, source_target_pairs={{0,96},{32,0},{64,32},{96,64},{128,224},{160,128},{192,160},{224,1... | collective-permute-start | bytes 393224 | tf_op jit(solution)/shard_map/ppermute | solution.py:421
  81.2 0.0 collective-permute-done.3.refs_4_
  81.2 1.0 %collective-permute-start.6 = (f32[2,8,16,128]{3,2,1,0:T(8,128)S(1)}, f32[2,8,16,128]{3,2,1,0:T(8,128)S(1)}, u32[]{:S(2)}, u32[]{:S(2)}) collective-permute-start(f32[2,8,16,128]{3,2,1,0:T(8,128)S(1)} %collective-permute-done.3.refs_4_), channel_id=1, source_target_pairs={{0,32},{32,64},{64,96},{96,0},{128,160},{160,192},{192,224},{224,1... | collective-permute-start | bytes 393224 | tf_op jit(solution)/shard_map/ppermute | solution.py:421
  82.2 1.7 %collective-permute-start.5 = (f32[2,8,16,128]{3,2,1,0:T(8,128)S(1)}, f32[2,8,16,128]{3,2,1,0:T(8,128)S(1)}, u32[]{:S(2)}, u32[]{:S(2)}) collective-permute-start(f32[2,8,16,128]{3,2,1,0:T(8,128)S(1)} %collective-permute-done.3.refs_4_), channel_id=1, source_target_pairs={{0,96},{32,0},{64,32},{96,64},{128,224},{160,128},{192,160},{224,1... | collective-permute-start | bytes 393224 | tf_op jit(solution)/shard_map/ppermute | solution.py:421
  83.9 1.2 %collective-permute-start.4 = (f32[2,8,16,128]{3,2,1,0:T(8,128)S(1)}, f32[2,8,16,128]{3,2,1,0:T(8,128)S(1)}, u32[]{:S(2)}, u32[]{:S(2)}) collective-permute-start(f32[2,8,16,128]{3,2,1,0:T(8,128)S(1)} %collective-permute-done.refs_1_), channel_id=1, source_target_pairs={{0,128},{32,160},{64,192},{96,224},{128,0},{160,32},{192,64},{224,... | collective-permute-start | bytes 393224 | tf_op jit(solution)/shard_map/ppermute | solution.py:416
  85.0 3.7 %all-to-all-done.3.w_ref = f32[32,2,8,128]{3,2,1,0:T(8,128)S(1)} async-done(((f32[32,2,8,128]{3,2,1,0:T(8,128)}), f32[32,2,8,128]{3,2,1,0:T(8,128)S(1)}, u32[]{:S(2)}, u32[]{:S(2)}) %all-to-all-start.3) | async-done | bytes 262176 | tf_op jit(solution)/shard_map/all_to_all | solution.py:409
  88.8 1.9 %final.1 = bf16[2,64,4096]{2,1,0:T(8,128)(2,1)} custom-call(f32[32,2,8,128]{3,2,1,0:T(8,128)S(1)} %all-to-all-done.3.w_ref, bf16[2,64,4096]{2,1,0:T(8,128)(2,1)S(1)} %copy-done.2, bf16[128,128]{1,0:T(8,128)(2,1)S(1)} %get-tuple-element.25.map_ref, bf16[320,256]{1,0:T(8,128)(2,1)S(1)} %get-tuple-element.23.tables_ref), custom_call_target="tpu_custom_call" | custom-call | tf_op jit(solution)/shard_map/final/pallas_call | solution.py:380
  90.7 0.0 collective-permute-done.1.refs_2_
  90.7 0.0 collective-permute-done.6.refs_7_
  90.7 2.5 %weight_grads.1 = f32[8,16,64,128]{3,2,1,0:T(8,128)} custom-call(f32[2,8,16,128]{3,2,1,0:T(8,128)S(1)} %get-tuple-element.31.refs_0_, f32[2,8,16,128]{3,2,1,0:T(8,128)S(1)} %collective-permute-done.refs_1_, f32[2,8,16,128]{3,2,1,0:T(8,128)S(1)} %collective-permute-done.1.refs_2_, f32[2,8,16,128]{3,2,1,0:T(8,128)S(1)} %collective-permute-done.2.refs_3_, ...), custom_call_target="tpu_custom_call" | custom-call | tf_op jit(solution)/shard_map/weight_grads/pallas_call | solution.py:380
  (7 shorter events, 0.0 us)
Async XLA Ops:
  2.8 44.6 %copy-start = (bf16[1,2,64,4096]{3,2,1,0:T(8,128)(2,1)S(1)}, bf16[1,2,64,4096]{3,2,1,0:T(8,128)(2,1)}, u32[]{:S(2)}) copy-start(bf16[1,2,64,4096]{3,2,1,0:T(8,128)(2,1)} %param.6) | copy-start | bytes 3145732
  2.8 44.6 %copy-start.1 = (bf16[1,2,64,4096]{3,2,1,0:T(8,128)(2,1)S(1)}, bf16[1,2,64,4096]{3,2,1,0:T(8,128)(2,1)}, u32[]{:S(2)}) copy-start(bf16[1,2,64,4096]{3,2,1,0:T(8,128)(2,1)} %param.7) | copy-start | bytes 3145732
  50.4 38.4 %copy-start.2 = (bf16[2,64,4096]{2,1,0:T(8,128)(2,1)S(1)}, bf16[2,64,4096]{2,1,0:T(8,128)(2,1)}, u32[]{:S(2)}) copy-start(bf16[2,64,4096]{2,1,0:T(8,128)(2,1)} %get-tuple-element.30.gz) | copy-start | bytes 3145732
  70.2 18.6 %all-to-all-start.3 = ((f32[32,2,8,128]{3,2,1,0:T(8,128)}), f32[32,2,8,128]{3,2,1,0:T(8,128)S(1)}, u32[]{:S(2)}, u32[]{:S(2)}) async-start(f32[32,2,8,128]{3,2,1,0:T(8,128)} %bitcast.7), calls=%async_computation.3 | async-start | bytes 524288 | tf_op jit(solution)/shard_map/all_to_all | solution.py:409
  75.2 6.0 %collective-permute-start.3 = (f32[2,8,16,128]{3,2,1,0:T(8,128)S(1)}, f32[2,8,16,128]{3,2,1,0:T(8,128)S(1)}, u32[]{:S(2)}, u32[]{:S(2)}) collective-permute-start(f32[2,8,16,128]{3,2,1,0:T(8,128)S(1)} %get-tuple-element.31.refs_0_), channel_id=1, source_target_pairs={{0,128},{32,160},{64,192},{96,224},{128,0},{160,32},{192,64},{224,... | collective-permute-start | bytes 393224 | tf_op jit(solution)/shard_map/ppermute | solution.py:416
  75.6 8.3 %collective-permute-start = (f32[2,8,16,128]{3,2,1,0:T(8,128)S(1)}, f32[2,8,16,128]{3,2,1,0:T(8,128)S(1)}, u32[]{:S(2)}, u32[]{:S(2)}) collective-permute-start(f32[2,8,16,128]{3,2,1,0:T(8,128)S(1)} %get-tuple-element.31.refs_0_), channel_id=1, source_target_pairs={{0,64},{32,96},{64,0},{96,32},{128,192},{160,224},{192,128},{224,1... | collective-permute-start | bytes 393224 | tf_op jit(solution)/shard_map/ppermute | solution.py:421
  78.5 12.2 %collective-permute-start.2 = (f32[2,8,16,128]{3,2,1,0:T(8,128)S(1)}, f32[2,8,16,128]{3,2,1,0:T(8,128)S(1)}, u32[]{:S(2)}, u32[]{:S(2)}) collective-permute-start(f32[2,8,16,128]{3,2,1,0:T(8,128)S(1)} %get-tuple-element.31.refs_0_), channel_id=1, source_target_pairs={{0,32},{32,64},{64,96},{96,0},{128,160},{160,192},{192,224},{224,1... | collective-permute-start | bytes 393224 | tf_op jit(solution)/shard_map/ppermute | solution.py:421
  78.9 11.8 %collective-permute-start.1 = (f32[2,8,16,128]{3,2,1,0:T(8,128)S(1)}, f32[2,8,16,128]{3,2,1,0:T(8,128)S(1)}, u32[]{:S(2)}, u32[]{:S(2)}) collective-permute-start(f32[2,8,16,128]{3,2,1,0:T(8,128)S(1)} %get-tuple-element.31.refs_0_), channel_id=1, source_target_pairs={{0,96},{32,0},{64,32},{96,64},{128,224},{160,128},{192,160},{224,1... | collective-permute-start | bytes 393224 | tf_op jit(solution)/shard_map/ppermute | solution.py:421
  81.2 9.5 %collective-permute-start.6 = (f32[2,8,16,128]{3,2,1,0:T(8,128)S(1)}, f32[2,8,16,128]{3,2,1,0:T(8,128)S(1)}, u32[]{:S(2)}, u32[]{:S(2)}) collective-permute-start(f32[2,8,16,128]{3,2,1,0:T(8,128)S(1)} %collective-permute-done.3.refs_4_), channel_id=1, source_target_pairs={{0,32},{32,64},{64,96},{96,0},{128,160},{160,192},{192,224},{224,1... | collective-permute-start | bytes 393224 | tf_op jit(solution)/shard_map/ppermute | solution.py:421
  82.2 8.5 %collective-permute-start.5 = (f32[2,8,16,128]{3,2,1,0:T(8,128)S(1)}, f32[2,8,16,128]{3,2,1,0:T(8,128)S(1)}, u32[]{:S(2)}, u32[]{:S(2)}) collective-permute-start(f32[2,8,16,128]{3,2,1,0:T(8,128)S(1)} %collective-permute-done.3.refs_4_), channel_id=1, source_target_pairs={{0,96},{32,0},{64,32},{96,64},{128,224},{160,128},{192,160},{224,1... | collective-permute-start | bytes 393224 | tf_op jit(solution)/shard_map/ppermute | solution.py:421
  83.9 6.8 %collective-permute-start.4 = (f32[2,8,16,128]{3,2,1,0:T(8,128)S(1)}, f32[2,8,16,128]{3,2,1,0:T(8,128)S(1)}, u32[]{:S(2)}, u32[]{:S(2)}) collective-permute-start(f32[2,8,16,128]{3,2,1,0:T(8,128)S(1)} %collective-permute-done.refs_1_), channel_id=1, source_target_pairs={{0,128},{32,160},{64,192},{96,224},{128,0},{160,32},{192,64},{224,... | collective-permute-start | bytes 393224 | tf_op jit(solution)/shard_map/ppermute | solution.py:416

commit v7 on v6

--- a/solution.py
+++ b/solution.py
@@ -281,8 +281,7 @@
             grad[x, :, at] = (spec + channel_map(gz[x, :, at], map_ref[...], Y_TILES, 1)).astype(BF)
 
         backs[x].start()
-    for back in backs:
-        back.wait()
+    return backs
 
 
 M = 8
@@ -367,7 +366,14 @@
         for kx in range(K):
             grads[m, kx] = out[kx // 2 * C : (kx // 2 + 1) * C, kx % 2 * 128 : (kx % 2 + 1) * 128]
         copies[m].start()
-    for copy in copies:
+    return copies
+
+
+def finish_kernel(w_ref, gz, map_ref, tables_ref, *refs):
+    hats, (grad_out, modes_out, grad, syn, modes, sems, mode_sems) = refs[:DP], refs[DP:]
+    written = grads_kernel(*hats, modes_out, modes, mode_sems)
+    written += final_kernel(w_ref, gz, map_ref, tables_ref, grad_out, grad, syn, sems)
+    for copy in written:
         copy.wait()
 
 
@@ -418,8 +424,8 @@
 
 def y_neighbours(data):
     return [
-        lax.ppermute(data, "dp", [(i, i // Y_RING * Y_RING + (i + by) % Y_RING) for i in range(DP)])
-        for by in (2, 3, 1)
+        lax.ppermute(data, "dp", [(i, i ^ by) for i in range(DP)])
+        for by in (2, 1, 3)
     ]
 
 
@@ -480,26 +486,23 @@
     partner = x_partner(hats)
     opposite, back_one, next_one = y_neighbours(hats)
     others = [opposite, back_one, next_one, partner, x_partner(opposite), *y_neighbours(partner)[1:]]
-    grad_field = call(
-        final_kernel,
-        "final",
-        pltpu.HBM(grid_shape, BF),
-        IN_HBM,
-        [on_grid, BOTH_ROWS, pltpu.SemaphoreType.DMA((2,))],
+    grad_field, grad_modes = call(
+        finish_kernel,
+        "finish",
+        (pltpu.HBM(grid_shape, BF), pltpu.HBM((M, K, C, 2 * C), F32)),
+        [IN_HBM] * 2,
+        [
+            on_grid,
+            BOTH_ROWS,
+            pltpu.VMEM((M, K, C, 2 * C), F32),
+            pltpu.SemaphoreType.DMA((CX,)),
+            pltpu.SemaphoreType.DMA((M,)),
+        ],
         exchange(back.reshape(SPECTRA.shape)),
         *in_vmem(gz, wide_map, tables),
-        specs=[IN_VMEM] * 4,
-    )
-    grad_field, *others = lax.optimization_barrier((grad_field, *others))
-    grad_modes = call(
-        grads_kernel,
-        "weight_grads",
-        pltpu.HBM((M, K, C, 2 * C), F32),
-        IN_HBM,
-        [pltpu.VMEM((M, K, C, 2 * C), F32), pltpu.SemaphoreType.DMA((M,))],
         hats,
         *others,
-        specs=[IN_VMEM] * DP,
+        specs=[IN_VMEM] * (4 + DP),
     )
     return grad_field.reshape(field.shape), grad_modes
 

time: 93.5 us -> 92.8 us (level)
  waiting for transfers between devices: 3.72 us -> 6.47 us
  starting transfers between devices: 14.8 us -> 12.1 us
  Pallas kernels: 12.5 us -> 11 us
    ppermute x5, waiting for transfers between devices: 0.01 us -> 3.88 us  [y_neighbours(): lax.ppermute(data, 'dp', [(i, i ^ by) for i in range(DP)])]
    all_to_all x1, waiting for transfers between devices: 3.71 us -> 0.9 us  [exchange(): return lax.all_to_all(data, 'slab', 0, 0, tiled=True)]
    ppermute x5, starting transfers between devices: 8.27 us -> 6.43 us  [y_neighbours(): lax.ppermute(data, 'dp', [(i, i ^ by) for i in range(DP)])]
    ppermute x2, waiting for transfers between devices: 0.01 us -> 1.69 us  [x_partner(): return lax.ppermute(data, 'dp', [(i, (i + Y_RING) % DP) for i in range(DP)])]
    pallas_call x6 -> x5, Pallas kernels: 12.5 us -> 11 us  [call(): pl.pallas_call(kernel, name=name, out_shape=out_shapes, in_specs=specs, o...]
  transfers between devices with their start and end apart: 8 -> 8, of which waited for: 1 -> 7; matrix products, arithmetic and copies ran while one was open for 0% -> 0% of each run, Pallas kernels for 2% -> 0%
where the time goes in v7:
time: 92.8 us; the launch traced here: 91.6 us
  blocking collectives  61.4 us (66%)
  starting transfers between devices  12.1 us (13%)
  Pallas kernels  11 us (12%)
  waiting for transfers between devices  6.47 us (7%)
    all_to_all x3, blocking collectives, exchange(): return lax.all_to_all(data, 'slab', 0, 0, tiled=True)  61.4 us
    pallas_call x5, Pallas kernels, call(): pl.pallas_call(kernel, name=name, out_shape=out_shapes, in_specs=specs, o...  11 us
    ppermute x5, starting transfers between devices, y_neighbours(): lax.ppermute(data, 'dp', [(i, i ^ by) for i in range(DP)])  6.43 us
    all_to_all x1, starting transfers between devices, exchange(): return lax.all_to_all(data, 'slab', 0, 0, tiled=True)  5.01 us
    ppermute x5, waiting for transfers between devices, y_neighbours(): lax.ppermute(data, 'dp', [(i, i ^ by) for i in range(DP)])  3.88 us
  transfers between devices with their start and end apart: 8, of which 7 were waited for; matrix products, arithmetic and copies ran while one was open for 0% of the time, Pallas kernels for 0%

profile of v7, /device:TPU:1, one launch (start us, length us, event | category | flops | bytes accessed | tf_op | source)
XLA Modules:
  0.0 91.6 jit_solution(8213095709232045292)
XLA Ops:
  0.6 2.2 %analyse.1 = (f32[32,2,8,128]{3,2,1,0:T(8,128)S(1)}, bf16[8,1024,128]{2,1,0:T(8,128)(2,1)S(1)}, bf16[320,256]{1,0:T(8,128)(2,1)S(1)}, bf16[128,128]{1,0:T(8,128)(2,1)S(1)}, f32[1,128]{1,0:T(1,128)S(1)}) custom-call(bf16[2,64,4096]{2,1,0:T(8,128)(2,1)} %bitcast.9, bf16[8,1024,128]{2,1,0:T(8,128)(2,1)} %bitcast.15, bf16[320,256]{1,0:T(8,128)(2,1)} %constant.2.clone.tables_in, ...), custom_call_target="tpu_custom_call" | custom-call | tf_op jit(solution)/shard_map/analyse/pallas_call | solution.py:386
  2.8 0.0 copy-start
  2.8 0.0 copy-start.1
  2.8 25.9 %all_to_all.20 = f32[32,2,8,128]{3,2,1,0:T(8,128)S(1)} all-to-all(f32[32,2,8,128]{3,2,1,0:T(8,128)S(1)} %get-tuple-element.15), channel_id=1, replica_groups=mesh['dp'=8,'slab'=32] {'slab'}, dimensions={0} | all-to-all | bytes 524288 | tf_op jit(solution)/shard_map/all_to_all | solution.py:415
  28.8 1.0 %mix.1 = (f32[8,16,128]{2,1,0:T(8,128)S(1)}, f32[64,8,128]{2,1,0:T(8,128)S(1)}) custom-call(f32[64,8,128]{2,1,0:T(8,128)S(1)} %bitcast.12, bf16[8,1024,128]{2,1,0:T(8,128)(2,1)S(1)} %get-tuple-element.16.w_ref, bf16[320,256]{1,0:T(8,128)(2,1)S(1)} %get-tuple-element.17.tables_ref), custom_call_target="tpu_custom_call" | custom-call | tf_op jit(solution)/shard_map/mix/pallas_call | solution.py:386
  29.8 17.7 %all_to_all.21.w_ref = f32[32,2,8,128]{3,2,1,0:T(8,128)S(1)} all-to-all(f32[32,2,8,128]{3,2,1,0:T(8,128)S(1)} %bitcast.14), channel_id=1, replica_groups=mesh['dp'=8,'slab'=32] {'slab'}, dimensions={0} | all-to-all | bytes 524288 | tf_op jit(solution)/shard_map/all_to_all | solution.py:415
  47.5 2.9 %middle.1 = (bf16[2,64,4096]{2,1,0:T(8,128)(2,1)}, f32[32,2,8,128]{3,2,1,0:T(8,128)S(1)}) custom-call(f32[32,2,8,128]{3,2,1,0:T(8,128)S(1)} %all_to_all.21.w_ref, bf16[2,64,4096]{2,1,0:T(8,128)(2,1)S(1)} %bitcast.10, bf16[2,64,4096]{2,1,0:T(8,128)(2,1)S(1)} %bitcast.13, bf16[128,128]{1,0:T(8,128)(2,1)S(1)} %get-tuple-element.19.map_ref, ...), custom_call_target="tpu_custom_call" | custom-call | tf_op jit(solution)/shard_map/middle/pallas_call | solution.py:386
  50.4 0.0 copy-start.2
  50.4 17.8 %all_to_all.22 = f32[32,2,8,128]{3,2,1,0:T(8,128)S(1)} all-to-all(f32[32,2,8,128]{3,2,1,0:T(8,128)S(1)} %get-tuple-element.21), channel_id=1, replica_groups=mesh['dp'=8,'slab'=32] {'slab'}, dimensions={0} | all-to-all | bytes 524288 | tf_op jit(solution)/shard_map/all_to_all | solution.py:415
  68.2 2.0 %adjoint.1 = (f32[2,8,16,128]{3,2,1,0:T(8,128)S(1)}, f32[64,8,128]{2,1,0:T(8,128)}) custom-call(f32[64,8,128]{2,1,0:T(8,128)S(1)} %bitcast.11, f32[8,16,128]{2,1,0:T(8,128)S(1)} %get-tuple-element.22.u_ref, bf16[8,1024,128]{2,1,0:T(8,128)(2,1)S(1)} %get-tuple-element.16.w_ref, bf16[320,256]{1,0:T(8,128)(2,1)S(1)} %get-tuple-element.17.tables_ref), custom_call_target="tpu_custom_call" | custom-call | tf_op jit(solution)/shard_map/adjoint/pallas_call | solution.py:386
  70.2 5.0 %all-to-all-start.3 = ((f32[32,2,8,128]{3,2,1,0:T(8,128)}), f32[32,2,8,128]{3,2,1,0:T(8,128)S(1)}, u32[]{:S(2)}, u32[]{:S(2)}) async-start(f32[32,2,8,128]{3,2,1,0:T(8,128)} %bitcast.7), calls=%async_computation.3 | async-start | bytes 524288 | tf_op jit(solution)/shard_map/all_to_all | solution.py:415
  75.2 0.4 collective-permute-start.3
  75.6 2.9 %collective-permute-start = (f32[2,8,16,128]{3,2,1,0:T(8,128)S(1)}, f32[2,8,16,128]{3,2,1,0:T(8,128)S(1)}, u32[]{:S(2)}, u32[]{:S(2)}) collective-permute-start(f32[2,8,16,128]{3,2,1,0:T(8,128)S(1)} %get-tuple-element.25.refs_0_), channel_id=1, source_target_pairs={{0,64},{32,96},{64,0},{96,32},{128,192},{160,224},{192,128},{224,1... | collective-permute-start | bytes 393224 | tf_op jit(solution)/shard_map/ppermute | solution.py:427
  78.5 0.8 collective-permute-start.2
  79.3 1.6 %collective-permute-done.3.refs_4_ = f32[2,8,16,128]{3,2,1,0:T(8,128)S(1)} collective-permute-done((f32[2,8,16,128]{3,2,1,0:T(8,128)S(1)}, f32[2,8,16,128]{3,2,1,0:T(8,128)S(1)}, u32[]{:S(2)}, u32[]{:S(2)}) %collective-permute-start.3) | collective-permute-done | bytes 131104 | tf_op jit(solution)/shard_map/ppermute | solution.py:422
  80.9 2.7 %collective-permute-start.6 = (f32[2,8,16,128]{3,2,1,0:T(8,128)S(1)}, f32[2,8,16,128]{3,2,1,0:T(8,128)S(1)}, u32[]{:S(2)}, u32[]{:S(2)}) collective-permute-start(f32[2,8,16,128]{3,2,1,0:T(8,128)S(1)} %collective-permute-done.3.refs_4_), channel_id=1, source_target_pairs={{0,96},{32,64},{64,32},{96,0},{128,224},{160,192},{192,160},{224,1... | collective-permute-start | bytes 393224 | tf_op jit(solution)/shard_map/ppermute | solution.py:427
  83.7 0.2 collective-permute-start.4
  83.9 0.8 collective-permute-done.2.refs_3_
  84.7 0.1 collective-permute-done.1.refs_2_
  84.8 2.1 %collective-permute-done.6.refs_7_ = f32[2,8,16,128]{3,2,1,0:T(8,128)S(1)} collective-permute-done((f32[2,8,16,128]{3,2,1,0:T(8,128)S(1)}, f32[2,8,16,128]{3,2,1,0:T(8,128)S(1)}, u32[]{:S(2)}, u32[]{:S(2)}) %collective-permute-start.6) | collective-permute-done | bytes 131104 | tf_op jit(solution)/shard_map/ppermute | solution.py:427
  86.8 0.9 collective-permute-done.5.refs_6_
  87.8 0.1 collective-permute-done.4.refs_5_
  87.9 0.9 all-to-all-done.3.w_ref
  88.8 2.9 %finish.1 = (bf16[2,64,4096]{2,1,0:T(8,128)(2,1)}, f32[8,16,64,128]{3,2,1,0:T(8,128)}) custom-call(f32[32,2,8,128]{3,2,1,0:T(8,128)S(1)} %all-to-all-done.3.w_ref, bf16[2,64,4096]{2,1,0:T(8,128)(2,1)S(1)} %copy-done.2, bf16[128,128]{1,0:T(8,128)(2,1)S(1)} %get-tuple-element.19.map_ref, bf16[320,256]{1,0:T(8,128)(2,1)S(1)} %get-tuple-element.17.tables_ref, ...), custom_call_target="tpu_custom_call" | custom-call | tf_op jit(solution)/shard_map/finish/pallas_call | solution.py:386
  (6 shorter events, 0.0 us)
Async XLA Ops:
  2.8 44.6 %copy-start = (bf16[1,2,64,4096]{3,2,1,0:T(8,128)(2,1)S(1)}, bf16[1,2,64,4096]{3,2,1,0:T(8,128)(2,1)}, u32[]{:S(2)}) copy-start(bf16[1,2,64,4096]{3,2,1,0:T(8,128)(2,1)} %param.6) | copy-start | bytes 3145732
  2.8 44.6 %copy-start.1 = (bf16[1,2,64,4096]{3,2,1,0:T(8,128)(2,1)S(1)}, bf16[1,2,64,4096]{3,2,1,0:T(8,128)(2,1)}, u32[]{:S(2)}) copy-start(bf16[1,2,64,4096]{3,2,1,0:T(8,128)(2,1)} %param.7) | copy-start | bytes 3145732
  50.4 38.4 %copy-start.2 = (bf16[2,64,4096]{2,1,0:T(8,128)(2,1)S(1)}, bf16[2,64,4096]{2,1,0:T(8,128)(2,1)}, u32[]{:S(2)}) copy-start(bf16[2,64,4096]{2,1,0:T(8,128)(2,1)} %get-tuple-element.24.gz) | copy-start | bytes 3145732
  70.2 18.6 %all-to-all-start.3 = ((f32[32,2,8,128]{3,2,1,0:T(8,128)}), f32[32,2,8,128]{3,2,1,0:T(8,128)S(1)}, u32[]{:S(2)}, u32[]{:S(2)}) async-start(f32[32,2,8,128]{3,2,1,0:T(8,128)} %bitcast.7), calls=%async_computation.3 | async-start | bytes 524288 | tf_op jit(solution)/shard_map/all_to_all | solution.py:415
  75.2 5.7 %collective-permute-start.3 = (f32[2,8,16,128]{3,2,1,0:T(8,128)S(1)}, f32[2,8,16,128]{3,2,1,0:T(8,128)S(1)}, u32[]{:S(2)}, u32[]{:S(2)}) collective-permute-start(f32[2,8,16,128]{3,2,1,0:T(8,128)S(1)} %get-tuple-element.25.refs_0_), channel_id=1, source_target_pairs={{0,128},{32,160},{64,192},{96,224},{128,0},{160,32},{192,64},{224,... | collective-permute-start | bytes 393224 | tf_op jit(solution)/shard_map/ppermute | solution.py:422
  75.6 8.0 %collective-permute-start = (f32[2,8,16,128]{3,2,1,0:T(8,128)S(1)}, f32[2,8,16,128]{3,2,1,0:T(8,128)S(1)}, u32[]{:S(2)}, u32[]{:S(2)}) collective-permute-start(f32[2,8,16,128]{3,2,1,0:T(8,128)S(1)} %get-tuple-element.25.refs_0_), channel_id=1, source_target_pairs={{0,64},{32,96},{64,0},{96,32},{128,192},{160,224},{192,128},{224,1... | collective-permute-start | bytes 393224 | tf_op jit(solution)/shard_map/ppermute | solution.py:427
  78.5 6.1 %collective-permute-start.2 = (f32[2,8,16,128]{3,2,1,0:T(8,128)S(1)}, f32[2,8,16,128]{3,2,1,0:T(8,128)S(1)}, u32[]{:S(2)}, u32[]{:S(2)}) collective-permute-start(f32[2,8,16,128]{3,2,1,0:T(8,128)S(1)} %get-tuple-element.25.refs_0_), channel_id=1, source_target_pairs={{0,96},{32,64},{64,32},{96,0},{128,224},{160,192},{192,160},{224,1... | collective-permute-start | bytes 393224 | tf_op jit(solution)/shard_map/ppermute | solution.py:427
  79.3 5.5 %collective-permute-start.1 = (f32[2,8,16,128]{3,2,1,0:T(8,128)S(1)}, f32[2,8,16,128]{3,2,1,0:T(8,128)S(1)}, u32[]{:S(2)}, u32[]{:S(2)}) collective-permute-start(f32[2,8,16,128]{3,2,1,0:T(8,128)S(1)} %get-tuple-element.25.refs_0_), channel_id=1, source_target_pairs={{0,32},{32,0},{64,96},{96,64},{128,160},{160,128},{192,224},{224,1... | collective-permute-start | bytes 393224 | tf_op jit(solution)/shard_map/ppermute | solution.py:427
  80.9 5.9 %collective-permute-start.6 = (f32[2,8,16,128]{3,2,1,0:T(8,128)S(1)}, f32[2,8,16,128]{3,2,1,0:T(8,128)S(1)}, u32[]{:S(2)}, u32[]{:S(2)}) collective-permute-start(f32[2,8,16,128]{3,2,1,0:T(8,128)S(1)} %collective-permute-done.3.refs_4_), channel_id=1, source_target_pairs={{0,96},{32,64},{64,32},{96,0},{128,224},{160,192},{192,160},{224,1... | collective-permute-start | bytes 393224 | tf_op jit(solution)/shard_map/ppermute | solution.py:427
  83.6 4.1 %collective-permute-start.5 = (f32[2,8,16,128]{3,2,1,0:T(8,128)S(1)}, f32[2,8,16,128]{3,2,1,0:T(8,128)S(1)}, u32[]{:S(2)}, u32[]{:S(2)}) collective-permute-start(f32[2,8,16,128]{3,2,1,0:T(8,128)S(1)} %collective-permute-done.3.refs_4_), channel_id=1, source_target_pairs={{0,32},{32,0},{64,96},{96,64},{128,160},{160,128},{192,224},{224,1... | collective-permute-start | bytes 393224 | tf_op jit(solution)/shard_map/ppermute | solution.py:427
  83.7 4.2 %collective-permute-start.4 = (f32[2,8,16,128]{3,2,1,0:T(8,128)S(1)}, f32[2,8,16,128]{3,2,1,0:T(8,128)S(1)}, u32[]{:S(2)}, u32[]{:S(2)}) collective-permute-start(f32[2,8,16,128]{3,2,1,0:T(8,128)S(1)} %collective-permute-done.refs_1_), channel_id=1, source_target_pairs={{0,128},{32,160},{64,192},{96,224},{128,0},{160,32},{192,64},{224,... | collective-permute-start | bytes 393224 | tf_op jit(solution)/shard_map/ppermute | solution.py:422

commit v8 on v7

--- a/solution.py
+++ b/solution.py
@@ -308,10 +308,10 @@
     low = low_lanes((K, 128))
     other = swap(u)
     rows = jnp.concatenate([jnp.where(low, u, other), jnp.where(low, other, u)], 0)
-    parts = jnp.concatenate(split(rows), 0).astype(F32)
+    parts = jnp.concatenate(split(rows), 0)
     row = lax.broadcasted_iota(jnp.int32, (4 * K, 128), 0) % K
     half = lax.broadcasted_iota(jnp.int32, (4 * K, 128), 1) // C
-    left = lanes([jnp.where(row == 2 * j + half, parts, 0.0).astype(BF) for j in range(K // 2)])
+    left = lanes([jnp.where(row == 2 * j + half, parts, jnp.zeros_like(parts)) for j in range(K // 2)])
     res = dot(left, weights)
     res = res[: 2 * K] + res[2 * K :]
     return res[:K] + turned(res[K:])

time: 92.8 us -> 92.8 us (level)
  no operation moved by 1% of the time
where the time goes in v8:
time: 92.8 us; the launch traced here: 91.6 us
  blocking collectives  61.4 us (66%)
  starting transfers between devices  12.1 us (13%)
  Pallas kernels  11 us (12%)
  waiting for transfers between devices  6.47 us (7%)
    all_to_all x3, blocking collectives, exchange(): return lax.all_to_all(data, 'slab', 0, 0, tiled=True)  61.4 us
    pallas_call x5, Pallas kernels, call(): pl.pallas_call(kernel, name=name, out_shape=out_shapes, in_specs=specs, o...  11 us
    ppermute x5, starting transfers between devices, y_neighbours(): lax.ppermute(data, 'dp', [(i, i ^ by) for i in range(DP)])  6.43 us
    all_to_all x1, starting transfers between devices, exchange(): return lax.all_to_all(data, 'slab', 0, 0, tiled=True)  5.01 us
    ppermute x5, waiting for transfers between devices, y_neighbours(): lax.ppermute(data, 'dp', [(i, i ^ by) for i in range(DP)])  3.88 us
  transfers between devices with their start and end apart: 8, of which 7 were waited for; matrix products, arithmetic and copies ran while one was open for 0% of the time, Pallas kernels for 0%

profile of v8, /device:TPU:1, one launch (start us, length us, event | category | flops | bytes accessed | tf_op | source)
XLA Modules:
  0.0 91.6 jit_solution(15331724358407302918)
XLA Ops:
  0.6 2.2 %analyse.1 = (f32[32,2,8,128]{3,2,1,0:T(8,128)S(1)}, bf16[8,1024,128]{2,1,0:T(8,128)(2,1)S(1)}, bf16[320,256]{1,0:T(8,128)(2,1)S(1)}, bf16[128,128]{1,0:T(8,128)(2,1)S(1)}, f32[1,128]{1,0:T(1,128)S(1)}) custom-call(bf16[2,64,4096]{2,1,0:T(8,128)(2,1)} %bitcast.9, bf16[8,1024,128]{2,1,0:T(8,128)(2,1)} %bitcast.15, bf16[320,256]{1,0:T(8,128)(2,1)} %constant.2.clone.tables_in, ...), custom_call_target="tpu_custom_call" | custom-call | tf_op jit(solution)/shard_map/analyse/pallas_call | solution.py:386
  2.8 0.0 copy-start
  2.8 0.0 copy-start.1
  2.8 25.9 %all_to_all.20 = f32[32,2,8,128]{3,2,1,0:T(8,128)S(1)} all-to-all(f32[32,2,8,128]{3,2,1,0:T(8,128)S(1)} %get-tuple-element.15), channel_id=1, replica_groups=mesh['dp'=8,'slab'=32] {'slab'}, dimensions={0} | all-to-all | bytes 524288 | tf_op jit(solution)/shard_map/all_to_all | solution.py:415
  28.8 1.0 %mix.1 = (f32[8,16,128]{2,1,0:T(8,128)S(1)}, f32[64,8,128]{2,1,0:T(8,128)S(1)}) custom-call(f32[64,8,128]{2,1,0:T(8,128)S(1)} %bitcast.12, bf16[8,1024,128]{2,1,0:T(8,128)(2,1)S(1)} %get-tuple-element.16.w_ref, bf16[320,256]{1,0:T(8,128)(2,1)S(1)} %get-tuple-element.17.tables_ref), custom_call_target="tpu_custom_call" | custom-call | tf_op jit(solution)/shard_map/mix/pallas_call | solution.py:386
  29.8 17.7 %all_to_all.21.w_ref = f32[32,2,8,128]{3,2,1,0:T(8,128)S(1)} all-to-all(f32[32,2,8,128]{3,2,1,0:T(8,128)S(1)} %bitcast.14), channel_id=1, replica_groups=mesh['dp'=8,'slab'=32] {'slab'}, dimensions={0} | all-to-all | bytes 524288 | tf_op jit(solution)/shard_map/all_to_all | solution.py:415
  47.5 2.9 %middle.1 = (bf16[2,64,4096]{2,1,0:T(8,128)(2,1)}, f32[32,2,8,128]{3,2,1,0:T(8,128)S(1)}) custom-call(f32[32,2,8,128]{3,2,1,0:T(8,128)S(1)} %all_to_all.21.w_ref, bf16[2,64,4096]{2,1,0:T(8,128)(2,1)S(1)} %bitcast.10, bf16[2,64,4096]{2,1,0:T(8,128)(2,1)S(1)} %bitcast.13, bf16[128,128]{1,0:T(8,128)(2,1)S(1)} %get-tuple-element.19.map_ref, ...), custom_call_target="tpu_custom_call" | custom-call | tf_op jit(solution)/shard_map/middle/pallas_call | solution.py:386
  50.4 0.0 copy-start.2
  50.4 17.8 %all_to_all.22 = f32[32,2,8,128]{3,2,1,0:T(8,128)S(1)} all-to-all(f32[32,2,8,128]{3,2,1,0:T(8,128)S(1)} %get-tuple-element.21), channel_id=1, replica_groups=mesh['dp'=8,'slab'=32] {'slab'}, dimensions={0} | all-to-all | bytes 524288 | tf_op jit(solution)/shard_map/all_to_all | solution.py:415
  68.2 2.0 %adjoint.1 = (f32[2,8,16,128]{3,2,1,0:T(8,128)S(1)}, f32[64,8,128]{2,1,0:T(8,128)}) custom-call(f32[64,8,128]{2,1,0:T(8,128)S(1)} %bitcast.11, f32[8,16,128]{2,1,0:T(8,128)S(1)} %get-tuple-element.22.u_ref, bf16[8,1024,128]{2,1,0:T(8,128)(2,1)S(1)} %get-tuple-element.16.w_ref, bf16[320,256]{1,0:T(8,128)(2,1)S(1)} %get-tuple-element.17.tables_ref), custom_call_target="tpu_custom_call" | custom-call | tf_op jit(solution)/shard_map/adjoint/pallas_call | solution.py:386
  70.2 5.0 %all-to-all-start.3 = ((f32[32,2,8,128]{3,2,1,0:T(8,128)}), f32[32,2,8,128]{3,2,1,0:T(8,128)S(1)}, u32[]{:S(2)}, u32[]{:S(2)}) async-start(f32[32,2,8,128]{3,2,1,0:T(8,128)} %bitcast.7), calls=%async_computation.3 | async-start | bytes 524288 | tf_op jit(solution)/shard_map/all_to_all | solution.py:415
  75.2 0.4 collective-permute-start.3
  75.6 2.9 %collective-permute-start = (f32[2,8,16,128]{3,2,1,0:T(8,128)S(1)}, f32[2,8,16,128]{3,2,1,0:T(8,128)S(1)}, u32[]{:S(2)}, u32[]{:S(2)}) collective-permute-start(f32[2,8,16,128]{3,2,1,0:T(8,128)S(1)} %get-tuple-element.25.refs_0_), channel_id=1, source_target_pairs={{0,64},{32,96},{64,0},{96,32},{128,192},{160,224},{192,128},{224,1... | collective-permute-start | bytes 393224 | tf_op jit(solution)/shard_map/ppermute | solution.py:427
  78.5 0.8 collective-permute-start.2
  79.3 1.6 %collective-permute-done.3.refs_4_ = f32[2,8,16,128]{3,2,1,0:T(8,128)S(1)} collective-permute-done((f32[2,8,16,128]{3,2,1,0:T(8,128)S(1)}, f32[2,8,16,128]{3,2,1,0:T(8,128)S(1)}, u32[]{:S(2)}, u32[]{:S(2)}) %collective-permute-start.3) | collective-permute-done | bytes 131104 | tf_op jit(solution)/shard_map/ppermute | solution.py:422
  80.9 2.7 %collective-permute-start.6 = (f32[2,8,16,128]{3,2,1,0:T(8,128)S(1)}, f32[2,8,16,128]{3,2,1,0:T(8,128)S(1)}, u32[]{:S(2)}, u32[]{:S(2)}) collective-permute-start(f32[2,8,16,128]{3,2,1,0:T(8,128)S(1)} %collective-permute-done.3.refs_4_), channel_id=1, source_target_pairs={{0,96},{32,64},{64,32},{96,0},{128,224},{160,192},{192,160},{224,1... | collective-permute-start | bytes 393224 | tf_op jit(solution)/shard_map/ppermute | solution.py:427
  83.7 0.2 collective-permute-start.4
  83.9 0.8 collective-permute-done.2.refs_3_
  84.7 0.1 collective-permute-done.1.refs_2_
  84.8 2.1 %collective-permute-done.6.refs_7_ = f32[2,8,16,128]{3,2,1,0:T(8,128)S(1)} collective-permute-done((f32[2,8,16,128]{3,2,1,0:T(8,128)S(1)}, f32[2,8,16,128]{3,2,1,0:T(8,128)S(1)}, u32[]{:S(2)}, u32[]{:S(2)}) %collective-permute-start.6) | collective-permute-done | bytes 131104 | tf_op jit(solution)/shard_map/ppermute | solution.py:427
  86.8 0.9 collective-permute-done.5.refs_6_
  87.8 0.1 collective-permute-done.4.refs_5_
  87.9 0.9 all-to-all-done.3.w_ref
  88.8 2.9 %finish.1 = (bf16[2,64,4096]{2,1,0:T(8,128)(2,1)}, f32[8,16,64,128]{3,2,1,0:T(8,128)}) custom-call(f32[32,2,8,128]{3,2,1,0:T(8,128)S(1)} %all-to-all-done.3.w_ref, bf16[2,64,4096]{2,1,0:T(8,128)(2,1)S(1)} %copy-done.2, bf16[128,128]{1,0:T(8,128)(2,1)S(1)} %get-tuple-element.19.map_ref, bf16[320,256]{1,0:T(8,128)(2,1)S(1)} %get-tuple-element.17.tables_ref, ...), custom_call_target="tpu_custom_call" | custom-call | tf_op jit(solution)/shard_map/finish/pallas_call | solution.py:386
  (6 shorter events, 0.0 us)
Async XLA Ops:
  2.8 44.6 %copy-start = (bf16[1,2,64,4096]{3,2,1,0:T(8,128)(2,1)S(1)}, bf16[1,2,64,4096]{3,2,1,0:T(8,128)(2,1)}, u32[]{:S(2)}) copy-start(bf16[1,2,64,4096]{3,2,1,0:T(8,128)(2,1)} %param.6) | copy-start | bytes 3145732
  2.8 44.6 %copy-start.1 = (bf16[1,2,64,4096]{3,2,1,0:T(8,128)(2,1)S(1)}, bf16[1,2,64,4096]{3,2,1,0:T(8,128)(2,1)}, u32[]{:S(2)}) copy-start(bf16[1,2,64,4096]{3,2,1,0:T(8,128)(2,1)} %param.7) | copy-start | bytes 3145732
  50.4 38.4 %copy-start.2 = (bf16[2,64,4096]{2,1,0:T(8,128)(2,1)S(1)}, bf16[2,64,4096]{2,1,0:T(8,128)(2,1)}, u32[]{:S(2)}) copy-start(bf16[2,64,4096]{2,1,0:T(8,128)(2,1)} %get-tuple-element.24.gz) | copy-start | bytes 3145732
  70.2 18.6 %all-to-all-start.3 = ((f32[32,2,8,128]{3,2,1,0:T(8,128)}), f32[32,2,8,128]{3,2,1,0:T(8,128)S(1)}, u32[]{:S(2)}, u32[]{:S(2)}) async-start(f32[32,2,8,128]{3,2,1,0:T(8,128)} %bitcast.7), calls=%async_computation.3 | async-start | bytes 524288 | tf_op jit(solution)/shard_map/all_to_all | solution.py:415
  75.2 5.7 %collective-permute-start.3 = (f32[2,8,16,128]{3,2,1,0:T(8,128)S(1)}, f32[2,8,16,128]{3,2,1,0:T(8,128)S(1)}, u32[]{:S(2)}, u32[]{:S(2)}) collective-permute-start(f32[2,8,16,128]{3,2,1,0:T(8,128)S(1)} %get-tuple-element.25.refs_0_), channel_id=1, source_target_pairs={{0,128},{32,160},{64,192},{96,224},{128,0},{160,32},{192,64},{224,... | collective-permute-start | bytes 393224 | tf_op jit(solution)/shard_map/ppermute | solution.py:422
  75.6 8.0 %collective-permute-start = (f32[2,8,16,128]{3,2,1,0:T(8,128)S(1)}, f32[2,8,16,128]{3,2,1,0:T(8,128)S(1)}, u32[]{:S(2)}, u32[]{:S(2)}) collective-permute-start(f32[2,8,16,128]{3,2,1,0:T(8,128)S(1)} %get-tuple-element.25.refs_0_), channel_id=1, source_target_pairs={{0,64},{32,96},{64,0},{96,32},{128,192},{160,224},{192,128},{224,1... | collective-permute-start | bytes 393224 | tf_op jit(solution)/shard_map/ppermute | solution.py:427
  78.5 6.1 %collective-permute-start.2 = (f32[2,8,16,128]{3,2,1,0:T(8,128)S(1)}, f32[2,8,16,128]{3,2,1,0:T(8,128)S(1)}, u32[]{:S(2)}, u32[]{:S(2)}) collective-permute-start(f32[2,8,16,128]{3,2,1,0:T(8,128)S(1)} %get-tuple-element.25.refs_0_), channel_id=1, source_target_pairs={{0,96},{32,64},{64,32},{96,0},{128,224},{160,192},{192,160},{224,1... | collective-permute-start | bytes 393224 | tf_op jit(solution)/shard_map/ppermute | solution.py:427
  79.3 5.5 %collective-permute-start.1 = (f32[2,8,16,128]{3,2,1,0:T(8,128)S(1)}, f32[2,8,16,128]{3,2,1,0:T(8,128)S(1)}, u32[]{:S(2)}, u32[]{:S(2)}) collective-permute-start(f32[2,8,16,128]{3,2,1,0:T(8,128)S(1)} %get-tuple-element.25.refs_0_), channel_id=1, source_target_pairs={{0,32},{32,0},{64,96},{96,64},{128,160},{160,128},{192,224},{224,1... | collective-permute-start | bytes 393224 | tf_op jit(solution)/shard_map/ppermute | solution.py:427
  80.9 5.9 %collective-permute-start.6 = (f32[2,8,16,128]{3,2,1,0:T(8,128)S(1)}, f32[2,8,16,128]{3,2,1,0:T(8,128)S(1)}, u32[]{:S(2)}, u32[]{:S(2)}) collective-permute-start(f32[2,8,16,128]{3,2,1,0:T(8,128)S(1)} %collective-permute-done.3.refs_4_), channel_id=1, source_target_pairs={{0,96},{32,64},{64,32},{96,0},{128,224},{160,192},{192,160},{224,1... | collective-permute-start | bytes 393224 | tf_op jit(solution)/shard_map/ppermute | solution.py:427
  83.6 4.1 %collective-permute-start.5 = (f32[2,8,16,128]{3,2,1,0:T(8,128)S(1)}, f32[2,8,16,128]{3,2,1,0:T(8,128)S(1)}, u32[]{:S(2)}, u32[]{:S(2)}) collective-permute-start(f32[2,8,16,128]{3,2,1,0:T(8,128)S(1)} %collective-permute-done.3.refs_4_), channel_id=1, source_target_pairs={{0,32},{32,0},{64,96},{96,64},{128,160},{160,128},{192,224},{224,1... | collective-permute-start | bytes 393224 | tf_op jit(solution)/shard_map/ppermute | solution.py:427
  83.7 4.2 %collective-permute-start.4 = (f32[2,8,16,128]{3,2,1,0:T(8,128)S(1)}, f32[2,8,16,128]{3,2,1,0:T(8,128)S(1)}, u32[]{:S(2)}, u32[]{:S(2)}) collective-permute-start(f32[2,8,16,128]{3,2,1,0:T(8,128)S(1)} %collective-permute-done.refs_1_), channel_id=1, source_target_pairs={{0,128},{32,160},{64,192},{96,224},{128,0},{160,32},{192,64},{224,... | collective-permute-start | bytes 393224 | tf_op jit(solution)/shard_map/ppermute | solution.py:422
